TPU v7x, 32 devices: a whole 2x2x4 slice. The times are simulated.
32 devices in a mesh: frame: 8 (over y, x, core), tile: 4 (over z).
Axes of the slice: x: 2, y: 2, z: 4, core: 2. Of those that a mesh axis runs over, the one named last changes fastest.
Arguments:
- tokens: bfloat16 [32, 256, 1024], P('frame', 'tile'), may hold values from -6 to 6
- out_grad: bfloat16 [32, 256, 1024], P('frame', 'tile'), may hold values from -6 to 6
- actions: int32 [32], P('frame'), may hold values from 0 to 7
- segments: int32 [32], replicated, may hold values from 0 to 3, never falling along the last dimension, each value on 1 to 16 neighbouring positions
- frame_mask: int32 [32], replicated, may hold values 0 or 1
- embed: float32 [8, 1024], replicated, may hold values from -3 to 3
- ln1_gain: float32 [1024], replicated, may hold values from 0.1 to 1.9
- ln1_shift: float32 [1024], replicated, may hold values from -1.5 to 1.5
- spatial_qkv: bfloat16 [1024, 3072], P('frame'), may hold values from -0.25 to 0.25
- spatial_out: bfloat16 [1024, 1024], P('frame'), may hold values from -0.5 to 0.5
- ln2_gain: float32 [1024], replicated, may hold values from 0.1 to 1.9
- ln2_shift: float32 [1024], replicated, may hold values from -1.5 to 1.5
- temporal_qkv: bfloat16 [1024, 3072], P('frame'), may hold values from -0.25 to 0.25
- temporal_out: bfloat16 [1024, 1024], P('frame'), may hold values from -0.25 to 0.25
- ln3_gain: float32 [1024], replicated, may hold values from 0.1 to 1.9
- ln3_shift: float32 [1024], replicated, may hold values from -1.5 to 1.5
- ffn_in: bfloat16 [1024, 4096], P('frame'), may hold values from -0.1875 to 0.1875
- ffn_in_bias: float32 [4096], replicated, may hold values from -2.5 to 2.5
- ffn_out: bfloat16 [4096, 1024], P('frame'), may hold values from -0.125 to 0.125
- ffn_out_bias: float32 [1024], replicated, may hold values from -1.5 to 1.5
Outputs:
- result: bfloat16 [32, 256, 1024], P('frame', 'tile')
- tokens_grad: bfloat16 [32, 256, 1024], P('frame', 'tile')
- embed_grad: float32 [8, 1024], replicated
- ln1_gain_grad: float32 [1024], replicated
- ln1_shift_grad: float32 [1024], replicated
- spatial_qkv_grad: float32 [1024, 3072], P('frame')
- spatial_out_grad: float32 [1024, 1024], P('frame')
- ln2_gain_grad: float32 [1024], replicated
- ln2_shift_grad: float32 [1024], replicated
- temporal_qkv_grad: float32 [1024, 3072], P('frame')
- temporal_out_grad: float32 [1024, 1024], P('frame')
- ln3_gain_grad: float32 [1024], replicated
- ln3_shift_grad: float32 [1024], replicated
- ffn_in_grad: float32 [1024, 4096], P('frame')
- ffn_in_bias_grad: float32 [4096], replicated
- ffn_out_grad: float32 [4096, 1024], P('frame')
- ffn_out_bias_grad: float32 [1024], replicated
Inputs may be any that keep to these rules, and one draw needn't show every extreme that they name: `segments`: clip numbers never fall along the frames; each clip holds 1 to 16 consecutive frames and one holds exactly 16.
All inputs are finite; a program needn't handle non-finite values.
Results may differ from a plain program's by a relative error of at most 0.023.
Values may be sent and summed in bfloat16 or wider, within the bound.
A program may use at most 256 MiB of HBM per device.

v0:
```python
import jax
import jax.numpy as jnp
from jax import lax
from jax.sharding import PartitionSpec as P

HD = 64
MAXLEN = 16


highest = lax.Precision.HIGHEST


def from_behind(x, axis, by):
    length = lax.axis_size(axis)
    pairs = [(i, i + by) for i in range(length) if 0 <= i + by < length]
    return lax.ppermute(x, axis, pairs)


def layer_norm(hidden, gain, shift):
    mean_row = jnp.mean(hidden, -1, keepdims=True)
    centred = hidden - mean_row
    variance = jnp.mean(centred * centred, -1, keepdims=True)
    return centred * lax.rsqrt(variance + 1e-05) * gain + shift


def gelu_tanh(values):
    return jax.nn.gelu(values, approximate=True)


def fetch_weights(pieces):
    return (
        lax.all_gather(pieces[0], "frame", axis=0, tiled=True),
        lax.all_gather(pieces[1], "frame", axis=0, tiled=True),
        lax.all_gather(pieces[2], "frame", axis=0, tiled=True),
        lax.all_gather(pieces[3], "frame", axis=0, tiled=True),
        lax.all_gather(pieces[4], "frame", axis=0, tiled=True),
        lax.all_gather(pieces[5], "frame", axis=0, tiled=True),
    )


def dense(left, right):
    return jnp.dot(left, right, preferred_element_type=jnp.float32)


def left_grad(inputs, grads):
    return jnp.einsum("nd,ne->de", inputs, grads, preferred_element_type=jnp.float32)


def back_input(grads, weight):
    return jnp.einsum("ne,de->nd", grads, weight, preferred_element_type=jnp.float32)


def per_device(
    tokens,
    out_grad,
    actions,
    segments,
    frame_mask,
    embed,
    ln1_gain,
    ln1_shift,
    spatial_qkv,
    spatial_out,
    ln2_gain,
    ln2_shift,
    temporal_qkv,
    temporal_out,
    ln3_gain,
    ln3_shift,
    ffn_in,
    ffn_in_bias,
    ffn_out,
    ffn_out_bias,
):
    frames_dev, tile_tokens, model_width = tokens.shape
    head_count = model_width // HD
    tok_rows = frames_dev * tile_tokens
    score_scale = HD ** (-0.5)
    local_mats = (spatial_qkv, spatial_out, temporal_qkv, temporal_out, ffn_in, ffn_out)
    w_qs, w_os, w_qt, w_ot, w_in, w_out = fetch_weights(local_mats)
    one_hot = (actions[:, None] == jnp.arange(embed.shape[0], dtype=jnp.int32)[None, :]).astype(
        jnp.float32
    )
    added = jnp.dot(one_hot, embed, precision=highest)
    start = (tokens.astype(jnp.float32) + added[:, None, :]).reshape(tok_rows, model_width)
    unit1 = layer_norm(start, ln1_gain, ln1_shift).astype(jnp.bfloat16)
    qkv_one = dense(unit1, w_qs).astype(jnp.bfloat16)
    query1 = qkv_one[:, :model_width].reshape(frames_dev, tile_tokens, head_count, HD)
    key_one = qkv_one[:, model_width : 2 * model_width].reshape(
        frames_dev, tile_tokens, model_width
    )
    value_one = qkv_one[:, 2 * model_width :].reshape(frames_dev, tile_tokens, model_width)
    key_all, value_all = (
        lax.all_gather(key_one, "tile", axis=1, tiled=True),
        lax.all_gather(value_one, "tile", axis=1, tiled=True),
    )
    key_all = key_all.reshape(frames_dev, -1, head_count, HD)
    value_all = value_all.reshape(frames_dev, -1, head_count, HD)
    scores1 = (
        jnp.einsum("fqhd,fkhd->fhqk", query1, key_all, preferred_element_type=jnp.float32)
        * score_scale
    )
    top_one = jnp.max(scores1, -1, keepdims=True)
    expo_one = jnp.exp(scores1 - top_one)
    total_one = jnp.sum(expo_one, -1, keepdims=True)
    logsum_one = top_one + jnp.log(total_one)
    probs_one = (expo_one / total_one).astype(jnp.bfloat16)
    mixed1 = jnp.einsum("fhqk,fkhd->fqhd", probs_one, value_all, preferred_element_type=jnp.float32)
    mixed1 = mixed1.astype(jnp.bfloat16).reshape(tok_rows, model_width)
    after1 = start + dense(mixed1, w_os)
    unit2 = layer_norm(after1, ln2_gain, ln2_shift).astype(jnp.bfloat16)
    qkv_two = dense(unit2, w_qt).astype(jnp.bfloat16)
    query2 = qkv_two[:, :model_width].reshape(frames_dev, tile_tokens, head_count, HD)
    key_two = qkv_two[:, model_width : 2 * model_width].reshape(
        frames_dev, tile_tokens, model_width
    )
    value_two = qkv_two[:, 2 * model_width :].reshape(frames_dev, tile_tokens, model_width)
    history = (MAXLEN - 1 + frames_dev - 1) // frames_dev
    key_list = []
    value_list = []
    for distance in range(history, 0, -1):
        moved_key, moved_value = from_behind((key_two, value_two), "frame", distance)
        key_list.append(moved_key)
        value_list.append(moved_value)
    key_hist = jnp.concatenate(key_list + [key_two], 0).reshape(-1, tile_tokens, head_count, HD)
    value_hist = jnp.concatenate(value_list + [value_two], 0).reshape(
        -1, tile_tokens, head_count, HD
    )
    frame_base = lax.axis_index("frame") * frames_dev
    key_span = (history + 1) * frames_dev
    lead_frames = history * frames_dev
    seg_padded = jnp.concatenate([jnp.full((lead_frames,), -1, jnp.int32), segments])
    mask_padded = jnp.concatenate([jnp.zeros((lead_frames,), jnp.int32), frame_mask])
    seg_keys = lax.dynamic_slice_in_dim(seg_padded, frame_base, key_span)
    mask_keys = lax.dynamic_slice_in_dim(mask_padded, frame_base, key_span)
    seg_query = seg_keys[lead_frames:]
    key_place = jnp.arange(key_span, dtype=jnp.int32)
    query_place = jnp.arange(frames_dev, dtype=jnp.int32) + lead_frames
    allowed = (seg_keys[None, :] == seg_query[:, None]) & (
        key_place[None, :] <= query_place[:, None]
    )
    allowed = allowed & ((mask_keys[None, :] == 1) | (key_place[None, :] == query_place[:, None]))

    def temporal_scores():
        raw = (
            jnp.einsum("iphd,jphd->phij", query2, key_hist, preferred_element_type=jnp.float32)
            * score_scale
        )
        return jnp.where(allowed[None, None], raw, -1e30)

    scores2 = temporal_scores()
    top_two = jnp.max(scores2, -1, keepdims=True)
    expo_two = jnp.exp(scores2 - top_two)
    total_two = jnp.sum(expo_two, -1, keepdims=True)
    logsum_two = top_two + jnp.log(total_two)
    probs_two = (expo_two / total_two).astype(jnp.bfloat16)
    mixed2 = jnp.einsum(
        "phij,jphd->iphd", probs_two, value_hist, preferred_element_type=jnp.float32
    )
    mixed2 = mixed2.astype(jnp.bfloat16).reshape(tok_rows, model_width)
    after2 = after1 + dense(mixed2, w_ot)
    unit3 = layer_norm(after2, ln3_gain, ln3_shift).astype(jnp.bfloat16)
    pre_act = dense(unit3, w_in) + ffn_in_bias
    active = gelu_tanh(pre_act).astype(jnp.bfloat16)
    result = (after2 + dense(active, w_out) + ffn_out_bias).astype(jnp.bfloat16)
    result = result.reshape(frames_dev, tile_tokens, model_width)
    w_qs, w_os, w_qt, w_ot, w_in, w_out = fetch_weights(local_mats)
    grad_low = out_grad.reshape(tok_rows, model_width)
    grad_full = grad_low.astype(jnp.float32)
    d_out_bias = jnp.sum(grad_full, 0)
    d_wout = left_grad(active, grad_low)
    d_active = back_input(grad_low, w_out)
    gelu_value, gelu_pull = jax.vjp(gelu_tanh, pre_act)
    d_pre = gelu_pull(d_active)[0].astype(jnp.bfloat16)
    d_in_bias = jnp.sum(d_pre.astype(jnp.float32), 0)
    d_win = left_grad(unit3, d_pre)
    d_unit3 = back_input(d_pre, w_in)
    norm_three, pull_three = jax.vjp(layer_norm, after2, ln3_gain, ln3_shift)
    d_mid3, d_gain3, d_shift3 = pull_three(d_unit3)
    d_after2 = grad_full + d_mid3
    d_branch2 = d_after2.astype(jnp.bfloat16)
    d_wot = left_grad(mixed2, d_branch2)
    d_mixed2 = (
        back_input(d_branch2, w_ot)
        .astype(jnp.bfloat16)
        .reshape(frames_dev, tile_tokens, head_count, HD)
    )
    probs_again = jnp.exp(temporal_scores() - logsum_two)
    d_probs2 = jnp.einsum(
        "iphd,jphd->phij", d_mixed2, value_hist, preferred_element_type=jnp.float32
    )
    d_scores2 = probs_again * (d_probs2 - jnp.sum(probs_again * d_probs2, -1, keepdims=True))
    d_scores2 = d_scores2.astype(jnp.bfloat16)
    d_query2 = (
        jnp.einsum("phij,jphd->iphd", d_scores2, key_hist, preferred_element_type=jnp.float32)
        * score_scale
    )
    d_key_hist = (
        jnp.einsum("phij,iphd->jphd", d_scores2, query2, preferred_element_type=jnp.float32)
        * score_scale
    )
    d_value_hist = jnp.einsum(
        "phij,iphd->jphd",
        probs_again.astype(jnp.bfloat16),
        d_mixed2,
        preferred_element_type=jnp.float32,
    )
    d_key_hist = d_key_hist.reshape(history + 1, frames_dev, tile_tokens, model_width)
    d_value_hist = d_value_hist.reshape(history + 1, frames_dev, tile_tokens, model_width)
    d_key2 = d_key_hist[history]
    d_value2 = d_value_hist[history]
    for distance in range(1, history + 1):
        back_key, back_value = (
            from_behind(
                d_key_hist[history - distance].astype(jnp.bfloat16), "frame", -distance
            ).astype(jnp.float32),
            from_behind(
                d_value_hist[history - distance].astype(jnp.bfloat16), "frame", -distance
            ).astype(jnp.float32),
        )
        d_key2 = d_key2 + back_key
        d_value2 = d_value2 + back_value
    d_qkv2 = jnp.concatenate(
        [
            d_query2.reshape(tok_rows, model_width),
            d_key2.reshape(tok_rows, model_width),
            d_value2.reshape(tok_rows, model_width),
        ],
        1,
    ).astype(jnp.bfloat16)
    d_wqt = left_grad(unit2, d_qkv2)
    d_unit2 = back_input(d_qkv2, w_qt)
    norm_two, pull_two = jax.vjp(layer_norm, after1, ln2_gain, ln2_shift)
    d_mid2, d_gain2, d_shift2 = pull_two(d_unit2)
    d_after1 = d_after2 + d_mid2
    d_branch1 = d_after1.astype(jnp.bfloat16)
    d_wos = left_grad(mixed1, d_branch1)
    d_mixed1 = (
        back_input(d_branch1, w_os)
        .astype(jnp.bfloat16)
        .reshape(frames_dev, tile_tokens, head_count, HD)
    )
    scores_again = (
        jnp.einsum("fqhd,fkhd->fhqk", query1, key_all, preferred_element_type=jnp.float32)
        * score_scale
    )
    probs_back = jnp.exp(scores_again - logsum_one)
    d_probs1 = jnp.einsum(
        "fqhd,fkhd->fhqk", d_mixed1, value_all, preferred_element_type=jnp.float32
    )
    d_scores1 = probs_back * (d_probs1 - jnp.sum(probs_back * d_probs1, -1, keepdims=True))
    d_scores1 = d_scores1.astype(jnp.bfloat16)
    d_query1 = (
        jnp.einsum("fhqk,fkhd->fqhd", d_scores1, key_all, preferred_element_type=jnp.float32)
        * score_scale
    )
    d_key_all = (
        jnp.einsum("fhqk,fqhd->fkhd", d_scores1, query1, preferred_element_type=jnp.float32)
        * score_scale
    )
    d_value_all = jnp.einsum(
        "fhqk,fqhd->fkhd",
        probs_back.astype(jnp.bfloat16),
        d_mixed1,
        preferred_element_type=jnp.float32,
    )
    d_key_all = d_key_all.reshape(frames_dev, -1, model_width)
    d_value_all = d_value_all.reshape(frames_dev, -1, model_width)
    d_key1, d_value1 = (
        lax.psum_scatter(
            d_key_all.astype(jnp.bfloat16), "tile", scatter_dimension=1, tiled=True
        ).astype(jnp.float32),
        lax.psum_scatter(
            d_value_all.astype(jnp.bfloat16), "tile", scatter_dimension=1, tiled=True
        ).astype(jnp.float32),
    )
    d_qkv1 = jnp.concatenate(
        [
            d_query1.reshape(tok_rows, model_width),
            d_key1.reshape(tok_rows, model_width),
            d_value1.reshape(tok_rows, model_width),
        ],
        1,
    ).astype(jnp.bfloat16)
    d_wqs = left_grad(unit1, d_qkv1)
    d_unit1 = back_input(d_qkv1, w_qs)
    norm_one, pull_one = jax.vjp(layer_norm, start, ln1_gain, ln1_shift)
    d_mid1, d_gain1, d_shift1 = pull_one(d_unit1)
    d_start = d_after1 + d_mid1
    tokens_grad = d_start.astype(jnp.bfloat16).reshape(frames_dev, tile_tokens, model_width)
    frame_sums = jnp.sum(d_start.reshape(frames_dev, tile_tokens, model_width), 1)
    d_embed = jnp.einsum("fa,fd->ad", one_hot, frame_sums, precision=highest)
    small = lax.psum(
        (d_embed, d_gain1, d_shift1, d_gain2, d_shift2, d_gain3, d_shift3, d_in_bias, d_out_bias),
        ("frame", "tile"),
    )
    mat_grads = (d_wqs, d_wos, d_wqt, d_wot, d_win, d_wout)
    reduced = (
        lax.psum_scatter(mat_grads[0], "frame", scatter_dimension=0, tiled=True),
        lax.psum_scatter(mat_grads[1], "frame", scatter_dimension=0, tiled=True),
        lax.psum_scatter(mat_grads[2], "frame", scatter_dimension=0, tiled=True),
        lax.psum_scatter(mat_grads[3], "frame", scatter_dimension=0, tiled=True),
        lax.psum_scatter(mat_grads[4], "frame", scatter_dimension=0, tiled=True),
        lax.psum_scatter(mat_grads[5], "frame", scatter_dimension=0, tiled=True),
    )
    reduced = (
        lax.psum(reduced[0].astype(jnp.bfloat16), "tile").astype(jnp.float32),
        lax.psum(reduced[1].astype(jnp.bfloat16), "tile").astype(jnp.float32),
        lax.psum(reduced[2].astype(jnp.bfloat16), "tile").astype(jnp.float32),
        lax.psum(reduced[3].astype(jnp.bfloat16), "tile").astype(jnp.float32),
        lax.psum(reduced[4].astype(jnp.bfloat16), "tile").astype(jnp.float32),
        lax.psum(reduced[5].astype(jnp.bfloat16), "tile").astype(jnp.float32),
    )
    return (
        result,
        tokens_grad,
        small[0],
        small[1],
        small[2],
        reduced[0],
        reduced[1],
        small[3],
        small[4],
        reduced[2],
        reduced[3],
        small[5],
        small[6],
        reduced[4],
        small[7],
        reduced[5],
        small[8],
    )


def solution(mesh):
    in_specs = (
        P("frame", "tile", None),
        P("frame", "tile", None),
        P("frame"),
        P(),
        P(),
        P(),
        P(),
        P(),
        P("frame", None),
        P("frame", None),
        P(),
        P(),
        P("frame", None),
        P("frame", None),
        P(),
        P(),
        P("frame", None),
        P(),
        P("frame", None),
        P(),
    )
    out_specs = (
        P("frame", "tile", None),
        P("frame", "tile", None),
        P(),
        P(),
        P(),
        P("frame", None),
        P("frame", None),
        P(),
        P(),
        P("frame", None),
        P("frame", None),
        P(),
        P(),
        P("frame", None),
        P(),
        P("frame", None),
        P(),
    )
    return jax.shard_map(
        per_device, mesh=mesh, in_specs=in_specs, out_specs=out_specs, check_vma=False
    )
```

profile of v0, /device:TPU:0, one launch (start us, length us, event | category | flops | bytes accessed | tf_op | source)
XLA Modules:
  0.0 1536.1 jit_solution(8209242614176198755)
XLA Ops:
  12.6 45.6 %all-gather.9.cloned.1.call-done = bf16[1024,3072]{1,0:T(8,128)(2,1)} async-done(((bf16[128,3072]{1,0:T(8,128)(2,1)}), bf16[1024,3072]{1,0:T(8,128)(2,1)}) %all-gather.9.cloned.1.call-update) | async-done | bytes 6291472 | tf_op jit(solution)/shard_map/all_gather | solution.py:32
  58.2 4.6 convolution_convert_fusion.1
  70.4 39.7 %all-gather.13.cloned.1.call-done = bf16[4,256,1024]{2,1,0:T(8,128)(2,1)} async-done(((bf16[4,64,1024]{2,1,0:T(8,128)(2,1)}), bf16[4,256,1024]{2,1,0:T(8,128)(2,1)}) %all-gather.13.cloned.1.call-update) | async-done | bytes 2097168 | tf_op jit(solution)/shard_map/all_gather | solution.py:94
  112.9 44.0 %all-gather.11.cloned.1.call-done = bf16[4,256,1024]{2,1,0:T(8,128)(2,1)} async-done(((bf16[4,64,1024]{2,1,0:T(8,128)(2,1)}), bf16[4,256,1024]{2,1,0:T(8,128)(2,1)}) %all-gather.11.cloned.1.call-update) | async-done | bytes 2097168 | tf_op jit(solution)/shard_map/all_gather | solution.py:95
  156.9 3.9 copy.49
  169.2 16.1 %all-gather.15.cloned.1.call-done = bf16[1024,1024]{1,0:T(8,128)(2,1)} async-done(((bf16[128,1024]{1,0:T(8,128)(2,1)}), bf16[1024,1024]{1,0:T(8,128)(2,1)}) %all-gather.15.cloned.1.call-update) | async-done | bytes 2097168 | tf_op jit(solution)/shard_map/all_gather | solution.py:33
  188.0 44.6 %all-gather.17.cloned.1.call-done = bf16[1024,3072]{1,0:T(8,128)(2,1)} async-done(((bf16[128,3072]{1,0:T(8,128)(2,1)}), bf16[1024,3072]{1,0:T(8,128)(2,1)}) %all-gather.17.cloned.1.call-update) | async-done | bytes 6291472 | tf_op jit(solution)/shard_map/all_gather | solution.py:34
  232.6 4.7 convolution_convert_fusion
  240.6 3.4 collective-permute-start.6
  244.0 3.1 collective-permute-start.5
  251.6 9.1 collective-permute-start.2
  260.7 16.0 %collective-permute-start.1 = (bf16[4,64,1024]{2,1,0:T(8,128)(2,1)}, bf16[4,64,1024]{2,1,0:T(8,128)(2,1)}, u32[]{:S(2)}, u32[]{:S(2)}) collective-permute-start(bf16[4,64,1024]{2,1,0:T(8,128)(2,1)} %bitcast.6), channel_id=1, source_target_pairs={{0,12},{4,16},{8,20},{12,24},{16,28},{1,13},{5,17},{9,21},{13,25},... | collective-permute-start | bytes 1572872 | tf_op jit(solution)/shard_map/ppermute | solution.py:16
  276.8 35.2 %collective-permute-start = (bf16[4,64,1024]{2,1,0:T(8,128)(2,1)}, bf16[4,64,1024]{2,1,0:T(8,128)(2,1)}, u32[]{:S(2)}, u32[]{:S(2)}) collective-permute-start(bf16[4,64,1024]{2,1,0:T(8,128)(2,1)} %bitcast.6), channel_id=1, source_target_pairs={{0,16},{4,20},{8,24},{12,28},{1,17},{5,21},{9,25},{13,29},{2,18},{... | collective-permute-start | bytes 1572872 | tf_op jit(solution)/shard_map/ppermute | solution.py:16
  355.3 28.9 %concatenate.55 = bf16[20,64,16,64]{3,0,2,1:T(8,128)(2,1)} concatenate(bf16[4,64,16,64]{3,0,2,1:T(4,128)(2,1)} %copy.58, bf16[4,64,16,64]{3,0,2,1:T(4,128)(2,1)} %copy.59, bf16[4,64,16,64]{3,0,2,1:T(4,128)(2,1)} %copy.60, bf16[4,64,16,64]{3,0,2,1:T(4,128)(2,1)} %copy.61, bf16[4,64,16,64]{3,0,2,1:T(4,128)(2,1)} %copy.62), dimensions={0} | concatenate | bytes 5242880 | tf_op jit(solution)/shard_map/concatenate | solution.py:125
  384.3 25.3 %concatenate.47 = bf16[20,64,16,64]{3,0,2,1:T(8,128)(2,1)} concatenate(bf16[4,64,16,64]{3,0,2,1:T(4,128)(2,1)} %copy.53, bf16[4,64,16,64]{3,0,2,1:T(4,128)(2,1)} %copy.54, bf16[4,64,16,64]{3,0,2,1:T(4,128)(2,1)} %copy.55, bf16[4,64,16,64]{3,0,2,1:T(4,128)(2,1)S(1)} %copy-done.31, bf16[4,64,16,64]{3,0,2,1:T(4,128)(2,1)S(1)} %copy.57), dimensions={0} | concatenate | bytes 5242880 | tf_op jit(solution)/shard_map/concatenate | solution.py:126
  409.6 6.8 fusion.71
  418.8 3.0 fusion.20
  430.4 7.9 fusion.75
  438.3 10.9 convert_reduce_fusion
  450.6 3.2 multiply_reduce_fusion.3
  460.2 9.0 multiply_reduce_fusion.2
  469.2 8.6 fusion.73
  481.9 3.0 convert_element_type.224
  505.0 4.2 multiply_convert_fusion.5
  509.2 6.4 fusion.74
  534.2 4.8 fusion.21
  553.9 5.7 multiply_reduce_fusion.4
  565.6 4.5 fusion.14
  570.0 4.0 copy.84
  574.3 5.0 multiply_reduce_fusion
  584.0 4.0 copy.82
  595.8 7.6 fusion.38
  603.5 2.9 fusion.22
  608.1 31.2 %reduce-scatter.11.cloned.1.call-done = bf16[4,64,1024]{2,1,0:T(8,128)(2,1)} async-done(((bf16[4,256,1024]{2,1,0:T(8,128)(2,1)}), bf16[4,64,1024]{2,1,0:T(8,128)(2,1)}) %reduce-scatter.11.cloned.1.call-update) | async-done | bytes 524304 | tf_op jit(solution)/shard_map/reduce_scatter | solution.py:273
  639.3 46.1 %reduce-scatter.9.cloned.1.call-done = bf16[4,64,1024]{2,1,0:T(8,128)(2,1)} async-done(((bf16[4,256,1024]{2,1,0:T(8,128)(2,1)}), bf16[4,64,1024]{2,1,0:T(8,128)(2,1)}) %reduce-scatter.9.cloned.1.call-update) | async-done | bytes 524304 | tf_op jit(solution)/shard_map/reduce_scatter | solution.py:270
  685.4 7.7 fusion.36
  694.3 10.5 fusion.60
  705.9 10.8 fusion.61
  716.7 22.7 %reduce-scatter.19.cloned.1.call-done = f32[128,1024]{1,0:T(8,128)} async-done(((f32[1024,1024]{1,0:T(8,128)}), f32[128,1024]{1,0:T(8,128)}) %reduce-scatter.19.cloned.1.call-update) | async-done | bytes 524304 | tf_op jit(solution)/shard_map/reduce_scatter | solution.py:302
  741.2 53.2 %reduce-scatter.15.cloned.1.call-done = f32[128,1024]{1,0:T(8,128)} async-done(((f32[1024,1024]{1,0:T(8,128)}), f32[128,1024]{1,0:T(8,128)}) %reduce-scatter.15.cloned.1.call-update) | async-done | bytes 524304 | tf_op jit(solution)/shard_map/reduce_scatter | solution.py:300
  796.1 94.1 %reduce-scatter.17.cloned.1.call-done = f32[128,3072]{1,0:T(8,128)} async-done(((f32[1024,3072]{1,0:T(8,128)}), f32[128,3072]{1,0:T(8,128)}) %reduce-scatter.17.cloned.1.call-update) | async-done | bytes 1572880 | tf_op jit(solution)/shard_map/reduce_scatter | solution.py:301
  892.7 93.4 %reduce-scatter.13.cloned.1.call-done = f32[128,3072]{1,0:T(8,128)} async-done(((f32[1024,3072]{1,0:T(8,128)}), f32[128,3072]{1,0:T(8,128)}) %reduce-scatter.13.cloned.1.call-update) | async-done | bytes 1572880 | tf_op jit(solution)/shard_map/reduce_scatter | solution.py:299
  988.4 117.0 %reduce-scatter.21.cloned.1.call-done = f32[128,4096]{1,0:T(8,128)} async-done(((f32[1024,4096]{1,0:T(8,128)}), f32[128,4096]{1,0:T(8,128)}) %reduce-scatter.21.cloned.1.call-update) | async-done | bytes 2097168 | tf_op jit(solution)/shard_map/reduce_scatter | solution.py:303
  1108.2 116.7 %reduce-scatter.23.cloned.1.call-done = f32[512,1024]{1,0:T(8,128)} async-done(((f32[4096,1024]{1,0:T(8,128)}), f32[512,1024]{1,0:T(8,128)}) %reduce-scatter.23.cloned.1.call-update) | async-done | bytes 2097168 | tf_op jit(solution)/shard_map/reduce_scatter | solution.py:304
  1228.4 8.3 fusion.24
  1236.8 5.5 multiply_reduce_fusion.5
  1244.8 140.7 %all-reduce.9.cloned.1.call-done = (bf16[128,3072]{1,0:T(8,128)(2,1)}, bf16[128,1024]{1,0:T(8,128)(2,1)}, bf16[128,3072]{1,0:T(8,128)(2,1)}, bf16[128,1024]{1,0:...) async-done(((bf16[128,3072]{1,0:T(8,128)(2,1)}, bf16[128,1024]{1,0:T(8,128)(2,1)}, bf16[128,3072]{1,0:T(8,128)(2,1)}, bf16[128,1024]{1,0:T(8,128)(2,1)}, ...) | async-done | bytes 4194320 | tf_op jit(solution)/shard_map/psum | solution.py:307
  1396.1 121.1 %all-reduce.7.cloned.1.call-done = (f32[8,1024]{1,0:T(8,128)}, f32[1024]{0:T(1024)}, f32[1024]{0:T(1024)}, f32[1024]{0:T(1024)}, f32[1024]{0:T(1024)}, /*index=5...) async-done(((f32[8,1024]{1,0:T(8,128)}, f32[1024]{0:T(1024)}, f32[1024]{0:T(1024)}, f32[1024]{0:T(1024)}, f32[1024]{0:T(1024)}, /*index=5*/f32[1024]{0:T(1024)}, ...) | async-done | bytes 77840 | tf_op jit(solution)/shard_map/psum | solution.py:293
  (340 shorter events, 215.7 us)
Async XLA Ops:
  7.2 51.0 %all-gather.9.cloned.1.call-start = ((), (), s32[]{:S(2)}) async-start(), calls=%async_computation.8 | async-start | bytes 7077888 | tf_op jit(solution)/shard_map/all_gather | solution.py:32
  7.9 102.1 %all-gather.13.cloned.1.call-start = ((), (), s32[]{:S(2)}) async-start(), calls=%async_computation.10 | async-start | bytes 2621440 | tf_op jit(solution)/shard_map/all_gather | solution.py:94
  10.2 52.6 %copy-start.59 = (f32[256]{0:T(256)}, f32[256]{0:T(256)S(1)}, u32[]{:S(2)}) copy-start(f32[256]{0:T(256)S(1)} %div.79) | copy-start | bytes 3076
  11.5 173.8 %copy-start.9 = (f32[4,64,1024]{2,1,0:T(8,128)}, f32[4,64,1024]{2,1,0:T(8,128)S(1)}, u32[]{:S(2)}) copy-start(f32[4,64,1024]{2,1,0:T(8,128)S(1)} %get-tuple-element.64) | copy-start | bytes 3145732
  11.6 51.2 %copy-start.63 = (f32[256]{0:T(256)}, f32[256]{0:T(256)S(1)}, u32[]{:S(2)}) copy-start(f32[256]{0:T(256)S(1)} %add.217) | copy-start | bytes 3076
  11.6 51.2 %copy-start.61 = (f32[256]{0:T(256)}, f32[256]{0:T(256)S(1)}, u32[]{:S(2)}) copy-start(f32[256]{0:T(256)S(1)} %rsqrt.33) | copy-start | bytes 3076
  63.9 92.9 %all-gather.11.cloned.1.call-start = ((), (), s32[]{:S(2)}) async-start(), calls=%async_computation.9 | async-start | bytes 2621440 | tf_op jit(solution)/shard_map/all_gather | solution.py:95
  64.7 120.6 %all-gather.15.cloned.1.call-start = ((), (), s32[]{:S(2)}) async-start(), calls=%async_computation.11 | async-start | bytes 2359296 | tf_op jit(solution)/shard_map/all_gather | solution.py:33
  65.3 167.3 %all-gather.17.cloned.1.call-start = ((), (), s32[]{:S(2)}) async-start(), calls=%async_computation.12 | async-start | bytes 7077888 | tf_op jit(solution)/shard_map/all_gather | solution.py:34
  65.8 359.7 %all-gather.19.cloned.1.call-start = ((), (), s32[]{:S(2)}) async-start(), calls=%async_computation.13 | async-start | bytes 2359296 | tf_op jit(solution)/shard_map/all_gather | solution.py:35
  66.4 363.9 %all-gather.23.cloned.1.call-start = ((), (), s32[]{:S(2)}) async-start(), calls=%async_computation.15 | async-start | bytes 9437184 | tf_op jit(solution)/shard_map/all_gather | solution.py:37
  67.2 371.1 %all-gather.21.cloned.1.call-start = ((), (), s32[]{:S(2)}) async-start(), calls=%async_computation.14 | async-start | bytes 9437184 | tf_op jit(solution)/shard_map/all_gather | solution.py:36
  67.9 571.4 %reduce-scatter.11.cloned.1.call-start = ((), (), s32[]{:S(2)}) async-start(), calls=%async_computation.17 | async-start | bytes 2621440 | tf_op jit(solution)/shard_map/reduce_scatter | solution.py:273
  168.4 64.1 %copy-start.54 = (f32[1024]{0:T(1024)S(1)}, f32[1024]{0:T(1024)}, u32[]{:S(2)}) copy-start(f32[1024]{0:T(1024)} %param.30) | copy-start | bytes 12292
  168.4 64.1 %copy-start.56 = (f32[1024]{0:T(1024)S(1)}, f32[1024]{0:T(1024)}, u32[]{:S(2)}) copy-start(f32[1024]{0:T(1024)} %param.31) | copy-start | bytes 12292
  169.2 68.1 %copy-start.25 = (bf16[256,1024]{1,0:T(8,128)(2,1)}, bf16[256,1024]{1,0:T(8,128)(2,1)S(1)}, u32[]{:S(2)}) copy-start(bf16[256,1024]{1,0:T(8,128)(2,1)S(1)} %reshape.392) | copy-start | bytes 1572868
  187.9 59.2 %copy-start.68 = (s32[32]{0:T(128)S(1)}, s32[32]{0:T(128)}, u32[]{:S(2)}) copy-start(s32[32]{0:T(128)} %param.23) | copy-start | bytes 388
  187.9 124.0 %copy-start.69 = (s32[32]{0:T(128)S(1)}, s32[32]{0:T(128)}, u32[]{:S(2)}) copy-start(s32[32]{0:T(128)} %param.24) | copy-start | bytes 388
  238.4 13.1 collective-permute-start.7
  240.6 20.1 %collective-permute-start.6 = (bf16[4,64,1024]{2,1,0:T(8,128)(2,1)}, bf16[4,64,1024]{2,1,0:T(8,128)(2,1)S(1)}, u32[]{:S(2)}, u32[]{:S(2)}) collective-permute-start(bf16[4,64,1024]{2,1,0:T(8,128)(2,1)} %bitcast.7), channel_id=1, source_target_pairs={{0,8},{4,12},{8,16},{12,20},{16,24},{20,28},{1,9},{5,13},{9,17},{1... | collective-permute-start | bytes 1572872 | tf_op jit(solution)/shard_map/ppermute | solution.py:16
  244.0 32.8 %collective-permute-start.5 = (bf16[4,64,1024]{2,1,0:T(8,128)(2,1)}, bf16[4,64,1024]{2,1,0:T(8,128)(2,1)S(1)}, u32[]{:S(2)}, u32[]{:S(2)}) collective-permute-start(bf16[4,64,1024]{2,1,0:T(8,128)(2,1)} %bitcast.7), channel_id=1, source_target_pairs={{0,12},{4,16},{8,20},{12,24},{16,28},{1,13},{5,17},{9,21},{13,25},... | collective-permute-start | bytes 1572872 | tf_op jit(solution)/shard_map/ppermute | solution.py:16
  247.3 87.1 %collective-permute-start.4 = (bf16[4,64,1024]{2,1,0:T(8,128)(2,1)}, bf16[4,64,1024]{2,1,0:T(8,128)(2,1)}, u32[]{:S(2)}, u32[]{:S(2)}) collective-permute-start(bf16[4,64,1024]{2,1,0:T(8,128)(2,1)} %bitcast.7), channel_id=1, source_target_pairs={{0,16},{4,20},{8,24},{12,28},{1,17},{5,21},{9,25},{13,29},{2,18},{... | collective-permute-start | bytes 1572872 | tf_op jit(solution)/shard_map/ppermute | solution.py:16
  249.4 89.5 %collective-permute-start.3 = (bf16[4,64,1024]{2,1,0:T(8,128)(2,1)}, bf16[4,64,1024]{2,1,0:T(8,128)(2,1)}, u32[]{:S(2)}, u32[]{:S(2)}) collective-permute-start(bf16[4,64,1024]{2,1,0:T(8,128)(2,1)} %bitcast.6), channel_id=1, source_target_pairs={{0,4},{4,8},{8,12},{12,16},{16,20},{20,24},{24,28},{1,5},{5,9},{9,... | collective-permute-start | bytes 1572872 | tf_op jit(solution)/shard_map/ppermute | solution.py:16
  251.6 60.6 %copy-start.51 = (bf16[4,64,1024]{2,1,0:T(8,128)(2,1)}, bf16[4,64,1024]{2,1,0:T(8,128)(2,1)S(1)}, u32[]{:S(2)}) copy-start(bf16[4,64,1024]{2,1,0:T(8,128)(2,1)S(1)} %collective-permute-done.7) | copy-start | bytes 1572868
  251.6 91.4 %collective-permute-start.2 = (bf16[4,64,1024]{2,1,0:T(8,128)(2,1)}, bf16[4,64,1024]{2,1,0:T(8,128)(2,1)}, u32[]{:S(2)}, u32[]{:S(2)}) collective-permute-start(bf16[4,64,1024]{2,1,0:T(8,128)(2,1)} %bitcast.6), channel_id=1, source_target_pairs={{0,8},{4,12},{8,16},{12,20},{16,24},{20,28},{1,9},{5,13},{9,17},{1... | collective-permute-start | bytes 1572872 | tf_op jit(solution)/shard_map/ppermute | solution.py:16
  260.7 51.4 %copy-start.52 = (bf16[4,64,1024]{2,1,0:T(8,128)(2,1)}, bf16[4,64,1024]{2,1,0:T(8,128)(2,1)S(1)}, u32[]{:S(2)}) copy-start(bf16[4,64,1024]{2,1,0:T(8,128)(2,1)S(1)} %collective-permute-done.6) | copy-start | bytes 1572868
  260.7 86.4 %collective-permute-start.1 = (bf16[4,64,1024]{2,1,0:T(8,128)(2,1)}, bf16[4,64,1024]{2,1,0:T(8,128)(2,1)}, u32[]{:S(2)}, u32[]{:S(2)}) collective-permute-start(bf16[4,64,1024]{2,1,0:T(8,128)(2,1)} %bitcast.6), channel_id=1, source_target_pairs={{0,12},{4,16},{8,20},{12,24},{16,28},{1,13},{5,17},{9,21},{13,25},... | collective-permute-start | bytes 1572872 | tf_op jit(solution)/shard_map/ppermute | solution.py:16
  276.8 74.5 %collective-permute-start = (bf16[4,64,1024]{2,1,0:T(8,128)(2,1)}, bf16[4,64,1024]{2,1,0:T(8,128)(2,1)}, u32[]{:S(2)}, u32[]{:S(2)}) collective-permute-start(bf16[4,64,1024]{2,1,0:T(8,128)(2,1)} %bitcast.6), channel_id=1, source_target_pairs={{0,16},{4,20},{8,24},{12,28},{1,17},{5,21},{9,25},{13,29},{2,18},{... | collective-permute-start | bytes 1572872 | tf_op jit(solution)/shard_map/ppermute | solution.py:16
  484.8 45.3 %collective-permute-start.12 = (bf16[4,64,1024]{2,1,0:T(8,128)(2,1)}, bf16[4,64,1024]{2,1,0:T(8,128)(2,1)}, u32[]{:S(2)}, u32[]{:S(2)}) collective-permute-start(bf16[4,64,1024]{2,1,0:T(8,128)(2,1)} %convert_element_type.224), channel_id=1, source_target_pairs={{4,0},{8,4},{12,8},{16,12},{20,16},{24,20},{28,24},{5,1},{9,5},{13... | collective-permute-start | bytes 1572872 | tf_op jit(solution)/shard_map/ppermute | solution.py:16
  491.1 40.3 %collective-permute-start.15 = (bf16[4,64,1024]{2,1,0:T(8,128)(2,1)}, bf16[4,64,1024]{2,1,0:T(8,128)(2,1)}, u32[]{:S(2)}, u32[]{:S(2)}) collective-permute-start(bf16[4,64,1024]{2,1,0:T(8,128)(2,1)} %convert_element_type.230), channel_id=1, source_target_pairs={{16,0},{20,4},{24,8},{28,12},{17,1},{21,5},{25,9},{29,13},{18,2},{... | collective-permute-start | bytes 1572872 | tf_op jit(solution)/shard_map/ppermute | solution.py:16
  497.4 35.3 %collective-permute-start.14 = (bf16[4,64,1024]{2,1,0:T(8,128)(2,1)}, bf16[4,64,1024]{2,1,0:T(8,128)(2,1)}, u32[]{:S(2)}, u32[]{:S(2)}) collective-permute-start(bf16[4,64,1024]{2,1,0:T(8,128)(2,1)} %convert_element_type.228), channel_id=1, source_target_pairs={{12,0},{16,4},{20,8},{24,12},{28,16},{13,1},{17,5},{21,9},{25,13},... | collective-permute-start | bytes 1572872 | tf_op jit(solution)/shard_map/ppermute | solution.py:16
  503.6 45.7 %collective-permute-start.13 = (bf16[4,64,1024]{2,1,0:T(8,128)(2,1)}, bf16[4,64,1024]{2,1,0:T(8,128)(2,1)}, u32[]{:S(2)}, u32[]{:S(2)}) collective-permute-start(bf16[4,64,1024]{2,1,0:T(8,128)(2,1)} %convert_element_type.226), channel_id=1, source_target_pairs={{8,0},{12,4},{16,8},{20,12},{24,16},{28,20},{9,1},{13,5},{17,9},{2... | collective-permute-start | bytes 1572872 | tf_op jit(solution)/shard_map/ppermute | solution.py:16
  520.2 31.5 %collective-permute-start.8 = (bf16[4,64,1024]{2,1,0:T(8,128)(2,1)}, bf16[4,64,1024]{2,1,0:T(8,128)(2,1)}, u32[]{:S(2)}, u32[]{:S(2)}) collective-permute-start(bf16[4,64,1024]{2,1,0:T(8,128)(2,1)} %convert_element_type.215), channel_id=1, source_target_pairs={{4,0},{8,4},{12,8},{16,12},{20,16},{24,20},{28,24},{5,1},{9,5},{13... | collective-permute-start | bytes 1572872 | tf_op jit(solution)/shard_map/ppermute | solution.py:16
  530.1 21.6 %collective-permute-start.11 = (bf16[4,64,1024]{2,1,0:T(8,128)(2,1)}, bf16[4,64,1024]{2,1,0:T(8,128)(2,1)}, u32[]{:S(2)}, u32[]{:S(2)}) collective-permute-start(bf16[4,64,1024]{2,1,0:T(8,128)(2,1)} %convert_element_type.221), channel_id=1, source_target_pairs={{16,0},{20,4},{24,8},{28,12},{17,1},{21,5},{25,9},{29,13},{18,2},{... | collective-permute-start | bytes 1572872 | tf_op jit(solution)/shard_map/ppermute | solution.py:16
  531.4 20.3 %collective-permute-start.10 = (bf16[4,64,1024]{2,1,0:T(8,128)(2,1)}, bf16[4,64,1024]{2,1,0:T(8,128)(2,1)}, u32[]{:S(2)}, u32[]{:S(2)}) collective-permute-start(bf16[4,64,1024]{2,1,0:T(8,128)(2,1)} %convert_element_type.219), channel_id=1, source_target_pairs={{12,0},{16,4},{20,8},{24,12},{28,16},{13,1},{17,5},{21,9},{25,13},... | collective-permute-start | bytes 1572872 | tf_op jit(solution)/shard_map/ppermute | solution.py:16
  532.7 19.0 %collective-permute-start.9 = (bf16[4,64,1024]{2,1,0:T(8,128)(2,1)}, bf16[4,64,1024]{2,1,0:T(8,128)(2,1)}, u32[]{:S(2)}, u32[]{:S(2)}) collective-permute-start(bf16[4,64,1024]{2,1,0:T(8,128)(2,1)} %convert_element_type.217), channel_id=1, source_target_pairs={{8,0},{12,4},{16,8},{20,12},{24,16},{28,20},{9,1},{13,5},{17,9},{2... | collective-permute-start | bytes 1572872 | tf_op jit(solution)/shard_map/ppermute | solution.py:16
  574.0 111.3 %reduce-scatter.9.cloned.1.call-start = ((), (), s32[]{:S(2)}) async-start(), calls=%async_computation.16 | async-start | bytes 2621440 | tf_op jit(solution)/shard_map/reduce_scatter | solution.py:270
  588.1 151.3 %reduce-scatter.19.cloned.1.call-start = ((), (), s32[]{:S(2)}) async-start(), calls=%async_computation.21 | async-start | bytes 4718592 | tf_op jit(solution)/shard_map/reduce_scatter | solution.py:302
  591.1 203.3 %reduce-scatter.15.cloned.1.call-start = ((), (), s32[]{:S(2)}) async-start(), calls=%async_computation.19 | async-start | bytes 4718592 | tf_op jit(solution)/shard_map/reduce_scatter | solution.py:300
  594.8 295.4 %reduce-scatter.17.cloned.1.call-start = ((), (), s32[]{:S(2)}) async-start(), calls=%async_computation.20 | async-start | bytes 14155776 | tf_op jit(solution)/shard_map/reduce_scatter | solution.py:301
  603.4 382.6 %reduce-scatter.13.cloned.1.call-start = ((), (), s32[]{:S(2)}) async-start(), calls=%async_computation.18 | async-start | bytes 14155776 | tf_op jit(solution)/shard_map/reduce_scatter | solution.py:299
  608.1 84.9 %copy-start.36 = (bf16[256,1024]{1,0:T(8,128)(2,1)}, bf16[256,1024]{1,0:T(8,128)(2,1)S(1)}, u32[]{:S(2)}) copy-start(bf16[256,1024]{1,0:T(8,128)(2,1)S(1)} %reshape.404) | copy-start | bytes 1572868
  693.1 412.4 %reduce-scatter.21.cloned.1.call-start = ((), (), s32[]{:S(2)}) async-start(), calls=%async_computation.22 | async-start | bytes 18874368 | tf_op jit(solution)/shard_map/reduce_scatter | solution.py:303
  704.9 520.0 %reduce-scatter.23.cloned.1.call-start = ((), (), s32[]{:S(2)}) async-start(), calls=%async_computation.23 | async-start | bytes 18874368 | tf_op jit(solution)/shard_map/reduce_scatter | solution.py:304
  716.7 668.8 %all-reduce.9.cloned.1.call-start = ((), (), s32[]{:S(2)}) async-start(), calls=%async_computation.25 | async-start | bytes 8388608 | tf_op jit(solution)/shard_map/psum | solution.py:307
  1108.2 120.2 %copy-start.67 = (f32[1024]{0:T(1024)S(1)}, f32[1024]{0:T(1024)}, u32[]{:S(2)}) copy-start(f32[1024]{0:T(1024)} %param.39) | copy-start | bytes 12292
  1227.6 289.6 %all-reduce.7.cloned.1.call-start = ((), (), s32[]{:S(2)}) async-start(), calls=%async_computation.24 | async-start | bytes 155648 | tf_op jit(solution)/shard_map/psum | solution.py:293
  1391.7 137.1 %copy-start.1 = (f32[8,1024]{1,0:T(8,128)S(1)}, f32[8,1024]{1,0:T(8,128)}, u32[]{:S(2)}) copy-start(f32[8,1024]{1,0:T(8,128)} %param.25) | copy-start | bytes 98308
  (57 other events, 444.1 us)
Sparse Core Ops, SparseCore 0:
  9.9 48.2 all-gather.8
  64.1 45.9 all-gather.12
  112.2 44.6 all-gather.10
  158.6 26.5 all-gather.14
  187.0 45.5 all-gather.16
  234.3 68.0 all-gather.18
  304.2 65.4 all-gather.22
  371.7 54.3 all-gather.20
  574.2 65.0 reduce-scatter.10
  642.1 43.1 reduce-scatter.8
  688.7 50.6 reduce-scatter.18
  743.0 51.3 reduce-scatter.14
  797.8 92.3 reduce-scatter.16
  893.6 92.3 reduce-scatter.12
  989.5 115.9 reduce-scatter.20
  1108.9 115.9 reduce-scatter.22
  1228.7 156.7 all-reduce.8
  1394.6 122.5 all-reduce.6
where the time goes:
time: 1550 us; the launch traced here: 1540 us
  waiting for transfers between devices  1030 us (66%)
  local copies, waits for them, and re-layouts  198 us (13%)
  matrix products  160 us (10%)
  starting transfers between devices  85.1 us (5%)
  other arithmetic  46.9 us (3%)
  between operations  15.9 us (1%)
    psum x1, waiting for transfers between devices, per_device(): lax.psum(reduced[0].astype(jnp.bfloat16), 'tile').astype(jnp.float32)  141 us
    psum x1, waiting for transfers between devices, per_device(): lax.psum((d_embed, d_gain1, d_shift1, d_gain2, d_shift2, d_gain3, d_shift...  121 us
    reduce_scatter x1, waiting for transfers between devices, per_device(): lax.psum_scatter(mat_grads[4], 'frame', scatter_dimension=0, tiled=True)  117 us
    reduce_scatter x1, waiting for transfers between devices, per_device(): lax.psum_scatter(mat_grads[5], 'frame', scatter_dimension=0, tiled=True)  117 us
    reduce_scatter x1, waiting for transfers between devices, per_device(): lax.psum_scatter(mat_grads[2], 'frame', scatter_dimension=0, tiled=True)  94.1 us
    reduce_scatter x1, waiting for transfers between devices, per_device(): lax.psum_scatter(mat_grads[0], 'frame', scatter_dimension=0, tiled=True)  93.4 us
    ppermute x16, starting transfers between devices, from_behind(): return lax.ppermute(x, axis, pairs)  83.9 us
    reduce_scatter x1, waiting for transfers between devices, per_device(): lax.psum_scatter(mat_grads[1], 'frame', scatter_dimension=0, tiled=True)  53.2 us
  transfers between devices with their start and end apart: 34, of which 15 were waited for; matrix products, arithmetic and copies ran while one was open for 20% of the time, Pallas kernels for 0%

commit v1 on v0

v1 whole, which is shorter than its diff:
```python
import functools

import jax
import jax.numpy as jnp
from jax import lax
from jax.experimental import pallas as pl
from jax.experimental.pallas import tpu as pltpu
from jax.sharding import PartitionSpec as P

HD = 64
LANES = 128
EPS = 1e-5
MESH = pl.DeviceIdType.MESH
F32 = jnp.float32
BF16 = jnp.bfloat16
VMEM_SPEC = pl.BlockSpec(memory_space=pltpu.VMEM)
HBM_SPEC = pl.BlockSpec(memory_space=pltpu.HBM)


def params(**kw):
    return pltpu.CompilerParams(vmem_limit_bytes=58 * 1024 * 1024, **kw)


def at(j, size):
    return pl.ds(pl.multiple_of(j * size, size), size)


def each(n, fn):
    def step(i, carry):
        fn(i)
        return carry

    lax.fori_loop(0, n, step, 0)


def dot(a, b):
    return jnp.dot(a, b, preferred_element_type=F32)


def dot_nt(a, b):
    return lax.dot_general(a, b, (((1,), (1,)), ((), ())), preferred_element_type=F32)


def dot_tn(a, b):
    return lax.dot_general(a, b, (((0,), (0,)), ((), ())), preferred_element_type=F32)


def normed(h):
    cen = h - jnp.mean(h, -1, keepdims=True)
    inv = lax.rsqrt(jnp.mean(cen * cen, -1, keepdims=True) + EPS)
    return cen * inv, inv


ROWS = 32


def norm_rows(load, gain_ref, shift_ref, unit_ref):
    def step(i):
        rows = at(i, ROWS)
        xhat, _ = normed(load(rows))
        unit_ref[rows, :] = (xhat * gain_ref[...] + shift_ref[...]).astype(BF16)

    each(unit_ref.shape[0] // ROWS, step)


def fold(x):
    return jnp.sum(x.reshape(x.shape[0] // 8, 8, x.shape[1]), 0)


def norm_back(load, du_ref, gain_ref, dgain_ref, dshift_ref, acc_ref, store):
    acc_ref[...] = jnp.zeros_like(acc_ref)

    def step(i):
        rows = at(i, ROWS)
        xhat, inv = normed(load(rows))
        du = du_ref[rows, :]
        acc_ref[0] += fold(du * xhat)
        acc_ref[1] += fold(du)
        dx = du * gain_ref[...]
        dh = inv * (
            dx - jnp.mean(dx, -1, keepdims=True) - xhat * jnp.mean(dx * xhat, -1, keepdims=True)
        )
        store(rows, dh)

    each(du_ref.shape[0] // ROWS, step)
    dgain_ref[...] = jnp.sum(acc_ref[0], 0, keepdims=True)
    dshift_ref[...] = jnp.sum(acc_ref[1], 0, keepdims=True)


def head_masks():
    lane = lax.broadcasted_iota(jnp.int32, (1, LANES), 1)
    low = jnp.where(lane < HD, 1.0, 0.0)
    return low.astype(BF16), (1.0 - low).astype(BF16)


def head_probs(qm, k, bias_ref):
    s = dot_nt(qm, k) * (HD**-0.5)
    if bias_ref is not None:
        s = s + bias_ref[...]
    e = jnp.exp(s - jnp.max(s, -1, keepdims=True))
    return e * (1.0 / jnp.sum(e, -1, keepdims=True))


def attention(qkv_ref, bias_ref, mixed_ref):
    width = mixed_ref.shape[1]
    per = width // LANES
    masks = head_masks()

    def pair(p):
        q, k, v = (qkv_ref[:, at(p + i * per, LANES)] for i in range(3))
        out = 0.0
        for m in masks:
            out = out + dot(head_probs(q * m, k, bias_ref).astype(BF16), v * m)
        mixed_ref[:, at(p, LANES)] = out.astype(BF16)

    each(per, pair)


def attention_back(qkv_ref, bias_ref, dmix_ref, dqkv_ref):
    width = dmix_ref.shape[1]
    per = width // LANES
    masks = head_masks()
    scale = HD**-0.5

    def pair(p):
        q, k, v = (qkv_ref[:, at(p + i * per, LANES)] for i in range(3))
        dm = dmix_ref[:, at(p, LANES)]
        dq = dk = dv = 0.0
        for m in masks:
            qm = q * m
            dmm = dm * m
            probs = head_probs(qm, k, bias_ref)
            dp = dot_nt(dmm, v)
            ds = probs * (dp - jnp.sum(probs * dp, -1, keepdims=True))
            ds = ds.astype(BF16)
            dq = dq + dot(ds, k * m)
            dk = dk + dot_tn(ds, qm)
            dv = dv + dot_tn(probs.astype(BF16), dmm)
        dqkv_ref[:, at(p, LANES)] = (dq * scale).astype(BF16)
        dqkv_ref[:, at(p + per, LANES)] = (dk * scale).astype(BF16)
        dqkv_ref[:, at(p + 2 * per, LANES)] = dv.astype(BF16)

    each(per, pair)


def matmul(x_ref, w_ref, block, store):
    def step(j):
        cols = at(j, block)
        store(cols, dot(x_ref[...], w_ref[:, cols]))

    each(w_ref.shape[1] // block, step)


def matmul_nt(x_ref, w_ref, block, store):
    def step(j):
        rows = at(j, block)
        store(rows, dot_nt(x_ref[...], w_ref[rows, :]))

    each(w_ref.shape[0] // block, step)


def attn_fwd_kernel(masked, base_ref, added_ref, gain_ref, shift_ref, wqkv_ref, wo_ref, *rest):
    if masked:
        bias_ref, unit_ref, qkv_ref, mixed_ref, after_ref = rest
    else:
        bias_ref = None
        unit_ref, qkv_ref, mixed_ref, after_ref = rest

    def load(rows):
        return base_ref[rows, :].astype(F32) + added_ref[...]

    norm_rows(load, gain_ref, shift_ref, unit_ref)

    def put_qkv(cols, y):
        qkv_ref[:, cols] = y.astype(BF16)

    matmul(unit_ref, wqkv_ref, 512, put_qkv)
    attention(qkv_ref, bias_ref, mixed_ref)

    def put_after(cols, y):
        y = y + base_ref[:, cols].astype(F32) + added_ref[:, cols]
        after_ref[:, cols] = y.astype(after_ref.dtype)

    matmul(mixed_ref, wo_ref, 512, put_after)


def attn_fwd(base, added, gain, shift, wqkv, wo, bias, out_type, name):
    rows, width = base.shape
    ins = [base, added, gain, shift, wqkv, wo] + ([bias] if bias is not None else [])
    shapes = [(width, BF16), (3 * width, BF16), (width, BF16), (width, out_type)]
    return pl.pallas_call(
        functools.partial(attn_fwd_kernel, bias is not None),
        out_shape=[jax.ShapeDtypeStruct((rows, w), d) for w, d in shapes],
        in_specs=[VMEM_SPEC] * len(ins),
        out_specs=[VMEM_SPEC] * 4,
        compiler_params=params(),
        name=name,
    )(*ins)


def attn_bwd_kernel(masked, base_ref, added_ref, gain_ref, wqkv_ref, wo_ref, dout_ref, qkv_ref, *rest):
    if masked:
        bias_ref, *rest = rest
    else:
        bias_ref = None
    dlow_ref, dqkv_ref, dbase_ref, dgain_ref, dshift_ref, dmix_ref, du_ref, acc_ref = rest

    def cast(i):
        rows = at(i, ROWS)
        dlow_ref[rows, :] = dout_ref[rows, :].astype(BF16)

    each(dlow_ref.shape[0] // ROWS, cast)

    def put_mix(rows, y):
        dmix_ref[:, rows] = y.astype(BF16)

    matmul_nt(dlow_ref, wo_ref, 512, put_mix)
    attention_back(qkv_ref, bias_ref, dmix_ref, dqkv_ref)

    def put_du(rows, y):
        du_ref[:, rows] = y

    matmul_nt(dqkv_ref, wqkv_ref, 256, put_du)

    def load(rows):
        return base_ref[rows, :].astype(F32) + added_ref[...]

    def store(rows, dh):
        dbase_ref[rows, :] = (dout_ref[rows, :].astype(F32) + dh).astype(dbase_ref.dtype)

    norm_back(load, du_ref, gain_ref, dgain_ref, dshift_ref, acc_ref, store)


def attn_bwd(base, added, gain, wqkv, wo, dout, qkv, bias, out_type, name):
    rows, width = base.shape
    ins = [base, added, gain, wqkv, wo, dout, qkv] + ([bias] if bias is not None else [])
    outs = [
        jax.ShapeDtypeStruct((rows, width), BF16),
        jax.ShapeDtypeStruct((rows, 3 * width), BF16),
        jax.ShapeDtypeStruct((rows, width), out_type),
        jax.ShapeDtypeStruct((1, width), F32),
        jax.ShapeDtypeStruct((1, width), F32),
    ]
    return pl.pallas_call(
        functools.partial(attn_bwd_kernel, bias is not None),
        out_shape=outs,
        in_specs=[VMEM_SPEC] * len(ins),
        out_specs=[VMEM_SPEC] * len(outs),
        scratch_shapes=[
            pltpu.VMEM((rows, width), BF16),
            pltpu.VMEM((rows, width), F32),
            pltpu.VMEM((2, 8, width), F32),
        ],
        compiler_params=params(),
        name=name,
    )(*ins)


GELU_A = 0.7978845608
GELU_B = 0.044715


def ffn_fwd_kernel(after_ref, gain_ref, shift_ref, win_ref, bin_ref, wout_ref, bout_ref,
                   unit_ref, pre_ref, act_ref, res_ref):
    norm_rows(lambda rows: after_ref[rows, :], gain_ref, shift_ref, unit_ref)

    def put_pre(cols, y):
        v = y + bin_ref[:, cols]
        pre_ref[:, cols] = v
        act = 0.5 * v * (1.0 + jnp.tanh(GELU_A * (v + GELU_B * v * v * v)))
        act_ref[:, cols] = act.astype(BF16)

    matmul(unit_ref, win_ref, 512, put_pre)

    def put_res(cols, y):
        res_ref[:, cols] = (after_ref[:, cols] + y + bout_ref[:, cols]).astype(BF16)

    matmul(act_ref, wout_ref, 256, put_res)


def ffn_fwd(after, gain, shift, win, b_in, wout, b_out):
    rows, width = after.shape
    ff = win.shape[1]
    return pl.pallas_call(
        ffn_fwd_kernel,
        out_shape=[
            jax.ShapeDtypeStruct((rows, width), BF16),
            jax.ShapeDtypeStruct((rows, ff), F32),
            jax.ShapeDtypeStruct((rows, ff), BF16),
            jax.ShapeDtypeStruct((rows, width), BF16),
        ],
        in_specs=[VMEM_SPEC] * 7,
        out_specs=[VMEM_SPEC] * 4,
        compiler_params=params(),
        name="ffn_forward",
    )(after, gain, shift, win, b_in, wout, b_out)


def ffn_bwd_kernel(g_ref, pre_ref, after_ref, gain_ref, win_ref, wout_ref,
                   dpre_ref, dafter_ref, dgain_ref, dshift_ref, dbin_ref, dbout_ref, du_ref, acc_ref):
    def put_dpre(rows, y):
        v = pre_ref[:, rows]
        t = jnp.tanh(GELU_A * (v + GELU_B * v * v * v))
        slope = 0.5 * (1.0 + t) + 0.5 * v * (1.0 - t * t) * GELU_A * (1.0 + 3.0 * GELU_B * v * v)
        d = (y * slope).astype(BF16)
        dpre_ref[:, rows] = d
        dbin_ref[:, rows] = jnp.sum(d.astype(F32), 0, keepdims=True)

    matmul_nt(g_ref, wout_ref, 512, put_dpre)

    def put_du(rows, y):
        du_ref[:, rows] = y

    matmul_nt(dpre_ref, win_ref, 256, put_du)
    dbout_ref[...] = jnp.zeros_like(dbout_ref)

    def store(rows, dh):
        g = g_ref[rows, :].astype(F32)
        dafter_ref[rows, :] = g + dh
        dbout_ref[...] += jnp.sum(g, 0, keepdims=True)

    norm_back(lambda rows: after_ref[rows, :], du_ref, gain_ref, dgain_ref, dshift_ref, acc_ref, store)


def ffn_bwd(g, pre, after, gain, win, wout):
    rows, width = after.shape
    ff = win.shape[1]
    row = lambda n: jax.ShapeDtypeStruct((1, n), F32)
    return pl.pallas_call(
        ffn_bwd_kernel,
        out_shape=[
            jax.ShapeDtypeStruct((rows, ff), BF16),
            jax.ShapeDtypeStruct((rows, width), F32),
            row(width), row(width), row(ff), row(width),
        ],
        in_specs=[VMEM_SPEC] * 6,
        out_specs=[VMEM_SPEC] * 6,
        scratch_shapes=[pltpu.VMEM((rows, width), F32), pltpu.VMEM((2, 8, width), F32)],
        compiler_params=params(),
        name="ffn_backward",
    )(g, pre, after, gain, win, wout)


def wgrad_kernel(shard, left_ref, left2_ref, right_ref, right2_ref, out_ref, lt_ref):
    tok = left_ref.shape[0]
    lt_ref[:, :tok] = left_ref[...].T
    lt_ref[:, tok:] = left2_ref[...].T
    col_blocks = right_ref.shape[1] // 1024
    for rb in range(shard // 128):
        for cb in range(col_blocks):
            def step(j, rb=rb, cb=cb):
                cols = pl.ds(pl.multiple_of(cb * 1024 + j * 512, 512), 512)
                a = jnp.concatenate(
                    [lt_ref[q * shard + rb * 128 : q * shard + (rb + 1) * 128, :] for q in range(4)], 0
                )
                y = dot(a[:, :tok], right_ref[:, cols]) + dot(a[:, tok:], right2_ref[:, cols])
                y = y.astype(BF16)
                for q in range(4):
                    out_ref[rb * col_blocks + cb, q, :, at(j, 512)] = y[q * 128 : (q + 1) * 128]

            each(2, step)


def wgrad_units(left, right, shard, core, name):
    tok = left.shape[0]
    parts = left.reshape(tok, 4, 2, shard)
    mine = lax.dynamic_index_in_dim(parts, core, 2, False).reshape(tok, 4 * shard)
    other = lax.dynamic_index_in_dim(parts, 1 - core, 2, False).reshape(tok, 4 * shard)
    swap = [(i, i ^ 1) for i in range(8)]
    other = lax.ppermute(other, "frame", swap)
    right2 = lax.ppermute(right, "frame", swap)
    units = (shard // 128) * (right.shape[1] // 1024)
    return pl.pallas_call(
        functools.partial(wgrad_kernel, shard),
        out_shape=jax.ShapeDtypeStruct((units, 4, 128, 1024), BF16),
        in_specs=[VMEM_SPEC] * 4,
        out_specs=VMEM_SPEC,
        scratch_shapes=[pltpu.VMEM((4 * shard, 2 * tok), BF16)],
        compiler_params=params(),
        name=name,
    )(mine, other, right, right2)


def xor(a, b):
    bit = lax.rem(a // b, 2)
    return a + b - 2 * b * bit


def greet(partners):
    barrier = pltpu.get_barrier_semaphore()
    for p in partners:
        pl.semaphore_signal(barrier, inc=1, device_id=p, device_id_type=MESH)
    pl.semaphore_wait(barrier, len(partners))


def remote(src, dst, ssem, rsem, dev):
    return pltpu.make_async_remote_copy(
        src_ref=src, dst_ref=dst, send_sem=ssem, recv_sem=rsem, device_id=dev, device_id_type=MESH
    )


def xor_any(a, bits):
    for b in (1, 2, 4, 8, 16):
        if bits & b:
            a = xor(a, b)
    return a


def swap_kernel(axes, src_of, dst_of, src_ref, dst_ref, ssem, rsem, lsem):
    f = lax.axis_index("frame")
    t = lax.axis_index("tile")
    nf = 8 if "frame" in axes else 1
    nt = 4 if "tile" in axes else 1
    todo = [(a, b) for a in range(nf) for b in range(nt) if (a, b) != (0, 0)]
    devs = [(xor_any(f, a), xor_any(t, b)) for a, b in todo]
    greet(devs)
    own = pltpu.make_async_copy(src_ref.at[src_of(f, t)], dst_ref.at[dst_of(f, t)], lsem)
    own.start()
    for i, d in enumerate(devs):
        remote(src_ref.at[src_of(*d)], dst_ref.at[dst_of(f, t)], ssem.at[i], rsem.at[i], d).start()
    own.wait()
    for i, d in enumerate(devs):
        remote(src_ref.at[src_of(*d)], dst_ref.at[dst_of(*d)], ssem.at[i], rsem.at[i], d).wait()


def swap_blocks(x, shape, axes, src_of, dst_of, cid, name):
    n = (8 if "frame" in axes else 1) * (4 if "tile" in axes else 1)
    return pl.pallas_call(
        functools.partial(swap_kernel, axes, src_of, dst_of),
        out_shape=jax.ShapeDtypeStruct(shape, x.dtype),
        in_specs=[HBM_SPEC],
        out_specs=HBM_SPEC,
        scratch_shapes=[
            pltpu.SemaphoreType.DMA((n - 1,)),
            pltpu.SemaphoreType.DMA((n - 1,)),
            pltpu.SemaphoreType.DMA,
        ],
        compiler_params=params(collective_id=cid, has_side_effects=True),
        name=name,
    )(x)


def gather_chunks(shapes):
    out = []
    for i, (rows, cols) in enumerate(shapes):
        step = rows
        while step * cols > 200 * 1024 and step % 32 == 0:
            step //= 2
        out += [(i, r, step) for r in range(0, rows, step)]
    return out


def gather_kernel(n_arr, chunks, *refs):
    ins = refs[:n_arr]
    outs = refs[n_arr : 2 * n_arr]
    ssem, rsem, lsem = refs[2 * n_arr :]
    f = lax.axis_index("frame")
    t = lax.axis_index("tile")
    odd = lax.rem(t, 2)
    fx, fy = xor(f, 2), xor(f, 4)
    first = fx + (fy - fx) * odd
    second = fy + (fx - fy) * odd
    diag = xor_any(f, 6)
    tz = xor(t, 1)
    sib = xor(f, 1)
    to_sib, to_first, to_second, to_z = (sib, t), (first, t), (second, t), (f, tz)
    greet([to_sib, (fx, t), (fy, t), to_z])

    def piece(k, owner, chunk_only=True):
        a, r, n = chunks[k]
        return outs[a].at[pl.ds(pl.multiple_of(owner * ins[a].shape[0] + r, 16), n)]

    def own(k):
        a, r, n = chunks[k]
        return ins[a].at[pl.ds(r, n)]

    def copy(k, kind):
        dev = (to_first, to_second, to_z, to_sib, to_sib, to_sib, to_sib)[kind]
        owner = (f, first, first, f, first, diag, second)[kind]
        src = own(k) if kind in (0, 3) else piece(k, owner)
        return remote(src, piece(k, owner), ssem.at[k, kind], rsem.at[k, kind], dev)

    def arrived(k, kind):
        owner = (first, diag, second, sib, xor(first, 1), xor(diag, 1), xor(second, 1))[kind]
        dst = piece(k, owner)
        remote(dst, dst, ssem.at[k, kind], rsem.at[k, kind], to_sib).wait_recv()

    n = len(chunks)
    for k in range(n):
        pltpu.make_async_copy(own(k), piece(k, f), lsem.at[k]).start()
    for k in range(min(2, n)):
        copy(k, 0).start()
    for k in range(n + 1):
        if k < n:
            copy(k, 3).start()
            arrived(k, 0)
            if k + 2 < n:
                copy(k + 2, 0).start()
            for kind in (1, 2, 4):
                copy(k, kind).start()
        if k >= 1:
            for kind in (1, 2):
                arrived(k - 1, kind)
                copy(k - 1, kind + 4).start()
    for k in range(n):
        for kind in (3, 4, 5, 6):
            arrived(k, kind)
        for kind in range(7):
            copy(k, kind).wait_send()
        pltpu.make_async_copy(own(k), piece(k, f), lsem.at[k]).wait()


def gather_weights(mats):
    chunks = gather_chunks([m.shape for m in mats])
    n = len(mats)
    return pl.pallas_call(
        functools.partial(gather_kernel, n, chunks),
        out_shape=[jax.ShapeDtypeStruct((8 * m.shape[0], m.shape[1]), m.dtype) for m in mats],
        in_specs=[HBM_SPEC] * n,
        out_specs=[HBM_SPEC] * n,
        scratch_shapes=[
            pltpu.SemaphoreType.DMA((len(chunks), 7)),
            pltpu.SemaphoreType.DMA((len(chunks), 7)),
            pltpu.SemaphoreType.DMA((len(chunks),)),
        ],
        compiler_params=params(collective_id=0, has_side_effects=True),
        name="gather_weights",
    )(*mats)


def add_into(dst, a, b, rows):
    def step(i):
        r = at(i, 16)
        dst[r, :] = (a[r, :].astype(F32) + b[r, :].astype(F32)).astype(dst.dtype)

    each(rows // 16, step)


def reduce_kernel(units, n_arr, *refs):
    grads = refs[:n_arr]
    small_ref = refs[n_arr]
    out_ref, small_out = refs[n_arr + 1 : n_arr + 3]
    (g_ref, r1, r2, zin, zpeer, sm, smr, lsem, s1s, s1r, s2s, s2r, zs, zr, zps, zpr, sms, smrs) = refs[n_arr + 3 :]
    f = lax.axis_index("frame")
    t = lax.axis_index("tile")
    q = f // 2
    leaf = (t == 0) | (t == 3)
    inner = jnp.logical_not(leaf)
    fx, fy, sib = xor(f, 2), xor(f, 4), xor(f, 1)
    qx, qy, qd = xor(q, 1), xor(q, 2), xor_any(q, 3)
    to_x, to_y, to_sib, to_z, to_peer = (fx, t), (fy, t), (sib, t), (f, xor(t, 1)), (f, 3 - t)
    greet([to_x, to_y, to_sib, to_z, to_peer])
    n = len(units)

    def hop(u):
        return (to_x, qx, to_y, qy) if u % 2 == 0 else (to_y, qy, to_x, qx)

    def src(u, piece):
        a, i = units[u]
        return grads[a].at[i, piece]

    def local(u):
        dev1, p1, dev2, p2 = hop(u)
        return (
            pltpu.make_async_copy(src(u, q), g_ref.at[u, 0], lsem.at[u, 0]),
            pltpu.make_async_copy(src(u, p2), g_ref.at[u, 1], lsem.at[u, 1]),
        )

    def step1(u):
        dev1, p1, dev2, p2 = hop(u)
        return (
            remote(src(u, p1), r1.at[u, 0], s1s.at[u, 0], s1r.at[u, 0], dev1),
            remote(src(u, qd), r1.at[u, 1], s1s.at[u, 1], s1r.at[u, 1], dev1),
        )

    def step2(u):
        return remote(g_ref.at[u, 1], r2.at[u], s2s.at[u], s2r.at[u], hop(u)[2])

    def to_inner(u):
        return remote(g_ref.at[u, 0], zin.at[u], zs.at[u], zr.at[u], to_z)

    def across(u):
        return remote(g_ref.at[u, 0], zpeer.at[u], zps.at[u], zpr.at[u], to_peer)

    def to_leaf(u):
        return remote(r2.at[u], zin.at[u], zs.at[u], zr.at[u], to_z)

    def emit(u, ref):
        def step(i):
            r = at(i, 16)
            out_ref[u, r, :] = ref[u, r, :].astype(F32)

        each(8, step)

    for u in range(n):
        for c in local(u):
            c.start()
    for u in range(min(4, n)):
        for c in step1(u):
            c.start()
    sm[0] = small_ref[...]

    def small_copy(i, dev):
        return remote(sm.at[i], smr.at[i], sms.at[i], smrs.at[i], dev)

    hops = (to_sib, to_x, to_y)
    small_copy(0, to_sib).start()
    for s in range(n + 4):
        if s < 3:
            small_copy(s, hops[s]).wait()
            sm[s + 1] = sm[s] + smr[s]
            if s < 2:
                small_copy(s + 1, hops[s + 1]).start()
            else:
                @pl.when(leaf)
                def _():
                    small_copy(3, to_z).start()
        if s == 4:
            @pl.when(inner)
            def _():
                small_copy(3, to_z).wait_recv()
                sm[4] = sm[3] + smr[3]
                small_copy(4, to_peer).start()
        if s == 6:
            @pl.when(inner)
            def _():
                small_copy(4, to_peer).wait()
                sm[5] = sm[4] + smr[4]
                remote(sm.at[5], smr.at[3], sms.at[3], smrs.at[3], to_z).start()
                small_out[...] = sm[5]
        if s == 8:
            @pl.when(leaf)
            def _():
                small_copy(3, to_z).wait()
                small_out[...] = smr[3]

        if s < n:
            u = s
            for c in step1(u):
                c.wait_recv()
            for c in local(u):
                c.wait()
            add_into(g_ref.at[u, 1], g_ref.at[u, 1], r1.at[u, 1], 128)
            step2(u).start()
            if u + 4 < n:
                for c in step1(u + 4):
                    c.start()
            add_into(g_ref.at[u, 0], g_ref.at[u, 0], r1.at[u, 0], 128)
        u = s - 1
        if 0 <= u < n:
            step2(u).wait_recv()
            add_into(g_ref.at[u, 0], g_ref.at[u, 0], r2.at[u], 128)

            @pl.when(leaf)
            def _(u=u):
                to_inner(u).start()

        u = s - 2
        if 0 <= u < n:
            @pl.when(inner)
            def _(u=u):
                to_inner(u).wait_recv()
                add_into(g_ref.at[u, 0], g_ref.at[u, 0], zin.at[u], 128)
                across(u).start()

        u = s - 3
        if 0 <= u < n:
            @pl.when(inner)
            def _(u=u):
                across(u).wait_recv()
                add_into(r2.at[u], g_ref.at[u, 0], zpeer.at[u], 128)
                to_leaf(u).start()
                emit(u, r2)

        u = s - 4
        if 0 <= u < n:
            @pl.when(leaf)
            def _(u=u):
                to_leaf(u).wait_recv()
                emit(u, zin)

    for u in range(n):
        for c in step1(u):
            c.wait_send()
        step2(u).wait_send()
        to_inner(u).wait_send()

    @pl.when(inner)
    def _():
        for u in range(n):
            across(u).wait_send()
        remote(sm.at[5], smr.at[3], sms.at[3], smrs.at[3], to_z).wait_send()


def reduce_units(grads, small):
    units = [(i, u) for i, g in enumerate(grads) for u in range(g.shape[0])]
    n = len(units)
    unit = grads[0].shape[2:]
    dma = pltpu.SemaphoreType.DMA
    return pl.pallas_call(
        functools.partial(reduce_kernel, units, len(grads)),
        out_shape=[
            jax.ShapeDtypeStruct((n,) + unit, F32),
            jax.ShapeDtypeStruct(small.shape, F32),
        ],
        in_specs=[HBM_SPEC] * len(grads) + [VMEM_SPEC],
        out_specs=[VMEM_SPEC] * 2,
        scratch_shapes=[
            pltpu.VMEM((n, 2) + unit, BF16),
            pltpu.VMEM((n, 2) + unit, BF16),
            pltpu.VMEM((n,) + unit, BF16),
            pltpu.VMEM((n,) + unit, BF16),
            pltpu.VMEM((n,) + unit, BF16),
            pltpu.VMEM((6,) + small.shape, F32),
            pltpu.VMEM((5,) + small.shape, F32),
            dma((n, 2)), dma((n, 2)), dma((n, 2)), dma((n,)), dma((n,)),
            dma((n,)), dma((n,)), dma((n,)), dma((n,)), dma((6,)), dma((6,)),
        ],
        compiler_params=params(collective_id=1, has_side_effects=True),
        name="reduce_gradients",
    )(*grads, small)


def per_device(on_boxes, tokens, out_grad, actions, segments, frame_mask, embed,
               ln1_gain, ln1_shift, spatial_qkv, spatial_out,
               ln2_gain, ln2_shift, temporal_qkv, temporal_out,
               ln3_gain, ln3_shift, ffn_in, ffn_in_bias, ffn_out, ffn_out_bias):
    frames_dev, tile_tokens, width = tokens.shape
    n_frame = lax.axis_size("frame")
    n_tile = lax.axis_size("tile")
    f = lax.axis_index("frame")
    t = lax.axis_index("tile")
    frames = frames_dev * n_frame
    place = tile_tokens // n_frame
    rows = frames_dev * tile_tokens
    row = lambda v: v[None, :]

    mats = (spatial_qkv, spatial_out, temporal_qkv, temporal_out, ffn_in, ffn_out)

    grad4 = out_grad.reshape(frames_dev, n_frame, place, width)
    if on_boxes:
        w_qs, w_os, w_qt, w_ot, w_in, w_out = gather_weights(mats)
        base1 = swap_blocks(tokens, tokens.shape, ("tile",),
                            lambda f, t: t, lambda f, t: t, 2, "tokens_to_frames")
        g = swap_blocks(grad4, (n_frame, frames_dev, place, width), ("frame",),
                        lambda f, t: (slice(None), f), lambda f, t: f, 3, "grad_to_places")
    else:
        w_qs, w_os, w_qt, w_ot, w_in, w_out = (lax.all_gather(m, "frame", axis=0, tiled=True) for m in mats)
        base1 = lax.all_to_all(tokens, "tile", 0, 0, tiled=True)
        g = lax.all_to_all(grad4.transpose(1, 0, 2, 3), "frame", 0, 0, tiled=True)
    base1 = base1.reshape(rows, width)
    g = g.reshape(rows, width)

    action = lax.dynamic_index_in_dim(actions, t, keepdims=False)
    added = lax.dynamic_slice_in_dim(embed, action, 1, 0)

    unit1, qkv1, mixed1, after1 = attn_fwd(
        base1, added, row(ln1_gain), row(ln1_shift), w_qs, w_os, None, BF16, "spatial_forward")

    blocks = n_frame * n_tile

    def turn(x, forward, cid, name):
        x = x.reshape(blocks, rows // blocks, width)
        if on_boxes:
            by_place = lambda f, t: 8 * t + f
            by_frame = lambda f, t: 4 * f + t
            a, b = (by_place, by_frame) if forward else (by_frame, by_place)
            y = swap_blocks(x, x.shape, ("frame", "tile"), a, b, cid, name)
        else:
            if forward:
                y = x.reshape(n_tile, n_frame, -1, width).transpose(1, 0, 2, 3)
                y = lax.all_to_all(y.reshape(x.shape), ("frame", "tile"), 0, 0, tiled=True)
            else:
                y = lax.all_to_all(x, ("frame", "tile"), 0, 0, tiled=True)
                y = y.reshape(n_frame, n_tile, -1, width).transpose(1, 0, 2, 3)
        return y.reshape(rows, width)

    base2 = turn(after1, True, 4, "frames_to_places")

    number = jnp.arange(rows, dtype=jnp.int32)
    of_frame, of_place = number // place, number % place
    seg_row = jnp.repeat(segments, place)
    open_row = jnp.repeat(frame_mask, place)
    allowed = (
        (seg_row[:, None] == seg_row[None, :])
        & (of_place[:, None] == of_place[None, :])
        & (of_frame[None, :] <= of_frame[:, None])
        & ((open_row[None, :] == 1) | (of_frame[None, :] == of_frame[:, None]))
    )
    bias = jnp.where(allowed, 0.0, -1e30).astype(F32)
    nothing = jnp.zeros((1, width), F32)
    unit2, qkv2, mixed2, after2 = attn_fwd(
        base2, nothing, row(ln2_gain), row(ln2_shift), w_qt, w_ot, bias, F32, "temporal_forward")
    unit3, pre, act, result = ffn_fwd(
        after2, row(ln3_gain), row(ln3_shift), w_in, row(ffn_in_bias), w_out, row(ffn_out_bias))
    d_pre, d_after2, dg3, ds3, d_bin, d_bout = ffn_bwd(g, pre, after2, row(ln3_gain), w_in, w_out)
    low2, d_qkv2, d_after1, dg2, ds2 = attn_bwd(
        base2, nothing, row(ln2_gain), w_qt, w_ot, d_after2, qkv2, bias, BF16, "temporal_backward")
    d_out1 = turn(d_after1, False, 5, "places_to_frames")
    low1, d_qkv1, d_start, dg1, ds1 = attn_bwd(
        base1, added, row(ln1_gain), w_qs, w_os, d_out1, qkv1, None, F32, "spatial_backward")

    tokens_grad = d_start.astype(BF16).reshape(n_tile, tile_tokens, width)
    result = result.reshape(n_frame, frames_dev, place, width)
    if on_boxes:
        tokens_grad = swap_blocks(tokens_grad, tokens.shape, ("tile",),
                                  lambda f, t: t, lambda f, t: t, 6, "tokens_grad_to_tiles")
        result = swap_blocks(result, grad4.shape, ("frame",),
                             lambda f, t: f, lambda f, t: (slice(None), f), 7, "result_to_tiles")
    else:
        tokens_grad = lax.all_to_all(tokens_grad, "tile", 0, 0, tiled=True)
        result = lax.all_to_all(result, "frame", 0, 0, tiled=True).transpose(1, 0, 2, 3)
    result = result.reshape(tokens.shape)

    one_hot = (action == jnp.arange(embed.shape[0], dtype=jnp.int32)).astype(F32)
    d_embed = one_hot[:, None] * jnp.sum(d_start, 0, keepdims=True)

    pairs = (
        (unit1, d_qkv1, "spatial_qkv_grad"),
        (mixed1, low1, "spatial_out_grad"),
        (unit2, d_qkv2, "temporal_qkv_grad"),
        (mixed2, low2, "temporal_out_grad"),
        (unit3, d_pre, "ffn_in_grad"),
        (act, g, "ffn_out_grad"),
    )
    if on_boxes:
        small = jnp.concatenate(
            [d_embed, dg1, ds1, dg2, ds2, dg3, ds3, d_bout, d_bin.reshape(-1, width)], 0)
        small = jnp.pad(small, ((0, -small.shape[0] % 8), (0, 0)))
        core = lax.rem(f, 2)
        grads = [wgrad_units(a, b, a.shape[1] // 8, core, name) for a, b, name in pairs]
        order = (5, 4, 3, 2, 1, 0)
        out, small = reduce_units([grads[i] for i in order], small)
        summed = [None] * 6
        first = 0
        for i in order:
            n_row = pairs[i][0].shape[1] // 8 // 128
            n_col = pairs[i][1].shape[1] // 1024
            part = out[first : first + n_row * n_col].reshape(n_row, n_col, 128, 1024)
            summed[i] = part.transpose(0, 2, 1, 3).reshape(n_row * 128, n_col * 1024)
            first += n_row * n_col
        n_act = embed.shape[0]
        d_embed, vecs = small[:n_act], small[n_act:]
        dg1, ds1, dg2, ds2, dg3, ds3, d_bout = (vecs[i] for i in range(7))
        d_bin = vecs[7 : 7 + d_bin.shape[1] // width].reshape(-1)
    else:
        summed = []
        for a, b, _ in pairs:
            part = lax.dot_general(a, b, (((0,), (0,)), ((), ())), preferred_element_type=F32)
            part = lax.psum_scatter(part, "frame", scatter_dimension=0, tiled=True)
            summed.append(lax.psum(part.astype(BF16), "tile").astype(F32))
        d_embed, dg1, ds1, dg2, ds2, dg3, ds3, d_bin, d_bout = lax.psum(
            (d_embed, dg1[0], ds1[0], dg2[0], ds2[0], dg3[0], ds3[0], d_bin[0], d_bout[0]), ("frame", "tile"))

    return (result, tokens_grad, d_embed, dg1, ds1, summed[0], summed[1], dg2, ds2, summed[2], summed[3],
            dg3, ds3, summed[4], d_bin, summed[5], d_bout)


def solution(mesh):
    shard = P("frame", "tile", None)
    mat = P("frame", None)
    rep = P()
    in_specs = (shard, shard, P("frame"), rep, rep, rep, rep, rep, mat, mat, rep, rep, mat, mat,
                rep, rep, mat, rep, mat, rep)
    out_specs = (shard, shard, rep, rep, rep, mat, mat, rep, rep, mat, mat, rep, rep, mat, rep, mat, rep)
    on_boxes = mesh.shape["frame"] == 8 and mesh.shape["tile"] == 4
    return jax.shard_map(
        functools.partial(per_device, on_boxes),
        mesh=mesh, in_specs=in_specs, out_specs=out_specs, check_vma=False)
```

time: 1550 us -> 631 us (0.41)
  waiting for transfers between devices: 1030 us -> 0.17 us
  Pallas kernels: 0 us -> 535 us
  matrix products: 160 us -> 0 us
  local copies, waits for them, and re-layouts: 198 us -> 79.3 us
  starting transfers between devices: 85.1 us -> 3.23 us
  other arithmetic: 46.9 us -> 3.17 us
    reduce_scatter x8 -> x0, waiting for transfers between devices: 574 us -> none  [the longest x1 117 us: per_device(): lax.psum_scatter(mat_grads[4], 'frame', scatter_dimension=0, tiled=True)]
    pallas_call x0 -> x20, Pallas kernels: none -> 535 us  [the longest x1 180 us: reduce_units(): pl.pallas_call(functools.partial(reduce_kernel, units, len(grads)), out_s...]
    psum x2 -> x0, waiting for transfers between devices: 262 us -> none  [the longest x1 141 us: per_device(): lax.psum(reduced[0].astype(jnp.bfloat16), 'tile').astype(jnp.float32)]
    all_gather x8 -> x0, waiting for transfers between devices: 190 us -> none  [the longest x1 45.6 us: fetch_weights(): lax.all_gather(pieces[0], 'frame', axis=0, tiled=True)]
    dot_general x32 -> x0, matrix products: 160 us -> none  [the longest x6 42.2 us: left_grad(): jnp.einsum('nd,ne->de', inputs, grads, preferred_element_type=jnp.float32)]
    concatenate x22 -> x1, local copies, waits for them, and re-layouts: 94.8 us -> 0.17 us  [per_device(): jnp.concatenate([d_embed, dg1, ds1, dg2, ds2, dg3, ds3, d_bout, d_bin.res...]
    ppermute x16 -> x12, starting transfers between devices: 83.9 us -> 3.23 us  [the longest x6 1.63 us: wgrad_units(): right2 = lax.ppermute(right, 'frame', swap)]
    dynamic_slice x1 -> x7, local copies, waits for them, and re-layouts: 0.08 us -> 34.8 us  [the longest x5 33 us: wgrad_units(): lax.dynamic_index_in_dim(parts, 1 - core, 2, False).reshape(tok, 4 * shard)]
  transfers between devices with their start and end apart: 34 -> 12, of which waited for: 15 -> 1; matrix products, arithmetic and copies ran while one was open for 20% -> 9% of each run, Pallas kernels for 0% -> 17%
where the time goes in v1:
time: 631 us; the launch traced here: 625 us
  Pallas kernels  535 us (85%)
  local copies, waits for them, and re-layouts  79.3 us (13%)
    pallas_call x1, Pallas kernels, reduce_units(): pl.pallas_call(functools.partial(reduce_kernel, units, len(grads)), out_s...  180 us
    pallas_call x1, Pallas kernels, gather_weights(): pl.pallas_call(functools.partial(gather_kernel, n, chunks), out_shape=[ja...  132 us
    pallas_call x6, Pallas kernels, swap_blocks(): pl.pallas_call(functools.partial(swap_kernel, axes, src_of, dst_of), out_...  83.7 us
    pallas_call x2, Pallas kernels, attn_bwd(): pl.pallas_call(functools.partial(attn_bwd_kernel, bias is not None), out_...  36.9 us
    pallas_call x6, Pallas kernels, wgrad_units(): pl.pallas_call(functools.partial(wgrad_kernel, shard), out_shape=jax.Shap...  36.2 us
    dynamic_slice x5, local copies, waits for them, and re-layouts, wgrad_units(): lax.dynamic_index_in_dim(parts, 1 - core, 2, False).reshape(tok, 4 * shard)  33 us
    pallas_call x2, Pallas kernels, attn_fwd(): pl.pallas_call(functools.partial(attn_fwd_kernel, bias is not None), out_...  29.1 us
    unnamed x77, local copies, waits for them, and re-layouts  21.5 us
  transfers between devices with their start and end apart: 12, of which 1 were waited for; matrix products, arithmetic and copies ran while one was open for 9% of the time, Pallas kernels for 17%

profile of v1, /device:TPU:0, one launch (start us, length us, event | category | flops | bytes accessed | tf_op | source)
XLA Modules:
  0.0 624.6 jit_solution(13109265565250564658)
XLA Ops:
  0.7 1.3 dynamic_slice.45
  3.2 16.0 %tokens_to_frames.1 = bf16[4,64,1024]{2,1,0:T(8,128)(2,1)} custom-call(bf16[4,64,1024]{2,1,0:T(8,128)(2,1)} %src_ref.1), custom_call_target="tpu_custom_call" | custom-call | tf_op jit(solution)/shard_map/tokens_to_frames/pallas_call | solution.py:428
  20.5 132.3 %gather_weights.1 = (bf16[1024,3072]{1,0:T(8,128)(2,1)}, bf16[1024,1024]{1,0:T(8,128)(2,1)}, bf16[1024,3072]{1,0:T(8,128)(2,1)}, bf16[1024,1024]{1,0:T(8,128)(2,...) custom-call(bf16[128,3072]{1,0:T(8,128)(2,1)} %refs_0_.1, bf16[128,1024]{1,0:T(8,128)(2,1)} %refs_1_.1, ...), custom_call_target="tpu_custom_call" | custom-call | tf_op jit(solution)/shard_map/gather_weights/pallas_call | solution.py:516
  152.7 14.4 %spatial_forward.1 = (bf16[256,1024]{1,0:T(8,128)(2,1)}, bf16[256,3072]{1,0:T(8,128)(2,1)}, bf16[256,1024]{1,0:T(8,128)(2,1)}, bf16[256,1024]{1,0:T(8,128)(2,1)}) custom-call(bf16[256,1024]{1,0:T(8,128)(2,1)} %bitcast.101, f32[1,1024]{1,0:T(1,128)} %constant_dynamic-slice_fusion.added_ref, f32[1,1024]{1,0:T(1,128)} %bitcast.133, f32[1,1024]{1,0:T(1,128)} %bitcast.140, ...), custom_call_target="tpu_custom_call" | custom-call | tf_op jit(solution)/shard_map/spatial_forward/pallas_call | solution.py:191
  167.2 17.5 %frames_to_places.1 = bf16[32,8,1024]{2,1,0:T(8,128)(2,1)} custom-call(bf16[32,8,1024]{2,1,0:T(8,128)(2,1)} %bitcast.130), custom_call_target="tpu_custom_call" | custom-call | tf_op jit(solution)/shard_map/frames_to_places/pallas_call | solution.py:428
  185.0 9.6 %grad_to_places.1 = bf16[8,4,8,1024]{3,2,1,0:T(8,128)(2,1)} custom-call(bf16[4,8,8,1024]{3,2,1,0:T(8,128)(2,1)} %bitcast.127), custom_call_target="tpu_custom_call" | custom-call | tf_op jit(solution)/shard_map/grad_to_places/pallas_call | solution.py:428
  194.7 0.9 and_select_fusion.rest_0_
  196.2 14.6 %temporal_forward.1 = (bf16[256,1024]{1,0:T(8,128)(2,1)}, bf16[256,3072]{1,0:T(8,128)(2,1)}, bf16[256,1024]{1,0:T(8,128)(2,1)}, f32[256,1024]{1,0:T(8,128)}) custom-call(bf16[256,1024]{1,0:T(8,128)(2,1)} %bitcast.103, f32[1,1024]{1,0:T(1,128)} %broadcast_in_dim.54.added_ref, f32[1,1024]{1,0:T(1,128)} %bitcast.131, f32[1,1024]{1,0:T(1,128)} %bitcast.139, ...), custom_call_target="tpu_custom_call" | custom-call | tf_op jit(solution)/shard_map/temporal_forward/pallas_call | solution.py:191
  210.8 17.4 %ffn_forward.1 = (bf16[256,1024]{1,0:T(8,128)(2,1)}, f32[256,4096]{1,0:T(8,128)}, bf16[256,4096]{1,0:T(8,128)(2,1)}, bf16[256,1024]{1,0:T(8,128)(2,1)}) custom-call(f32[256,1024]{1,0:T(8,128)} %get-tuple-element.58.after_ref, f32[1,1024]{1,0:T(1,128)} %bitcast.137, f32[1,1024]{1,0:T(1,128)} %bitcast.148, bf16[1024,4096]{1,0:T(8,128)(2,1)} %get-tuple-element.59.win_ref, ...), custom_call_target="tpu_custom_call" | custom-call | tf_op jit(solution)/shard_map/ffn_forward/pallas_call | solution.py:284
  228.2 20.2 %ffn_backward.1 = (bf16[256,4096]{1,0:T(8,128)(2,1)}, f32[256,1024]{1,0:T(8,128)}, f32[1,1024]{1,0:T(1,128)}, f32[1,1024]{1,0:T(1,128)}, f32[1,4096]{1,0:T(1,128)}, /*index=5*/f32[1,1024]{1,0:T(1,128)}) custom-call(bf16[256,1024]{1,0:T(8,128)(2,1)} %bitcast.98, f32[256,4096]{1,0:T(8,128)} %get-tuple-element.62.pre_ref, ...), custom_call_target="tpu_custom_call" | custom-call | tf_op jit(solution)/shard_map/ffn_backward/pallas_call | solution.py:329
  249.5 7.3 %dynamic-slice_reduce_fusion.2 = (bf16[256,4,128]{2,1,0:T(4,128)(2,1)S(1)}, bf16[256,4,128]{2,1,0:T(4,128)(2,1)}, bf16[256,4,128]{2,1,0:T(4,128)(2,1)S(1)}, bf16[256,4,128]{2,1,0:T(4,128)(2,1)S(1)}) fusion(bf16[256,4,2,128]{3,2,1,0:T(2,128)(2,1)S(1)} %reshape.240, s32[]{:T(128)S(6)} %select_n.65, s32[]{:T(128)S(6)} %select_n.64, ...), kind=kLoop, calls=%fused_computation.7 | loop fusion | bytes 2097160 | tf_op jit(solution)/shard_map/jit(dynamic_index_in_dim)/dynamic_slice | solution.py:368
  258.8 18.4 %temporal_backward.1 = (bf16[256,1024]{1,0:T(8,128)(2,1)}, bf16[256,3072]{1,0:T(8,128)(2,1)}, bf16[256,1024]{1,0:T(8,128)(2,1)}, f32[1,1024]{1,0:T(1,128)}, f32[1,1024]{1,0:T(1,128)}) custom-call(bf16[256,1024]{1,0:T(8,128)(2,1)} %bitcast.104, f32[1,1024]{1,0:T(1,128)} %broadcast_in_dim.54.added_ref, f32[1,1024]{1,0:T(1,128)} %bitcast.132, ...), custom_call_target="tpu_custom_call" | custom-call | tf_op jit(solution)/shard_map/temporal_backward/pallas_call | solution.py:244
  277.2 17.4 %places_to_frames.1 = bf16[32,8,1024]{2,1,0:T(8,128)(2,1)} custom-call(bf16[32,8,1024]{2,1,0:T(8,128)(2,1)} %bitcast.129), custom_call_target="tpu_custom_call" | custom-call | tf_op jit(solution)/shard_map/places_to_frames/pallas_call | solution.py:428
  294.6 18.5 %spatial_backward.1 = (bf16[256,1024]{1,0:T(8,128)(2,1)}, bf16[256,3072]{1,0:T(8,128)(2,1)}, f32[256,1024]{1,0:T(8,128)}, f32[1,1024]{1,0:T(1,128)}, f32[1,1024]{1,0:T(1,128)}) custom-call(bf16[256,1024]{1,0:T(8,128)(2,1)} %bitcast.102, f32[1,1024]{1,0:T(1,128)} %constant_dynamic-slice_fusion.added_ref, f32[1,1024]{1,0:T(1,128)} %bitcast.134, ...), custom_call_target="tpu_custom_call" | custom-call | tf_op jit(solution)/shard_map/spatial_backward/pallas_call | solution.py:244
  314.0 4.0 dynamic-slice_reduce_fusion.8
  318.8 3.3 reshape.225
  322.7 13.6 %dynamic-slice_reduce_fusion = (bf16[256,4,512]{2,1,0:T(4,128)(2,1)S(1)}, bf16[256,4,512]{2,1,0:T(4,128)(2,1)S(1)}) fusion(bf16[256,4,2,512]{3,2,1,0:T(2,128)(2,1)S(1)} %reshape.225, s32[]{:T(128)S(6)} %select_n.65, s32[]{:T(128)S(6)} %select_n.64), kind=kLoop, calls=%fused_computation.1 | loop fusion | bytes 4194312 | tf_op jit(solution)/shard_map/jit(dynamic_index_in_dim)/dynamic_slice | solution.py:368
  336.6 1.2 copy.80
  339.1 1.4 reshape.234
  340.5 4.0 dynamic-slice_reduce_fusion.6
  345.2 1.4 reshape.228
  346.8 4.0 dynamic-slice_reduce_fusion.10
  351.5 0.9 fusion.2
  355.8 0.8 copy.104
  357.3 1.7 copy.108
  358.9 0.7 copy.110
  359.7 1.7 copy.112
  361.4 1.2 copy.79
  362.6 13.5 %tokens_grad_to_tiles.1 = bf16[4,64,1024]{2,1,0:T(8,128)(2,1)} custom-call(bf16[4,64,1024]{2,1,0:T(8,128)(2,1)} %bitcast.108), custom_call_target="tpu_custom_call" | custom-call | tf_op jit(solution)/shard_map/tokens_grad_to_tiles/pallas_call | solution.py:428
  376.2 9.6 %result_to_tiles.1 = bf16[4,8,8,1024]{3,2,1,0:T(8,128)(2,1)} custom-call(bf16[8,4,8,1024]{3,2,1,0:T(8,128)(2,1)} %bitcast.128), custom_call_target="tpu_custom_call" | custom-call | tf_op jit(solution)/shard_map/result_to_tiles/pallas_call | solution.py:428
  385.8 3.4 spatial_out_grad.1.refs_4_
  389.2 3.5 temporal_out_grad.1.refs_2_
  392.7 8.2 %ffn_out_grad.1.refs_0_ = bf16[4,4,128,1024]{3,2,1,0:T(8,128)(2,1)} custom-call(bf16[256,2048]{1,0:T(8,128)(2,1)} %bitcast.105, bf16[256,2048]{1,0:T(8,128)(2,1)} %copy-done.7, bf16[256,1024]{1,0:T(8,128)(2,1)} %bitcast.99, bf16[256,1024]{1,0:T(8,128)(2,1)} %collective-permute-done.1.right2_ref), custom_call_target="tpu_custom_call" | custom-call | tf_op jit(solution)/shard_map/ffn_out_grad/pallas_call | solution.py:373
  400.8 6.5 %spatial_qkv_grad.1.refs_5_ = bf16[3,4,128,1024]{3,2,1,0:T(8,128)(2,1)} custom-call(bf16[256,512]{1,0:T(8,128)(2,1)} %bitcast.126, bf16[256,512]{1,0:T(8,128)(2,1)} %collective-permute-done.10.left2_ref, bf16[256,3072]{1,0:T(8,128)(2,1)} %get-tuple-element.78.right_ref, bf16[256,3072]{1,0:T(8,128)(2,1)} %collective-permute-done.11.right2_ref), custom_call_target="tpu_custom_call" | custom-call | tf_op jit(solution)/shard_map/spatial_qkv_grad/pallas_call | solution.py:373
  407.4 6.6 %temporal_qkv_grad.1.refs_3_ = bf16[3,4,128,1024]{3,2,1,0:T(8,128)(2,1)} custom-call(bf16[256,512]{1,0:T(8,128)(2,1)} %bitcast.125, bf16[256,512]{1,0:T(8,128)(2,1)} %collective-permute-done.6.left2_ref, bf16[256,3072]{1,0:T(8,128)(2,1)} %get-tuple-element.74.right_ref, bf16[256,3072]{1,0:T(8,128)(2,1)} %collective-permute-done.7.right2_ref), custom_call_target="tpu_custom_call" | custom-call | tf_op jit(solution)/shard_map/temporal_qkv_grad/pallas_call | solution.py:373
  414.7 8.0 %ffn_in_grad.1.refs_1_ = bf16[4,4,128,1024]{3,2,1,0:T(8,128)(2,1)} custom-call(bf16[256,512]{1,0:T(8,128)(2,1)} %bitcast.114, bf16[256,512]{1,0:T(8,128)(2,1)} %copy-done.17, bf16[256,4096]{1,0:T(8,128)(2,1)} %get-tuple-element.70.right_ref, bf16[256,4096]{1,0:T(8,128)(2,1)} %collective-permute-done.3.right2_ref), custom_call_target="tpu_custom_call" | custom-call | tf_op jit(solution)/shard_map/ffn_in_grad/pallas_call | solution.py:373
  422.7 179.5 %reduce_gradients.1 = (f32[16,128,1024]{2,1,0:T(8,128)}, f32[24,1024]{1,0:T(8,128)}) custom-call(bf16[4,4,128,1024]{3,2,1,0:T(8,128)(2,1)} %ffn_out_grad.1.refs_0_, bf16[4,4,128,1024]{3,2,1,0:T(8,128)(2,1)} %ffn_in_grad.1.refs_1_, bf16[1,4,128,1024]{3,2,1,0:T(8,128)(2,1)} %temporal_out_grad.1.refs_2_, bf16[3,4,128,1024]{3,2,1,0:T(8,128)(2,1)} %temporal_qkv_grad.1.refs_3_, ...), custom_call_target="tpu_custom_call" | custom-call | tf_op jit(solution)/shard_map/reduce_gradients/pallas_call | solution.py:700
  602.3 5.1 fusion.1
  607.4 1.1 copy-done.2
  608.4 1.9 slice_bitcast_fusion.1
  610.3 1.0 slice_bitcast_fusion.3
  612.6 1.9 copy.63
  614.5 1.8 copy.66
  616.3 1.9 copy.61
  618.2 1.6 copy.64
  620.3 1.6 copy.65
  622.6 0.8 copy.116
  623.4 0.8 copy.117
  (110 shorter events, 16.9 us)
Async XLA Ops:
  0.7 19.2 %copy-start = (f32[8,1024]{1,0:T(8,128)S(1)}, f32[8,1024]{1,0:T(8,128)}, u32[]{:S(2)}) copy-start(f32[8,1024]{1,0:T(8,128)} %param.25) | copy-start | bytes 98308
  152.7 32.0 %copy-start.27 = (s32[32]{0:T(128)S(1)}, s32[32]{0:T(128)}, u32[]{:S(2)}) copy-start(s32[32]{0:T(128)} %param.23) | copy-start | bytes 388
  152.7 32.1 %copy-start.28 = (s32[32]{0:T(128)S(1)}, s32[32]{0:T(128)}, u32[]{:S(2)}) copy-start(s32[32]{0:T(128)} %param.24) | copy-start | bytes 388
  228.2 20.5 %copy-start.15 = (bf16[256,1024]{1,0:T(8,128)(2,1)S(1)}, bf16[256,1024]{1,0:T(8,128)(2,1)}, u32[]{:S(2)}) copy-start(bf16[256,1024]{1,0:T(8,128)(2,1)} %get-tuple-element.75) | copy-start | bytes 1572868
  228.2 20.9 %copy-start.14 = (bf16[256,1024]{1,0:T(8,128)(2,1)S(1)}, bf16[256,1024]{1,0:T(8,128)(2,1)}, u32[]{:S(2)}) copy-start(bf16[256,1024]{1,0:T(8,128)(2,1)} %get-tuple-element.77) | copy-start | bytes 1572868
  248.4 165.6 %collective-permute-start.3 = (bf16[256,4096]{1,0:T(8,128)(2,1)}, bf16[256,4096]{1,0:T(8,128)(2,1)}, u32[]{:S(2)}, u32[]{:S(2)}) collective-permute-start(bf16[256,4096]{1,0:T(8,128)(2,1)} %get-tuple-element.70.right_ref), channel_id=1, source_target_pairs={{0,4},{4,0},{8,12},{12,8},{16,20},{20,16},{24,28},{28,24},{1,5},{5... | collective-permute-start | bytes 6291464 | tf_op jit(solution)/shard_map/ppermute | solution.py:371
  257.6 64.6 %collective-permute-start.10 = (bf16[256,512]{1,0:T(8,128)(2,1)}, bf16[256,512]{1,0:T(8,128)(2,1)}, u32[]{:S(2)}, u32[]{:S(2)}) collective-permute-start(bf16[256,512]{1,0:T(8,128)(2,1)} %bitcast.84), channel_id=1, source_target_pairs={{0,4},{4,0},{8,12},{12,8},{16,20},{20,16},{24,28},{28,24},{1,5},{5... | collective-permute-start | bytes 786440 | tf_op jit(solution)/shard_map/ppermute | solution.py:370
  258.5 63.9 %collective-permute-start.8 = (bf16[256,512]{1,0:T(8,128)(2,1)}, bf16[256,512]{1,0:T(8,128)(2,1)}, u32[]{:S(2)}, u32[]{:S(2)}) collective-permute-start(bf16[256,512]{1,0:T(8,128)(2,1)} %bitcast.86), channel_id=1, source_target_pairs={{0,4},{4,0},{8,12},{12,8},{16,20},{20,16},{24,28},{28,24},{1,5},{5... | collective-permute-start | bytes 786440 | tf_op jit(solution)/shard_map/ppermute | solution.py:370
  294.6 19.1 %copy-start.13 = (bf16[256,1024]{1,0:T(8,128)(2,1)S(1)}, bf16[256,1024]{1,0:T(8,128)(2,1)}, u32[]{:S(2)}) copy-start(bf16[256,1024]{1,0:T(8,128)(2,1)} %get-tuple-element.71) | copy-start | bytes 1572868
  313.1 24.7 %collective-permute-start.9 = (bf16[256,1024]{1,0:T(8,128)(2,1)}, bf16[256,1024]{1,0:T(8,128)(2,1)}, u32[]{:S(2)}, u32[]{:S(2)}) collective-permute-start(bf16[256,1024]{1,0:T(8,128)(2,1)} %get-tuple-element.76.right_ref), channel_id=1, source_target_pairs={{0,4},{4,0},{8,12},{12,8},{16,20},{20,16},{24,28},{28,24},{1,5},{5... | collective-permute-start | bytes 1572872 | tf_op jit(solution)/shard_map/ppermute | solution.py:371
  313.4 87.5 %collective-permute-start.11 = (bf16[256,3072]{1,0:T(8,128)(2,1)}, bf16[256,3072]{1,0:T(8,128)(2,1)}, u32[]{:S(2)}, u32[]{:S(2)}) collective-permute-start(bf16[256,3072]{1,0:T(8,128)(2,1)} %get-tuple-element.78.right_ref), channel_id=1, source_target_pairs={{0,4},{4,0},{8,12},{12,8},{16,20},{20,16},{24,28},{28,24},{1,5},{5... | collective-permute-start | bytes 4718600 | tf_op jit(solution)/shard_map/ppermute | solution.py:371
  322.1 85.3 %collective-permute-start.7 = (bf16[256,3072]{1,0:T(8,128)(2,1)}, bf16[256,3072]{1,0:T(8,128)(2,1)}, u32[]{:S(2)}, u32[]{:S(2)}) collective-permute-start(bf16[256,3072]{1,0:T(8,128)(2,1)} %get-tuple-element.74.right_ref), channel_id=1, source_target_pairs={{0,4},{4,0},{8,12},{12,8},{16,20},{20,16},{24,28},{28,24},{1,5},{5... | collective-permute-start | bytes 4718600 | tf_op jit(solution)/shard_map/ppermute | solution.py:371
  322.4 13.9 %copy-start.11 = (bf16[256,1024]{1,0:T(8,128)(2,1)S(1)}, bf16[256,1024]{1,0:T(8,128)(2,1)}, u32[]{:S(2)}) copy-start(bf16[256,1024]{1,0:T(8,128)(2,1)} %get-tuple-element.72.right_ref) | copy-start | bytes 1572868
  322.4 13.9 %collective-permute-start.4 = (bf16[256,512]{1,0:T(8,128)(2,1)}, bf16[256,512]{1,0:T(8,128)(2,1)S(1)}, u32[]{:S(2)}, u32[]{:S(2)}) collective-permute-start(bf16[256,512]{1,0:T(8,128)(2,1)} %bitcast.90), channel_id=1, source_target_pairs={{0,4},{4,0},{8,12},{12,8},{16,20},{20,16},{24,28},{28,24},{1,5},{5... | collective-permute-start | bytes 786440 | tf_op jit(solution)/shard_map/ppermute | solution.py:370
  336.3 2.0 copy-start.4
  336.3 2.2 copy-start.16
  336.3 2.0 collective-permute-start.5
  337.9 14.8 %collective-permute-start = (bf16[256,2048]{1,0:T(8,128)(2,1)}, bf16[256,2048]{1,0:T(8,128)(2,1)S(1)}, u32[]{:S(2)}, u32[]{:S(2)}) collective-permute-start(bf16[256,2048]{1,0:T(8,128)(2,1)} %bitcast.44), channel_id=1, source_target_pairs={{0,4},{4,0},{8,12},{12,8},{16,20},{20,16},{24,28},{28,24},{1,5},{5... | collective-permute-start | bytes 3145736 | tf_op jit(solution)/shard_map/ppermute | solution.py:370
  338.3 0.8 copy-start.12
  338.3 14.1 %collective-permute-start.1 = (bf16[256,1024]{1,0:T(8,128)(2,1)S(1)}, bf16[256,1024]{1,0:T(8,128)(2,1)}, u32[]{:S(2)}, u32[]{:S(2)}) collective-permute-start(bf16[256,1024]{1,0:T(8,128)(2,1)S(1)} %bitcast.100), channel_id=1, source_target_pairs={{0,4},{4,0},{8,12},{12,8},{16,20},{20,16},{24,28},{28,24},{1,5},{5... | collective-permute-start | bytes 1572872 | tf_op jit(solution)/shard_map/ppermute | solution.py:371
  346.7 4.9 copy-start.9
  346.7 7.4 %copy-start.19 = (f32[1,4096]{1,0:T(1,128)S(1)}, f32[1,4096]{1,0:T(1,128)}, u32[]{:S(2)}) copy-start(f32[1,4096]{1,0:T(1,128)} %get-tuple-element.86) | copy-start | bytes 49156
  346.7 8.2 %copy-start.20 = (f32[1,1024]{1,0:T(1,128)S(1)}, f32[1,1024]{1,0:T(1,128)}, u32[]{:S(2)}) copy-start(f32[1,1024]{1,0:T(1,128)} %get-tuple-element.83) | copy-start | bytes 12292
  346.7 8.2 %copy-start.21 = (f32[1,1024]{1,0:T(1,128)S(1)}, f32[1,1024]{1,0:T(1,128)}, u32[]{:S(2)}) copy-start(f32[1,1024]{1,0:T(1,128)} %get-tuple-element.84) | copy-start | bytes 12292
  346.7 8.2 %copy-start.22 = (f32[1,1024]{1,0:T(1,128)S(1)}, f32[1,1024]{1,0:T(1,128)}, u32[]{:S(2)}) copy-start(f32[1,1024]{1,0:T(1,128)} %get-tuple-element.85) | copy-start | bytes 12292
  346.7 8.2 %copy-start.23 = (f32[1,1024]{1,0:T(1,128)S(1)}, f32[1,1024]{1,0:T(1,128)}, u32[]{:S(2)}) copy-start(f32[1,1024]{1,0:T(1,128)} %get-tuple-element.81) | copy-start | bytes 12292
  346.7 8.2 %copy-start.24 = (f32[1,1024]{1,0:T(1,128)S(1)}, f32[1,1024]{1,0:T(1,128)}, u32[]{:S(2)}) copy-start(f32[1,1024]{1,0:T(1,128)} %get-tuple-element.82) | copy-start | bytes 12292
  346.7 8.2 %copy-start.25 = (f32[1,1024]{1,0:T(1,128)S(1)}, f32[1,1024]{1,0:T(1,128)}, u32[]{:S(2)}) copy-start(f32[1,1024]{1,0:T(1,128)} %get-tuple-element.79) | copy-start | bytes 12292
  346.7 8.2 %copy-start.26 = (f32[1,1024]{1,0:T(1,128)S(1)}, f32[1,1024]{1,0:T(1,128)}, u32[]{:S(2)}) copy-start(f32[1,1024]{1,0:T(1,128)} %get-tuple-element.80) | copy-start | bytes 12292
  350.8 5.0 copy-start.8
  350.8 8.2 %copy-start.10 = (bf16[256,4,128]{2,1,0:T(4,128)(2,1)S(1)}, bf16[256,4,128]{2,1,0:T(4,128)(2,1)}, u32[]{:S(2)}) copy-start(bf16[256,4,128]{2,1,0:T(4,128)(2,1)} %get-tuple-element.115) | copy-start | bytes 786436
  352.4 55.0 %collective-permute-start.6 = (bf16[256,512]{1,0:T(8,128)(2,1)}, bf16[256,512]{1,0:T(8,128)(2,1)}, u32[]{:S(2)}, u32[]{:S(2)}) collective-permute-start(bf16[256,512]{1,0:T(8,128)(2,1)} %bitcast.88), channel_id=1, source_target_pairs={{0,4},{4,0},{8,12},{12,8},{16,20},{20,16},{24,28},{28,24},{1,5},{5... | collective-permute-start | bytes 786440 | tf_op jit(solution)/shard_map/ppermute | solution.py:370
  352.6 10.0 %copy-start.7 = (bf16[256,2048]{1,0:T(8,128)(2,1)}, bf16[256,2048]{1,0:T(8,128)(2,1)S(1)}, u32[]{:S(2)}) copy-start(bf16[256,2048]{1,0:T(8,128)(2,1)S(1)} %collective-permute-done.left2_ref) | copy-start | bytes 3145732
  352.6 61.3 %collective-permute-start.2 = (bf16[256,512]{1,0:T(8,128)(2,1)}, bf16[256,512]{1,0:T(8,128)(2,1)S(1)}, u32[]{:S(2)}, u32[]{:S(2)}) collective-permute-start(bf16[256,512]{1,0:T(8,128)(2,1)} %bitcast.92), channel_id=1, source_target_pairs={{0,4},{4,0},{8,12},{12,8},{16,20},{20,16},{24,28},{28,24},{1,5},{5... | collective-permute-start | bytes 786440 | tf_op jit(solution)/shard_map/ppermute | solution.py:370
  414.0 0.7 copy-start.17
  602.3 6.2 copy-start.2
  610.3 1.0 copy-start.18
  618.2 1.6 copy-start.3
  620.3 2.3 copy-start.6
  620.3 3.8 copy-start.1
  620.3 3.0 copy-start.5

commit v2 on v1

--- a/solution.py
+++ b/solution.py
@@ -260,50 +260,11 @@
 GELU_B = 0.044715
 
 
-def ffn_fwd_kernel(after_ref, gain_ref, shift_ref, win_ref, bin_ref, wout_ref, bout_ref,
-                   unit_ref, pre_ref, act_ref, res_ref):
-    norm_rows(lambda rows: after_ref[rows, :], gain_ref, shift_ref, unit_ref)
-
-    def put_pre(cols, y):
-        v = y + bin_ref[:, cols]
-        pre_ref[:, cols] = v
-        act = 0.5 * v * (1.0 + jnp.tanh(GELU_A * (v + GELU_B * v * v * v)))
-        act_ref[:, cols] = act.astype(BF16)
-
-    matmul(unit_ref, win_ref, 512, put_pre)
-
-    def put_res(cols, y):
-        res_ref[:, cols] = (after_ref[:, cols] + y + bout_ref[:, cols]).astype(BF16)
-
-    matmul(act_ref, wout_ref, 256, put_res)
-
-
-def ffn_fwd(after, gain, shift, win, b_in, wout, b_out):
-    rows, width = after.shape
-    ff = win.shape[1]
-    return pl.pallas_call(
-        ffn_fwd_kernel,
-        out_shape=[
-            jax.ShapeDtypeStruct((rows, width), BF16),
-            jax.ShapeDtypeStruct((rows, ff), F32),
-            jax.ShapeDtypeStruct((rows, ff), BF16),
-            jax.ShapeDtypeStruct((rows, width), BF16),
-        ],
-        in_specs=[VMEM_SPEC] * 7,
-        out_specs=[VMEM_SPEC] * 4,
-        compiler_params=params(),
-        name="ffn_forward",
-    )(after, gain, shift, win, b_in, wout, b_out)
-
-
-def ffn_bwd_kernel(g_ref, pre_ref, after_ref, gain_ref, win_ref, wout_ref,
-                   dpre_ref, dafter_ref, dgain_ref, dshift_ref, dbin_ref, dbout_ref, du_ref, acc_ref):
+def ffn_bwd_kernel(g_ref, slope_ref, after_ref, gain_ref, win_ref, wout_ref,
+                   dslope_ref, dafter_ref, dgain_ref, dshift_ref, dbin_ref, dbout_ref, du_ref, acc_ref):
     def put_dpre(rows, y):
-        v = pre_ref[:, rows]
-        t = jnp.tanh(GELU_A * (v + GELU_B * v * v * v))
-        slope = 0.5 * (1.0 + t) + 0.5 * v * (1.0 - t * t) * GELU_A * (1.0 + 3.0 * GELU_B * v * v)
-        d = (y * slope).astype(BF16)
-        dpre_ref[:, rows] = d
+        d = (y * slope_ref[:, rows].astype(F32)).astype(BF16)
+        dslope_ref[:, rows] = d
         dbin_ref[:, rows] = jnp.sum(d.astype(F32), 0, keepdims=True)
 
     matmul_nt(g_ref, wout_ref, 512, put_dpre)
@@ -311,7 +272,7 @@
     def put_du(rows, y):
         du_ref[:, rows] = y
 
-    matmul_nt(dpre_ref, win_ref, 256, put_du)
+    matmul_nt(dslope_ref, win_ref, 256, put_du)
     dbout_ref[...] = jnp.zeros_like(dbout_ref)
 
     def store(rows, dh):
@@ -322,7 +283,7 @@
     norm_back(lambda rows: after_ref[rows, :], du_ref, gain_ref, dgain_ref, dshift_ref, acc_ref, store)
 
 
-def ffn_bwd(g, pre, after, gain, win, wout):
+def ffn_bwd(g, slope, after, gain, win, wout):
     rows, width = after.shape
     ff = win.shape[1]
     row = lambda n: jax.ShapeDtypeStruct((1, n), F32)
@@ -338,7 +299,7 @@
         scratch_shapes=[pltpu.VMEM((rows, width), F32), pltpu.VMEM((2, 8, width), F32)],
         compiler_params=params(),
         name="ffn_backward",
-    )(g, pre, after, gain, win, wout)
+    )(g, slope, after, gain, win, wout)
 
 
 def wgrad_kernel(shard, left_ref, left2_ref, right_ref, right2_ref, out_ref, lt_ref):
@@ -381,6 +342,28 @@
     )(mine, other, right, right2)
 
 
+def wgrad(core, shard, left, left_x, right, right_x, out, lt):
+    tok = left.shape[0]
+    col_blocks = right.shape[1] // TILE
+    for rb in range(shard // 128):
+        for q in range(4):
+            cols = pl.ds(pl.multiple_of((2 * q + core) * shard + rb * 128, 128), 128)
+            lt[q * 128 : (q + 1) * 128, :tok] = left[:, cols].T
+            cols = pl.ds(q * shard + rb * 128, 128)
+            lt[q * 128 : (q + 1) * 128, tok:] = left_x[:, cols].T
+
+        def step(j, rb=rb):
+            cols = at(j, 512)
+            y = dot(lt[:, :tok], right[:, cols]) + dot(lt[:, tok:], right_x[:, cols])
+            y = y.astype(BF16)
+            unit = rb * col_blocks + j // 2
+            half = pl.ds(pl.multiple_of(lax.rem(j, 2) * 512, 512), 512)
+            for q in range(4):
+                out[unit, q, :, half] = y[q * 128 : (q + 1) * 128]
+
+        each(2 * col_blocks, step)
+
+
 def xor(a, b):
     bit = lax.rem(a // b, 2)
     return a + b - 2 * b * bit
@@ -440,39 +423,56 @@
     )(x)
 
 
+TILE = 1024
+SLOTS = 6
+AHEAD = 3
+
+
 def gather_chunks(shapes):
     out = []
     for i, (rows, cols) in enumerate(shapes):
         step = rows
-        while step * cols > 200 * 1024 and step % 32 == 0:
+        while step * cols > 128 * 1024 and step % 32 == 0:
             step //= 2
         out += [(i, r, step) for r in range(0, rows, step)]
     return out
 
 
-def gather_kernel(n_arr, chunks, *refs):
-    ins = refs[:n_arr]
-    outs = refs[n_arr : 2 * n_arr]
-    ssem, rsem, lsem = refs[2 * n_arr :]
+def weight_tiles(shapes):
+    return [
+        (i, r, c)
+        for i, (rows, cols) in enumerate(shapes)
+        for r in range(0, rows, TILE)
+        for c in range(0, cols, TILE)
+    ]
+
+
+def forward_kernel(chunks, tiles, *refs):
+    shards = refs[:6]
+    (tokens, grad4, added, g1, s1, g2, s2, g3, s3, b_in, b_out, bias) = refs[6:18]
+    full = refs[18:24]
+    (base1, unit1, qkv1, mixed1, base2, unit2, qkv2, mixed2, after2, unit3, slope, act, g2d, gout, result) = refs[24:39]
+    (wt, base_in, out1, in2, g_in, y_ref, res_out, act_x, g_x, lt, ssem, rsem, bsem, tsem, z3s, z3r, z3l,
+     f7s, f7r, f7l, turn_s, turn_r, turn_l, x_s, x_r, o7s, o7r, o7l) = refs[39:]
     f = lax.axis_index("frame")
     t = lax.axis_index("tile")
+    core = lax.rem(f, 2)
     odd = lax.rem(t, 2)
     fx, fy = xor(f, 2), xor(f, 4)
     first = fx + (fy - fx) * odd
     second = fy + (fx - fy) * odd
     diag = xor_any(f, 6)
-    tz = xor(t, 1)
     sib = xor(f, 1)
-    to_sib, to_first, to_second, to_z = (sib, t), (first, t), (second, t), (f, tz)
-    greet([to_sib, (fx, t), (fy, t), to_z])
-
-    def piece(k, owner, chunk_only=True):
+    to_sib, to_first, to_second, to_z = (sib, t), (first, t), (second, t), (f, xor(t, 1))
+    greet([(xor_any(f, a), xor_any(t, b)) for a in range(8) for b in range(4) if a or b])
+
+    def piece(k, owner):
         a, r, n = chunks[k]
-        return outs[a].at[pl.ds(pl.multiple_of(owner * ins[a].shape[0] + r, 16), n)]
+        return full[a].at[pl.ds(pl.multiple_of(owner * shards[a].shape[0] + r, 16), n)]
 
     def own(k):
         a, r, n = chunks[k]
-        return ins[a].at[pl.ds(r, n)]
+        return shards[a].at[pl.ds(r, n)]
 
     def copy(k, kind):
         dev = (to_first, to_second, to_z, to_sib, to_sib, to_sib, to_sib)[kind]
@@ -486,46 +486,295 @@
         remote(dst, dst, ssem.at[k, kind], rsem.at[k, kind], to_sib).wait_recv()
 
     n = len(chunks)
+
+    def hop(k):
+        copy(k, 3).start()
+        arrived(k, 0)
+        if k + AHEAD < n:
+            copy(k + AHEAD, 0).start()
+        for kind in (1, 2, 4):
+            copy(k, kind).start()
+
+    def relay(k):
+        for kind in (1, 2):
+            arrived(k, kind)
+            copy(k, kind + 4).start()
+
+    progress = [0, 0]
+
+    def advance(hops):
+        while progress[0] < min(hops, n):
+            hop(progress[0])
+            progress[0] += 1
+            if progress[0] >= 2:
+                relay(progress[1])
+                progress[1] += 1
+        if hops > n and progress[1] < n:
+            relay(progress[1])
+            progress[1] += 1
+
+    bounce = []
+    for a, shard in enumerate(shards):
+        for r in range(0, shard.shape[0], 128):
+            for c in range(0, shard.shape[1], TILE):
+                i = len(bounce)
+                bounce.append((a, r, c, wt.at[4 + i // 8, pl.ds(i % 8 * 128, 128)]))
+
+    def bounce_in(i):
+        a, r, c, via = bounce[i]
+        return pltpu.make_async_copy(shards[a].at[pl.ds(r, 128), pl.ds(c, TILE)], via, bsem.at[i])
+
+    def bounce_out(i):
+        a, r, c, via = bounce[i]
+        row = pl.multiple_of(f * shards[a].shape[0] + r, 128)
+        return pltpu.make_async_copy(via, full[a].at[pl.ds(row, 128), pl.ds(c, TILE)], bsem.at[i])
+
+    def tile_load(i):
+        a, r, c = tiles[i]
+        src = full[a].at[pl.ds(r, TILE), pl.ds(c, TILE)]
+        return pltpu.make_async_copy(src, wt.at[i % SLOTS], tsem.at[i])
+
+    def tile(i):
+        return wt.at[i % SLOTS]
+
+    def tiles_of(a):
+        return [i for i, x in enumerate(tiles) if x[0] == a]
+
+    def complete(a):
+        ks = [k for k in range(n) if chunks[k][0] == a]
+        advance(ks[-1] + 2)
+        for k in ks:
+            for kind in (3, 4, 5, 6):
+                arrived(k, kind)
+
+    def load(ids):
+        for i in ids:
+            tile_load(i).start()
+
+    def ready(ids):
+        for i in ids:
+            tile_load(i).wait()
+
+    def token_copy(i):
+        d = xor_any(t, i)
+        return remote(tokens.at[d], base_in.at[pl.ds(pl.multiple_of(t * 64, 64), 64)], z3s.at[i - 1], z3r.at[i - 1], (f, d))
+
+    def token_arrived(i):
+        d = xor_any(t, i)
+        dst = base_in.at[pl.ds(pl.multiple_of(d * 64, 64), 64)]
+        remote(tokens.at[d], dst, z3s.at[i - 1], z3r.at[i - 1], (f, d)).wait()
+
+    own_tokens = pltpu.make_async_copy(tokens.at[t], base_in.at[pl.ds(pl.multiple_of(t * 64, 64), 64)], z3l)
+    own_tokens.start()
+    for i in (1, 2, 3):
+        token_copy(i).start()
+    for k in range(AHEAD):
+        copy(k, 0).start()
+    for i in range(len(bounce)):
+        bounce_in(i).start()
+
+    def grad_copy(i, dst_slot):
+        d = xor_any(f, i)
+        return remote(grad4.at[:, d], g_in.at[pl.ds(4 * dst_slot, 4)], f7s.at[i - 1], f7r.at[i - 1], (d, t))
+
+    own_grad = pltpu.make_async_copy(grad4.at[:, f], g_in.at[pl.ds(4 * f, 4)], f7l)
+
+    advance(1)
+    for i in range(len(bounce)):
+        bounce_in(i).wait()
+        bounce_out(i).start()
+    own_tokens.wait()
+    for i in (1, 2, 3):
+        token_arrived(i)
+
+    def plain(i):
+        rows = at(i, ROWS)
+        base1[rows, :] = base_in[rows, :]
+
+    each(base1.shape[0] // ROWS, plain)
+    norm_rows(lambda rows: base1[rows, :].astype(F32) + added[...], g1, s1, unit1)
+    own_grad.start()
+    for i in range(1, 8):
+        grad_copy(i, f).start()
+    for i in range(len(bounce)):
+        bounce_out(i).wait()
+
+    def project(unit, ids, out_ref):
+        for j, i in enumerate(ids):
+            def put(cols, y, j=j):
+                start = pl.multiple_of(cols.start + j * TILE, 512)
+                out_ref[:, pl.ds(start, 512)] = y.astype(BF16)
+
+            matmul(unit, tile(i), 512, put)
+
+    complete(0)
+    load(tiles_of(0))
+    ready(tiles_of(0))
+    project(unit1, tiles_of(0), qkv1)
+    complete(1)
+    load(tiles_of(1))
+    attention(qkv1, None, mixed1)
+    ready(tiles_of(1))
+
+    def put_after1(cols, y):
+        y = y + base1[:, cols].astype(F32) + added[:, cols]
+        y_ref[:, cols] = y
+
+    matmul(mixed1, tile(tiles_of(1)[0]), 512, put_after1)
+
+    def split(i):
+        rows = at(i, ROWS)
+        out1[pl.ds(4 * i, 4)] = y_ref[rows, :].reshape(4, 8, TILE).astype(BF16)
+
+    each(y_ref.shape[0] // ROWS, split)
+
+    slot = 4 * f + t
+    others = [(a, b) for a in range(8) for b in range(4) if a or b]
+
+    def turn_copy(i, d, dst_slot):
+        return remote(out1.at[8 * d[1] + d[0]], in2.at[dst_slot], turn_s.at[i], turn_r.at[i], d)
+
+    own_turn = pltpu.make_async_copy(out1.at[8 * t + f], in2.at[slot], turn_l)
+    own_turn.start()
+    for i, (a, b) in enumerate(others):
+        turn_copy(i, (xor_any(f, a), xor_any(t, b)), slot).start()
+    complete(2)
+    load(tiles_of(2))
+    complete(3)
+    load(tiles_of(3))
+    own_turn.wait()
+    for i, (a, b) in enumerate(others):
+        d = (xor_any(f, a), xor_any(t, b))
+        turn_copy(i, d, 4 * d[0] + d[1]).wait()
+
+    def join(i):
+        base2[at(i, ROWS), :] = in2[pl.ds(4 * i, 4)].astype(F32).reshape(ROWS, TILE).astype(BF16)
+
+    each(base2.shape[0] // ROWS, join)
+    norm_rows(lambda rows: base2[rows, :].astype(F32), g2, s2, unit2)
+    ready(tiles_of(2))
+    project(unit2, tiles_of(2), qkv2)
+    advance(12)
+    attention(qkv2, bias, mixed2)
+    advance(14)
+    ready(tiles_of(3))
+
+    def put_after2(cols, y):
+        after2[:, cols] = y + base2[:, cols].astype(F32)
+
+    matmul(mixed2, tile(tiles_of(3)[0]), 512, put_after2)
+    norm_rows(lambda rows: after2[rows, :], g3, s3, unit3)
+    complete(4)
+    load(tiles_of(4))
+
+    own_grad.wait()
+    for i in range(1, 8):
+        grad_copy(i, xor_any(f, i)).wait()
+
+    def join_grad(i):
+        g2d[at(i, ROWS), :] = g_in[pl.ds(4 * i, 4)].astype(F32).reshape(ROWS, TILE).astype(BF16)
+
+    each(g2d.shape[0] // ROWS, join_grad)
+
+    for j, i in enumerate(tiles_of(4)):
+        tile_load(i).wait()
+
+        def put_pre(cols, y, j=j):
+            cols = pl.ds(pl.multiple_of(cols.start + j * TILE, 256), 256)
+            v = y + b_in[:, cols]
+            th = jnp.tanh(GELU_A * (v + GELU_B * v * v * v))
+            act[:, cols] = (0.5 * v * (1.0 + th)).astype(BF16)
+            rise = 0.5 * (1.0 + th) + 0.5 * v * (1.0 - th * th) * GELU_A * (1.0 + 3.0 * GELU_B * v * v)
+            slope[:, cols] = rise.astype(BF16)
+
+        matmul(unit3, tile(i), 256, put_pre)
+
+    shard = shards[5].shape[0]
+    swaps = [
+        remote(act.at[:, pl.ds(pl.multiple_of((2 * q + 1 - core) * shard, shard), shard)],
+               act_x.at[:, pl.ds(q * shard, shard)], x_s.at[q], x_r.at[q], to_sib)
+        for q in range(4)
+    ]
+    swaps.append(remote(g2d, g_x, x_s.at[4], x_r.at[4], to_sib))
+    for c in swaps:
+        c.start()
+    advance(16)
+    for c in swaps:
+        c.wait()
+    wgrad(core, shard, act, act_x, g2d, g_x, gout, lt)
+    complete(5)
+    ids = tiles_of(5)
+    load(ids)
+    for j, i in enumerate(ids):
+        tile_load(i).wait()
+
+        def part(h, i=i, j=j):
+            cols = at(h, 512)
+            y = dot(act[:, j * TILE : (j + 1) * TILE], wt[i % SLOTS, :, cols])
+            y_ref[:, cols] = y + (after2[:, cols] + b_out[:, cols] if j == 0 else y_ref[:, cols])
+
+        each(2, part)
+
+    def split_res(i):
+        res_out[pl.ds(4 * i, 4)] = y_ref[at(i, ROWS), :].reshape(4, 8, TILE).astype(BF16)
+
+    each(y_ref.shape[0] // ROWS, split_res)
+
+    def res_copy(i, dst):
+        d = xor_any(f, i)
+        return remote(res_out.at[pl.ds(4 * d, 4)], result.at[:, dst], o7s.at[i - 1], o7r.at[i - 1], (d, t))
+
+    own_res = pltpu.make_async_copy(res_out.at[pl.ds(4 * f, 4)], result.at[:, f], o7l)
+    own_res.start()
+    for i in range(1, 8):
+        res_copy(i, f).start()
     for k in range(n):
-        pltpu.make_async_copy(own(k), piece(k, f), lsem.at[k]).start()
-    for k in range(min(2, n)):
-        copy(k, 0).start()
-    for k in range(n + 1):
-        if k < n:
-            copy(k, 3).start()
-            arrived(k, 0)
-            if k + 2 < n:
-                copy(k + 2, 0).start()
-            for kind in (1, 2, 4):
-                copy(k, kind).start()
-        if k >= 1:
-            for kind in (1, 2):
-                arrived(k - 1, kind)
-                copy(k - 1, kind + 4).start()
-    for k in range(n):
-        for kind in (3, 4, 5, 6):
-            arrived(k, kind)
         for kind in range(7):
             copy(k, kind).wait_send()
-        pltpu.make_async_copy(own(k), piece(k, f), lsem.at[k]).wait()
-
-
-def gather_weights(mats):
+    own_res.wait()
+    for i in range(1, 8):
+        res_copy(i, xor_any(f, i)).wait()
+
+
+def forward(mats, tokens, grad4, added, vecs, bias):
+    width = tokens.shape[2]
+    rows = tokens.shape[0] * tokens.shape[1]
+    ff = mats[4].shape[1]
+    fulls = [(8 * m.shape[0], m.shape[1]) for m in mats]
     chunks = gather_chunks([m.shape for m in mats])
-    n = len(mats)
+    tiles = weight_tiles(fulls)
+    n = len(chunks)
+    dma = pltpu.SemaphoreType.DMA
+    act_shapes = [
+        (width, BF16), (width, BF16), (3 * width, BF16), (width, BF16),
+        (width, BF16), (width, BF16), (3 * width, BF16), (width, BF16),
+        (width, F32), (width, BF16), (ff, BF16), (ff, BF16), (width, BF16),
+    ]
+    units = mats[5].shape[0] // 128
+    outs = [jax.ShapeDtypeStruct(s, BF16) for s in fulls]
+    outs += [jax.ShapeDtypeStruct((rows, w), d) for w, d in act_shapes]
+    outs += [jax.ShapeDtypeStruct((units, 4, 128, TILE), BF16), jax.ShapeDtypeStruct(grad4.shape, BF16)]
+    blocks = (32, 8, width)
     return pl.pallas_call(
-        functools.partial(gather_kernel, n, chunks),
-        out_shape=[jax.ShapeDtypeStruct((8 * m.shape[0], m.shape[1]), m.dtype) for m in mats],
-        in_specs=[HBM_SPEC] * n,
-        out_specs=[HBM_SPEC] * n,
+        functools.partial(forward_kernel, chunks, tiles),
+        out_shape=outs,
+        in_specs=[HBM_SPEC] * 8 + [VMEM_SPEC] * 10,
+        out_specs=[HBM_SPEC] * 6 + [VMEM_SPEC] * 14 + [HBM_SPEC],
         scratch_shapes=[
-            pltpu.SemaphoreType.DMA((len(chunks), 7)),
-            pltpu.SemaphoreType.DMA((len(chunks), 7)),
-            pltpu.SemaphoreType.DMA((len(chunks),)),
+            pltpu.VMEM((SLOTS, TILE, TILE), BF16),
+            pltpu.VMEM((rows, width), BF16),
+            pltpu.VMEM(blocks, BF16), pltpu.VMEM(blocks, BF16), pltpu.VMEM(blocks, BF16),
+            pltpu.VMEM((rows, width), F32),
+            pltpu.VMEM(blocks, BF16),
+            pltpu.VMEM((rows, ff // 2), BF16), pltpu.VMEM((rows, width), BF16),
+            pltpu.VMEM((512, 2 * rows), BF16),
+            dma((n, 7)), dma((n, 7)), dma((16,)), dma((len(tiles),)),
+            dma((3,)), dma((3,)), dma, dma((7,)), dma((7,)), dma,
+            dma((31,)), dma((31,)), dma, dma((5,)), dma((5,)), dma((7,)), dma((7,)), dma,
         ],
         compiler_params=params(collective_id=0, has_side_effects=True),
-        name="gather_weights",
-    )(*mats)
+        name="forward",
+    )(*mats, tokens, grad4, added, *vecs, bias)
 
 
 def add_into(dst, a, b, rows):
@@ -721,6 +970,12 @@
     )(*grads, small)
 
 
+def plain_norm(h, gain, shift):
+    cen = h - jnp.mean(h, -1, keepdims=True)
+    inv = lax.rsqrt(jnp.mean(cen * cen, -1, keepdims=True) + EPS)
+    return cen * inv * gain + shift
+
+
 def per_device(on_boxes, tokens, out_grad, actions, segments, frame_mask, embed,
                ln1_gain, ln1_shift, spatial_qkv, spatial_out,
                ln2_gain, ln2_shift, temporal_qkv, temporal_out,
@@ -738,24 +993,8 @@
     mats = (spatial_qkv, spatial_out, temporal_qkv, temporal_out, ffn_in, ffn_out)
 
     grad4 = out_grad.reshape(frames_dev, n_frame, place, width)
-    if on_boxes:
-        w_qs, w_os, w_qt, w_ot, w_in, w_out = gather_weights(mats)
-        base1 = swap_blocks(tokens, tokens.shape, ("tile",),
-                            lambda f, t: t, lambda f, t: t, 2, "tokens_to_frames")
-        g = swap_blocks(grad4, (n_frame, frames_dev, place, width), ("frame",),
-                        lambda f, t: (slice(None), f), lambda f, t: f, 3, "grad_to_places")
-    else:
-        w_qs, w_os, w_qt, w_ot, w_in, w_out = (lax.all_gather(m, "frame", axis=0, tiled=True) for m in mats)
-        base1 = lax.all_to_all(tokens, "tile", 0, 0, tiled=True)
-        g = lax.all_to_all(grad4.transpose(1, 0, 2, 3), "frame", 0, 0, tiled=True)
-    base1 = base1.reshape(rows, width)
-    g = g.reshape(rows, width)
-
     action = lax.dynamic_index_in_dim(actions, t, keepdims=False)
     added = lax.dynamic_slice_in_dim(embed, action, 1, 0)
-
-    unit1, qkv1, mixed1, after1 = attn_fwd(
-        base1, added, row(ln1_gain), row(ln1_shift), w_qs, w_os, None, BF16, "spatial_forward")
 
     blocks = n_frame * n_tile
 
@@ -775,8 +1014,6 @@
                 y = y.reshape(n_frame, n_tile, -1, width).transpose(1, 0, 2, 3)
         return y.reshape(rows, width)
 
-    base2 = turn(after1, True, 4, "frames_to_places")
-
     number = jnp.arange(rows, dtype=jnp.int32)
     of_frame, of_place = number // place, number % place
     seg_row = jnp.repeat(segments, place)
@@ -789,11 +1026,29 @@
     )
     bias = jnp.where(allowed, 0.0, -1e30).astype(F32)
     nothing = jnp.zeros((1, width), F32)
-    unit2, qkv2, mixed2, after2 = attn_fwd(
-        base2, nothing, row(ln2_gain), row(ln2_shift), w_qt, w_ot, bias, F32, "temporal_forward")
-    unit3, pre, act, result = ffn_fwd(
-        after2, row(ln3_gain), row(ln3_shift), w_in, row(ffn_in_bias), w_out, row(ffn_out_bias))
-    d_pre, d_after2, dg3, ds3, d_bin, d_bout = ffn_bwd(g, pre, after2, row(ln3_gain), w_in, w_out)
+    vecs = [row(v) for v in (ln1_gain, ln1_shift, ln2_gain, ln2_shift, ln3_gain, ln3_shift, ffn_in_bias, ffn_out_bias)]
+    if on_boxes:
+        (w_qs, w_os, w_qt, w_ot, w_in, w_out, base1, unit1, qkv1, mixed1, base2, unit2, qkv2, mixed2,
+         after2, unit3, slope, act, g, g_out, result) = forward(mats, tokens, grad4, added, vecs, bias)
+    else:
+        w_qs, w_os, w_qt, w_ot, w_in, w_out = (lax.all_gather(m, "frame", axis=0, tiled=True) for m in mats)
+        base1 = lax.all_to_all(tokens, "tile", 0, 0, tiled=True).reshape(rows, width)
+        g = lax.all_to_all(grad4.transpose(1, 0, 2, 3), "frame", 0, 0, tiled=True).reshape(rows, width)
+        unit1, qkv1, mixed1, after1 = attn_fwd(
+            base1, added, vecs[0], vecs[1], w_qs, w_os, None, BF16, "spatial_forward")
+        base2 = turn(after1, True, 4, "frames_to_places")
+        unit2, qkv2, mixed2, after2 = attn_fwd(
+            base2, nothing, vecs[2], vecs[3], w_qt, w_ot, bias, F32, "temporal_forward")
+        unit3 = plain_norm(after2, ln3_gain, ln3_shift).astype(BF16)
+        pre = jnp.dot(unit3, w_in, preferred_element_type=F32) + ffn_in_bias
+        th = jnp.tanh(GELU_A * (pre + GELU_B * pre * pre * pre))
+        act = (0.5 * pre * (1.0 + th)).astype(BF16)
+        slope = 0.5 * (1.0 + th) + 0.5 * pre * (1.0 - th * th) * GELU_A * (1.0 + 3.0 * GELU_B * pre * pre)
+        slope = slope.astype(BF16)
+        result = after2 + jnp.dot(act, w_out, preferred_element_type=F32) + ffn_out_bias
+        result = result.astype(BF16).reshape(n_frame, frames_dev, place, width)
+        result = lax.all_to_all(result, "frame", 0, 0, tiled=True).transpose(1, 0, 2, 3)
+    d_pre, d_after2, dg3, ds3, d_bin, d_bout = ffn_bwd(g, slope, after2, row(ln3_gain), w_in, w_out)
     low2, d_qkv2, d_after1, dg2, ds2 = attn_bwd(
         base2, nothing, row(ln2_gain), w_qt, w_ot, d_after2, qkv2, bias, BF16, "temporal_backward")
     d_out1 = turn(d_after1, False, 5, "places_to_frames")
@@ -801,15 +1056,11 @@
         base1, added, row(ln1_gain), w_qs, w_os, d_out1, qkv1, None, F32, "spatial_backward")
 
     tokens_grad = d_start.astype(BF16).reshape(n_tile, tile_tokens, width)
-    result = result.reshape(n_frame, frames_dev, place, width)
     if on_boxes:
         tokens_grad = swap_blocks(tokens_grad, tokens.shape, ("tile",),
                                   lambda f, t: t, lambda f, t: t, 6, "tokens_grad_to_tiles")
-        result = swap_blocks(result, grad4.shape, ("frame",),
-                             lambda f, t: f, lambda f, t: (slice(None), f), 7, "result_to_tiles")
     else:
         tokens_grad = lax.all_to_all(tokens_grad, "tile", 0, 0, tiled=True)
-        result = lax.all_to_all(result, "frame", 0, 0, tiled=True).transpose(1, 0, 2, 3)
     result = result.reshape(tokens.shape)
 
     one_hot = (action == jnp.arange(embed.shape[0], dtype=jnp.int32)).astype(F32)
@@ -828,7 +1079,7 @@
             [d_embed, dg1, ds1, dg2, ds2, dg3, ds3, d_bout, d_bin.reshape(-1, width)], 0)
         small = jnp.pad(small, ((0, -small.shape[0] % 8), (0, 0)))
         core = lax.rem(f, 2)
-        grads = [wgrad_units(a, b, a.shape[1] // 8, core, name) for a, b, name in pairs]
+        grads = [wgrad_units(a, b, a.shape[1] // 8, core, name) for a, b, name in pairs[:5]] + [g_out]
         order = (5, 4, 3, 2, 1, 0)
         out, small = reduce_units([grads[i] for i in order], small)
         summed = [None] * 6

time: 631 us -> 543 us (0.86)
  Pallas kernels: 535 us -> 463 us
  local copies, waits for them, and re-layouts: 79.3 us -> 59.9 us
    pallas_call x6 -> x2, Pallas kernels: 83.7 us -> 31 us  [swap_blocks(): pl.pallas_call(functools.partial(swap_kernel, axes, src_of, dst_of), out_...]
    dynamic_slice x5, local copies, waits for them, and re-layouts: 33 us -> 17.9 us  [wgrad_units(): lax.dynamic_index_in_dim(parts, 1 - core, 2, False).reshape(tok, 4 * shard)]
    pallas_call x4 -> x1, Pallas kernels: 179 us -> 170 us  [forward(): pl.pallas_call(functools.partial(forward_kernel, chunks, tiles), out_shap...]
    pallas_call x6 -> x5, Pallas kernels: 36.2 us -> 28.2 us  [wgrad_units(): pl.pallas_call(functools.partial(wgrad_kernel, shard), out_shape=jax.Shap...]
    unnamed x77 -> x45, local copies, waits for them, and re-layouts: 21.5 us -> 16.9 us
  transfers between devices with their start and end apart: 12 -> 10, of which waited for: 1 -> 1; matrix products, arithmetic and copies ran while one was open for 9% -> 7% of each run, Pallas kernels for 17% -> 16%
where the time goes in v2:
time: 543 us; the launch traced here: 534 us
  Pallas kernels  463 us (85%)
  local copies, waits for them, and re-layouts  59.9 us (11%)
    pallas_call x1, Pallas kernels, reduce_units(): pl.pallas_call(functools.partial(reduce_kernel, units, len(grads)), out_s...  179 us
    pallas_call x1, Pallas kernels, forward(): pl.pallas_call(functools.partial(forward_kernel, chunks, tiles), out_shap...  170 us
    pallas_call x2, Pallas kernels, attn_bwd(): pl.pallas_call(functools.partial(attn_bwd_kernel, bias is not None), out_...  36.9 us
    pallas_call x2, Pallas kernels, swap_blocks(): pl.pallas_call(functools.partial(swap_kernel, axes, src_of, dst_of), out_...  31 us
    pallas_call x5, Pallas kernels, wgrad_units(): pl.pallas_call(functools.partial(wgrad_kernel, shard), out_shape=jax.Shap...  28.2 us
    dynamic_slice x5, local copies, waits for them, and re-layouts, wgrad_units(): lax.dynamic_index_in_dim(parts, 1 - core, 2, False).reshape(tok, 4 * shard)  17.9 us
    pallas_call x1, Pallas kernels, ffn_bwd(): pl.pallas_call(ffn_bwd_kernel, out_shape=[jax.ShapeDtypeStruct((rows, ff)...  17.7 us
    unnamed x45, local copies, waits for them, and re-layouts  16.9 us
  transfers between devices with their start and end apart: 10, of which 1 were waited for; matrix products, arithmetic and copies ran while one was open for 7% of the time, Pallas kernels for 16%

profile of v2, /device:TPU:0, one launch (start us, length us, event | category | flops | bytes accessed | tf_op | source)
XLA Modules:
  0.0 533.6 jit_solution(11482054135001494903)
XLA Ops:
  0.7 1.3 dynamic_slice.38
  3.2 0.7 broadcast_in_dim.60
  6.1 0.9 and_select_fusion.refs_17_.rest_0_
  7.0 169.9 %forward.1 = (bf16[1024,3072]{1,0:T(8,128)(2,1)}, bf16[1024,1024]{1,0:T(8,128)(2,1)}, bf16[1024,3072]{1,0:T(8,128)(2,1)}, bf16[1024,1024]{1,0:T(8,128)(2,1)}, bf...) custom-call(bf16[128,3072]{1,0:T(8,128)(2,1)} %refs_0_.1, ...), custom_call_target="tpu_custom_call" | custom-call | tf_op jit(solution)/shard_map/forward/pallas_call | solution.py:758
  177.0 17.7 %ffn_backward.1 = (bf16[256,4096]{1,0:T(8,128)(2,1)}, f32[256,1024]{1,0:T(8,128)}, f32[1,1024]{1,0:T(1,128)}, f32[1,1024]{1,0:T(1,128)}, f32[1,4096]{1,0:T(1,128)}, /*index=5*/f32[1,1024]{1,0:T(1,128)}) custom-call(bf16[256,1024]{1,0:T(8,128)(2,1)} %get-tuple-element.62.g_ref, bf16[256,4096]{1,0:T(8,128)(2,1)} %get-tuple-element.63.slope_ref, ...), custom_call_target="tpu_custom_call" | custom-call | tf_op jit(solution)/shard_map/ffn_backward/pallas_call | solution.py:290
  195.3 18.7 %temporal_backward.1 = (bf16[256,1024]{1,0:T(8,128)(2,1)}, bf16[256,3072]{1,0:T(8,128)(2,1)}, bf16[256,1024]{1,0:T(8,128)(2,1)}, f32[1,1024]{1,0:T(1,128)}, f32[1,1024]{1,0:T(1,128)}) custom-call(bf16[256,1024]{1,0:T(8,128)(2,1)} %get-tuple-element.59.base_ref, f32[1,1024]{1,0:T(1,128)} %broadcast_in_dim.64.added_ref, f32[1,1024]{1,0:T(1,128)} %bitcast.112, ...), custom_call_target="tpu_custom_call" | custom-call | tf_op jit(solution)/shard_map/temporal_backward/pallas_call | solution.py:244
  214.0 17.5 %places_to_frames.1 = bf16[32,8,1024]{2,1,0:T(8,128)(2,1)} custom-call(bf16[32,8,1024]{2,1,0:T(8,128)(2,1)} %bitcast.108), custom_call_target="tpu_custom_call" | custom-call | tf_op jit(solution)/shard_map/places_to_frames/pallas_call | solution.py:411
  231.5 18.3 %spatial_backward.1 = (bf16[256,1024]{1,0:T(8,128)(2,1)}, bf16[256,3072]{1,0:T(8,128)(2,1)}, f32[256,1024]{1,0:T(8,128)}, f32[1,1024]{1,0:T(1,128)}, f32[1,1024]{1,0:T(1,128)}) custom-call(bf16[256,1024]{1,0:T(8,128)(2,1)} %get-tuple-element.56.base_ref, f32[1,1024]{1,0:T(1,128)} %constant_dynamic-slice_fusion.refs_8_.added_ref, f32[1,1024]{1,0:T(1,128)} %bitcast.116, ...), custom_call_target="tpu_custom_call" | custom-call | tf_op jit(solution)/shard_map/spatial_backward/pallas_call | solution.py:244
  250.3 1.4 reshape.206
  251.7 3.3 dynamic-slice_reduce_fusion
  255.0 0.7 copy.95
  256.3 3.3 dynamic-slice_reduce_fusion.2
  259.6 0.7 copy.97
  260.7 1.4 reshape.197
  262.1 3.3 dynamic-slice_reduce_fusion.6
  266.2 1.0 collective-permute-done.2.left2_ref
  267.9 1.4 reshape.200
  269.3 4.0 dynamic-slice_reduce_fusion.4
  273.3 0.7 copy.99
  274.1 1.4 reshape.194
  275.5 4.0 dynamic-slice_reduce_fusion.8
  279.5 0.7 copy.103
  280.3 0.9 fusion.2
  283.6 1.0 concatenate.3
  285.2 0.7 copy.96
  285.9 0.8 copy.98
  286.7 0.7 copy.100
  287.5 0.7 copy.102
  288.2 0.7 copy.104
  288.9 13.5 %tokens_grad_to_tiles.1 = bf16[4,64,1024]{2,1,0:T(8,128)(2,1)} custom-call(bf16[4,64,1024]{2,1,0:T(8,128)(2,1)} %bitcast.89), custom_call_target="tpu_custom_call" | custom-call | tf_op jit(solution)/shard_map/tokens_grad_to_tiles/pallas_call | solution.py:411
  302.4 3.4 spatial_out_grad.1.refs_4_
  305.8 3.5 temporal_out_grad.1.refs_2_
  309.3 6.5 %spatial_qkv_grad.1.refs_5_ = bf16[3,4,128,1024]{3,2,1,0:T(8,128)(2,1)} custom-call(bf16[256,512]{1,0:T(8,128)(2,1)} %bitcast.106, bf16[256,512]{1,0:T(8,128)(2,1)} %collective-permute-done.8.left2_ref, bf16[256,3072]{1,0:T(8,128)(2,1)} %get-tuple-element.82.right_ref, bf16[256,3072]{1,0:T(8,128)(2,1)} %collective-permute-done.9.right2_ref), custom_call_target="tpu_custom_call" | custom-call | tf_op jit(solution)/shard_map/spatial_qkv_grad/pallas_call | solution.py:334
  315.8 6.5 %temporal_qkv_grad.1.refs_3_ = bf16[3,4,128,1024]{3,2,1,0:T(8,128)(2,1)} custom-call(bf16[256,512]{1,0:T(8,128)(2,1)} %bitcast.105, bf16[256,512]{1,0:T(8,128)(2,1)} %collective-permute-done.4.left2_ref, bf16[256,3072]{1,0:T(8,128)(2,1)} %get-tuple-element.78.right_ref, bf16[256,3072]{1,0:T(8,128)(2,1)} %collective-permute-done.5.right2_ref), custom_call_target="tpu_custom_call" | custom-call | tf_op jit(solution)/shard_map/temporal_qkv_grad/pallas_call | solution.py:334
  322.4 1.3 copy-done.4
  323.7 8.3 %ffn_in_grad.1.refs_1_ = bf16[4,4,128,1024]{3,2,1,0:T(8,128)(2,1)} custom-call(bf16[256,512]{1,0:T(8,128)(2,1)} %bitcast.92, bf16[256,512]{1,0:T(8,128)(2,1)} %collective-permute-done.left2_ref, bf16[256,4096]{1,0:T(8,128)(2,1)} %get-tuple-element.74.right_ref, bf16[256,4096]{1,0:T(8,128)(2,1)} %copy-done.4), custom_call_target="tpu_custom_call" | custom-call | tf_op jit(solution)/shard_map/ffn_in_grad/pallas_call | solution.py:334
  332.0 179.5 %reduce_gradients.1 = (f32[16,128,1024]{2,1,0:T(8,128)}, f32[24,1024]{1,0:T(8,128)}) custom-call(bf16[4,4,128,1024]{3,2,1,0:T(8,128)(2,1)} %get-tuple-element.72.refs_0_, bf16[4,4,128,1024]{3,2,1,0:T(8,128)(2,1)} %ffn_in_grad.1.refs_1_, bf16[1,4,128,1024]{3,2,1,0:T(8,128)(2,1)} %temporal_out_grad.1.refs_2_, ...), custom_call_target="tpu_custom_call" | custom-call | tf_op jit(solution)/shard_map/reduce_gradients/pallas_call | solution.py:949
  511.5 5.1 fusion.1
  516.6 1.1 copy-done.2
  517.6 1.9 slice_bitcast_fusion.1
  519.5 1.0 slice_bitcast_fusion.3
  521.8 1.9 copy.59
  523.7 1.8 copy.62
  525.5 1.9 copy.57
  527.4 1.6 copy.60
  529.5 1.6 copy.61
  531.8 0.8 copy.108
  532.5 0.8 copy.109
  (65 shorter events, 10.6 us)
Async XLA Ops:
  0.7 4.9 copy-start
  194.6 127.7 %collective-permute-start.1 = (bf16[256,4096]{1,0:T(8,128)(2,1)}, bf16[256,4096]{1,0:T(8,128)(2,1)S(1)}, u32[]{:S(2)}, u32[]{:S(2)}) collective-permute-start(bf16[256,4096]{1,0:T(8,128)(2,1)} %get-tuple-element.74.right_ref), channel_id=1, source_target_pairs={{0,4},{4,0},{8,12},{12,8},{16,20},{20,16},{24,28},{28,24},{1,5},{5... | collective-permute-start | bytes 6291464 | tf_op jit(solution)/shard_map/ppermute | solution.py:332
  249.8 6.1 %copy-start.10 = (bf16[256,1024]{1,0:T(8,128)(2,1)S(1)}, bf16[256,1024]{1,0:T(8,128)(2,1)}, u32[]{:S(2)}) copy-start(bf16[256,1024]{1,0:T(8,128)(2,1)} %get-tuple-element.79) | copy-start | bytes 1572868
  249.8 59.5 %collective-permute-start.9 = (bf16[256,3072]{1,0:T(8,128)(2,1)}, bf16[256,3072]{1,0:T(8,128)(2,1)}, u32[]{:S(2)}, u32[]{:S(2)}) collective-permute-start(bf16[256,3072]{1,0:T(8,128)(2,1)} %get-tuple-element.82.right_ref), channel_id=1, source_target_pairs={{0,4},{4,0},{8,12},{12,8},{16,20},{20,16},{24,28},{28,24},{1,5},{5... | collective-permute-start | bytes 4718600 | tf_op jit(solution)/shard_map/ppermute | solution.py:332
  249.9 65.9 %collective-permute-start.5 = (bf16[256,3072]{1,0:T(8,128)(2,1)}, bf16[256,3072]{1,0:T(8,128)(2,1)}, u32[]{:S(2)}, u32[]{:S(2)}) collective-permute-start(bf16[256,3072]{1,0:T(8,128)(2,1)} %get-tuple-element.78.right_ref), channel_id=1, source_target_pairs={{0,4},{4,0},{8,12},{12,8},{16,20},{20,16},{24,28},{28,24},{1,5},{5... | collective-permute-start | bytes 4718600 | tf_op jit(solution)/shard_map/ppermute | solution.py:332
  255.7 9.7 %collective-permute-start.8 = (bf16[256,512]{1,0:T(8,128)(2,1)}, bf16[256,512]{1,0:T(8,128)(2,1)}, u32[]{:S(2)}, u32[]{:S(2)}) collective-permute-start(bf16[256,512]{1,0:T(8,128)(2,1)} %bitcast.75), channel_id=1, source_target_pairs={{0,4},{4,0},{8,12},{12,8},{16,20},{20,16},{24,28},{28,24},{1,5},{5... | collective-permute-start | bytes 786440 | tf_op jit(solution)/shard_map/ppermute | solution.py:331
  260.3 5.5 %collective-permute-start.6 = (bf16[256,512]{1,0:T(8,128)(2,1)}, bf16[256,512]{1,0:T(8,128)(2,1)}, u32[]{:S(2)}, u32[]{:S(2)}) collective-permute-start(bf16[256,512]{1,0:T(8,128)(2,1)} %bitcast.77), channel_id=1, source_target_pairs={{0,4},{4,0},{8,12},{12,8},{16,20},{20,16},{24,28},{28,24},{1,5},{5... | collective-permute-start | bytes 786440 | tf_op jit(solution)/shard_map/ppermute | solution.py:331
  265.4 1.8 collective-permute-start.2
  265.9 15.3 %collective-permute-start.7 = (bf16[256,1024]{1,0:T(8,128)(2,1)}, bf16[256,1024]{1,0:T(8,128)(2,1)}, u32[]{:S(2)}, u32[]{:S(2)}) collective-permute-start(bf16[256,1024]{1,0:T(8,128)(2,1)} %get-tuple-element.80.right_ref), channel_id=1, source_target_pairs={{0,4},{4,0},{8,12},{12,8},{16,20},{20,16},{24,28},{28,24},{1,5},{5... | collective-permute-start | bytes 1572872 | tf_op jit(solution)/shard_map/ppermute | solution.py:332
  267.2 0.7 copy-start.11
  267.2 14.1 %collective-permute-start.3 = (bf16[256,1024]{1,0:T(8,128)(2,1)}, bf16[256,1024]{1,0:T(8,128)(2,1)}, u32[]{:S(2)}, u32[]{:S(2)}) collective-permute-start(bf16[256,1024]{1,0:T(8,128)(2,1)} %get-tuple-element.76.right_ref), channel_id=1, source_target_pairs={{0,4},{4,0},{8,12},{12,8},{16,20},{20,16},{24,28},{28,24},{1,5},{5... | collective-permute-start | bytes 1572872 | tf_op jit(solution)/shard_map/ppermute | solution.py:332
  275.5 4.8 copy-start.6
  275.5 7.3 %copy-start.13 = (f32[1,4096]{1,0:T(1,128)S(1)}, f32[1,4096]{1,0:T(1,128)}, u32[]{:S(2)}) copy-start(f32[1,4096]{1,0:T(1,128)} %get-tuple-element.90) | copy-start | bytes 49156
  279.5 7.2 %copy-start.7 = (bf16[256,4,128]{2,1,0:T(4,128)(2,1)S(1)}, bf16[256,4,128]{2,1,0:T(4,128)(2,1)}, u32[]{:S(2)}) copy-start(bf16[256,4,128]{2,1,0:T(4,128)(2,1)} %get-tuple-element.115) | copy-start | bytes 786436
  280.3 7.9 %copy-start.8 = (bf16[256,4,128]{2,1,0:T(4,128)(2,1)S(1)}, bf16[256,4,128]{2,1,0:T(4,128)(2,1)}, u32[]{:S(2)}) copy-start(bf16[256,4,128]{2,1,0:T(4,128)(2,1)} %get-tuple-element.119) | copy-start | bytes 786436
  281.2 34.7 %collective-permute-start.4 = (bf16[256,512]{1,0:T(8,128)(2,1)}, bf16[256,512]{1,0:T(8,128)(2,1)}, u32[]{:S(2)}, u32[]{:S(2)}) collective-permute-start(bf16[256,512]{1,0:T(8,128)(2,1)} %bitcast.79), channel_id=1, source_target_pairs={{0,4},{4,0},{8,12},{12,8},{16,20},{20,16},{24,28},{28,24},{1,5},{5... | collective-permute-start | bytes 786440 | tf_op jit(solution)/shard_map/ppermute | solution.py:331
  281.3 41.0 %collective-permute-start = (bf16[256,512]{1,0:T(8,128)(2,1)}, bf16[256,512]{1,0:T(8,128)(2,1)}, u32[]{:S(2)}, u32[]{:S(2)}) collective-permute-start(bf16[256,512]{1,0:T(8,128)(2,1)} %bitcast.83), channel_id=1, source_target_pairs={{0,4},{4,0},{8,12},{12,8},{16,20},{20,16},{24,28},{28,24},{1,5},{5... | collective-permute-start | bytes 786440 | tf_op jit(solution)/shard_map/ppermute | solution.py:331
  322.4 1.3 copy-start.4
  511.5 6.2 %copy-start.2 = (f32[16,128,1024]{2,1,0:T(8,128)S(1)}, f32[16,128,1024]{2,1,0:T(8,128)}, u32[]{:S(2)}) copy-start(f32[16,128,1024]{2,1,0:T(8,128)} %get-tuple-element.92) | copy-start | bytes 25165828
  519.5 1.0 copy-start.12
  527.4 1.6 copy-start.3
  529.5 2.3 copy-start.9
  529.5 3.8 copy-start.1
  529.5 3.0 copy-start.5

commit v3 on v2

v3 whole, which is shorter than its diff:
```python
import functools

import jax
import jax.numpy as jnp
from jax import lax
from jax.experimental import pallas as pl
from jax.experimental.pallas import tpu as pltpu
from jax.sharding import PartitionSpec as P

HD = 64
LANES = 128
EPS = 1e-5
MESH = pl.DeviceIdType.MESH
F32 = jnp.float32
BF16 = jnp.bfloat16
VMEM_SPEC = pl.BlockSpec(memory_space=pltpu.VMEM)
HBM_SPEC = pl.BlockSpec(memory_space=pltpu.HBM)


def params(**kw):
    return pltpu.CompilerParams(vmem_limit_bytes=58 * 1024 * 1024, **kw)


def at(j, size):
    return pl.ds(pl.multiple_of(j * size, size), size)


def each(n, fn):
    def step(i, carry):
        fn(i)
        return carry

    lax.fori_loop(0, n, step, 0)


def dot(a, b):
    return jnp.dot(a, b, preferred_element_type=F32)


def dot_nt(a, b):
    return lax.dot_general(a, b, (((1,), (1,)), ((), ())), preferred_element_type=F32)


def dot_tn(a, b):
    return lax.dot_general(a, b, (((0,), (0,)), ((), ())), preferred_element_type=F32)


def normed(h):
    cen = h - jnp.mean(h, -1, keepdims=True)
    inv = lax.rsqrt(jnp.mean(cen * cen, -1, keepdims=True) + EPS)
    return cen * inv, inv


ROWS = 32


def norm_rows(load, gain_ref, shift_ref, unit_ref):
    def step(i):
        rows = at(i, ROWS)
        xhat, _ = normed(load(rows))
        unit_ref[rows, :] = (xhat * gain_ref[...] + shift_ref[...]).astype(BF16)

    each(unit_ref.shape[0] // ROWS, step)


def fold(x):
    return jnp.sum(x.reshape(x.shape[0] // 8, 8, x.shape[1]), 0)


def norm_back(load, du_ref, gain_ref, dgain_ref, dshift_ref, acc_ref, store):
    acc_ref[...] = jnp.zeros_like(acc_ref)

    def step(i):
        rows = at(i, ROWS)
        xhat, inv = normed(load(rows))
        du = du_ref[rows, :]
        acc_ref[0] += fold(du * xhat)
        acc_ref[1] += fold(du)
        dx = du * gain_ref[...]
        dh = inv * (
            dx - jnp.mean(dx, -1, keepdims=True) - xhat * jnp.mean(dx * xhat, -1, keepdims=True)
        )
        store(rows, dh)

    each(du_ref.shape[0] // ROWS, step)
    dgain_ref[...] = jnp.sum(acc_ref[0], 0, keepdims=True)
    dshift_ref[...] = jnp.sum(acc_ref[1], 0, keepdims=True)


def head_masks():
    lane = lax.broadcasted_iota(jnp.int32, (1, LANES), 1)
    low = jnp.where(lane < HD, 1.0, 0.0)
    return low.astype(BF16), (1.0 - low).astype(BF16)


def head_probs(qm, k, bias_ref):
    s = dot_nt(qm, k) * (HD**-0.5)
    if bias_ref is not None:
        s = s + bias_ref[...]
    e = jnp.exp(s - jnp.max(s, -1, keepdims=True))
    return e * (1.0 / jnp.sum(e, -1, keepdims=True))


def attention(qkv_ref, bias_ref, mixed_ref):
    width = mixed_ref.shape[1]
    per = width // LANES
    masks = head_masks()

    def pair(p):
        q, k, v = (qkv_ref[:, at(p + i * per, LANES)] for i in range(3))
        out = 0.0
        for m in masks:
            out = out + dot(head_probs(q * m, k, bias_ref).astype(BF16), v * m)
        mixed_ref[:, at(p, LANES)] = out.astype(BF16)

    each(per, pair)


def attention_back(qkv_ref, bias_ref, dmix_ref, dqkv_ref):
    width = dmix_ref.shape[1]
    per = width // LANES
    masks = head_masks()
    scale = HD**-0.5

    def pair(p):
        q, k, v = (qkv_ref[:, at(p + i * per, LANES)] for i in range(3))
        dm = dmix_ref[:, at(p, LANES)]
        dq = dk = dv = 0.0
        for m in masks:
            qm = q * m
            dmm = dm * m
            probs = head_probs(qm, k, bias_ref)
            dp = dot_nt(dmm, v)
            ds = probs * (dp - jnp.sum(probs * dp, -1, keepdims=True))
            ds = ds.astype(BF16)
            dq = dq + dot(ds, k * m)
            dk = dk + dot_tn(ds, qm)
            dv = dv + dot_tn(probs.astype(BF16), dmm)
        dqkv_ref[:, at(p, LANES)] = (dq * scale).astype(BF16)
        dqkv_ref[:, at(p + per, LANES)] = (dk * scale).astype(BF16)
        dqkv_ref[:, at(p + 2 * per, LANES)] = dv.astype(BF16)

    each(per, pair)


def matmul(x_ref, w_ref, block, store):
    def step(j):
        cols = at(j, block)
        store(cols, dot(x_ref[...], w_ref[:, cols]))

    each(w_ref.shape[1] // block, step)


def matmul_nt(x_ref, w_ref, block, store):
    def step(j):
        rows = at(j, block)
        store(rows, dot_nt(x_ref[...], w_ref[rows, :]))

    each(w_ref.shape[0] // block, step)


def wgrad(core, shard, left, left_x, right, right_x, out, lt):
    tok = left.shape[0]
    col_blocks = right.shape[1] // TILE
    for rb in range(shard // 128):
        for q in range(4):
            cols = pl.ds(pl.multiple_of((2 * q + core) * shard + rb * 128, 128), 128)
            lt[q * 128 : (q + 1) * 128, :tok] = left[:, cols].T
            cols = pl.ds(q * shard + rb * 128, 128)
            lt[q * 128 : (q + 1) * 128, tok:] = left_x[:, cols].T

        def step(j, rb=rb):
            cols = at(j, 512)
            y = dot(lt[:, :tok], right[:, cols]) + dot(lt[:, tok:], right_x[:, cols])
            y = y.astype(BF16)
            unit = rb * col_blocks + j // 2
            half = pl.ds(pl.multiple_of(lax.rem(j, 2) * 512, 512), 512)
            for q in range(4):
                out[unit, q, :, half] = y[q * 128 : (q + 1) * 128]

        each(2 * col_blocks, step)


GELU_A = 0.7978845608
GELU_B = 0.044715


def xor(a, b):
    bit = lax.rem(a // b, 2)
    return a + b - 2 * b * bit


def greet(partners):
    barrier = pltpu.get_barrier_semaphore()
    for p in partners:
        pl.semaphore_signal(barrier, inc=1, device_id=p, device_id_type=MESH)
    pl.semaphore_wait(barrier, len(partners))


def remote(src, dst, ssem, rsem, dev):
    return pltpu.make_async_remote_copy(
        src_ref=src, dst_ref=dst, send_sem=ssem, recv_sem=rsem, device_id=dev, device_id_type=MESH
    )


def xor_any(a, bits):
    for b in (1, 2, 4, 8, 16):
        if bits & b:
            a = xor(a, b)
    return a


TILE = 1024
SLOTS = 6
AHEAD = 3


def gather_chunks(shapes):
    out = []
    for i, (rows, cols) in enumerate(shapes):
        step = rows
        while step * cols > 128 * 1024 and step % 32 == 0:
            step //= 2
        out += [(i, r, step) for r in range(0, rows, step)]
    return out


def weight_tiles(shapes):
    return [
        (i, r, c)
        for i, (rows, cols) in enumerate(shapes)
        for r in range(0, rows, TILE)
        for c in range(0, cols, TILE)
    ]


def forward_kernel(chunks, tiles, *refs):
    shards = refs[:6]
    (tokens, grad4, added, g1, s1, g2, s2, g3, s3, b_in, b_out, bias) = refs[6:18]
    full = refs[18:24]
    kept = refs[24:38]
    held = refs[38:52]
    (base1, unit1, qkv1, mixed1, base2, unit2, qkv2, mixed2, after2, unit3, slope, g2d, gout, res_out) = held
    (act, wt, base_in, out1, in2, g_in, y_ref, act_x, g_x, lt, ssem, rsem, bsem, tsem, z3s, z3r, z3l,
     f7s, f7r, f7l, turn_s, turn_r, turn_l, x_s, x_r, ksem) = refs[52:]
    f = lax.axis_index("frame")
    t = lax.axis_index("tile")
    core = lax.rem(f, 2)
    odd = lax.rem(t, 2)
    fx, fy = xor(f, 2), xor(f, 4)
    first = fx + (fy - fx) * odd
    second = fy + (fx - fy) * odd
    diag = xor_any(f, 6)
    sib = xor(f, 1)
    to_sib, to_first, to_second, to_z = (sib, t), (first, t), (second, t), (f, xor(t, 1))
    greet([(xor_any(f, a), xor_any(t, b)) for a in range(8) for b in range(4) if a or b])

    saves = [pltpu.make_async_copy(v, h, ksem.at[i]) for i, (v, h) in enumerate(zip(held, kept))]

    def piece(k, owner):
        a, r, n = chunks[k]
        return full[a].at[pl.ds(pl.multiple_of(owner * shards[a].shape[0] + r, 16), n)]

    def own(k):
        a, r, n = chunks[k]
        return shards[a].at[pl.ds(r, n)]

    def copy(k, kind):
        dev = (to_first, to_second, to_z, to_sib, to_sib, to_sib, to_sib)[kind]
        owner = (f, first, first, f, first, diag, second)[kind]
        src = own(k) if kind in (0, 3) else piece(k, owner)
        return remote(src, piece(k, owner), ssem.at[k, kind], rsem.at[k, kind], dev)

    def arrived(k, kind):
        owner = (first, diag, second, sib, xor(first, 1), xor(diag, 1), xor(second, 1))[kind]
        dst = piece(k, owner)
        remote(dst, dst, ssem.at[k, kind], rsem.at[k, kind], to_sib).wait_recv()

    n = len(chunks)

    def hop(k):
        copy(k, 3).start()
        arrived(k, 0)
        if k + AHEAD < n:
            copy(k + AHEAD, 0).start()
        for kind in (1, 2, 4):
            copy(k, kind).start()

    def relay(k):
        for kind in (1, 2):
            arrived(k, kind)
            copy(k, kind + 4).start()

    progress = [0, 0]

    def advance(hops):
        while progress[0] < min(hops, n):
            hop(progress[0])
            progress[0] += 1
            if progress[0] >= 2:
                relay(progress[1])
                progress[1] += 1
        if hops > n and progress[1] < n:
            relay(progress[1])
            progress[1] += 1

    bounce = []
    for a, shard in enumerate(shards):
        for r in range(0, shard.shape[0], 128):
            for c in range(0, shard.shape[1], TILE):
                i = len(bounce)
                bounce.append((a, r, c, wt.at[4 + i // 8, pl.ds(i % 8 * 128, 128)]))

    def bounce_in(i):
        a, r, c, via = bounce[i]
        return pltpu.make_async_copy(shards[a].at[pl.ds(r, 128), pl.ds(c, TILE)], via, bsem.at[i])

    def bounce_out(i):
        a, r, c, via = bounce[i]
        row = pl.multiple_of(f * shards[a].shape[0] + r, 128)
        return pltpu.make_async_copy(via, full[a].at[pl.ds(row, 128), pl.ds(c, TILE)], bsem.at[i])

    def tile_load(i):
        a, r, c = tiles[i]
        src = full[a].at[pl.ds(r, TILE), pl.ds(c, TILE)]
        return pltpu.make_async_copy(src, wt.at[i % SLOTS], tsem.at[i])

    def tile(i):
        return wt.at[i % SLOTS]

    def tiles_of(a):
        return [i for i, x in enumerate(tiles) if x[0] == a]

    def complete(a):
        ks = [k for k in range(n) if chunks[k][0] == a]
        advance(ks[-1] + 2)
        for k in ks:
            for kind in (3, 4, 5, 6):
                arrived(k, kind)

    def load(ids):
        for i in ids:
            tile_load(i).start()

    def ready(ids):
        for i in ids:
            tile_load(i).wait()

    def token_copy(i):
        d = xor_any(t, i)
        return remote(tokens.at[d], base_in.at[pl.ds(pl.multiple_of(t * 64, 64), 64)], z3s.at[i - 1], z3r.at[i - 1], (f, d))

    def token_arrived(i):
        d = xor_any(t, i)
        dst = base_in.at[pl.ds(pl.multiple_of(d * 64, 64), 64)]
        remote(tokens.at[d], dst, z3s.at[i - 1], z3r.at[i - 1], (f, d)).wait()

    own_tokens = pltpu.make_async_copy(tokens.at[t], base_in.at[pl.ds(pl.multiple_of(t * 64, 64), 64)], z3l)
    own_tokens.start()
    for i in (1, 2, 3):
        token_copy(i).start()
    for k in range(AHEAD):
        copy(k, 0).start()
    for i in range(len(bounce)):
        bounce_in(i).start()

    def grad_copy(i, dst_slot):
        d = xor_any(f, i)
        return remote(grad4.at[:, d], g_in.at[pl.ds(4 * dst_slot, 4)], f7s.at[i - 1], f7r.at[i - 1], (d, t))

    own_grad = pltpu.make_async_copy(grad4.at[:, f], g_in.at[pl.ds(4 * f, 4)], f7l)

    advance(1)
    for i in range(len(bounce)):
        bounce_in(i).wait()
        bounce_out(i).start()
    own_tokens.wait()
    for i in (1, 2, 3):
        token_arrived(i)

    def plain(i):
        rows = at(i, ROWS)
        base1[rows, :] = base_in[rows, :]

    each(base1.shape[0] // ROWS, plain)
    norm_rows(lambda rows: base1[rows, :].astype(F32) + added[...], g1, s1, unit1)
    own_grad.start()
    for i in range(1, 8):
        grad_copy(i, f).start()
    for i in range(len(bounce)):
        bounce_out(i).wait()

    def project(unit, ids, out_ref):
        for j, i in enumerate(ids):
            def put(cols, y, j=j):
                start = pl.multiple_of(cols.start + j * TILE, 512)
                out_ref[:, pl.ds(start, 512)] = y.astype(BF16)

            matmul(unit, tile(i), 512, put)

    saves[0].start()
    saves[1].start()
    complete(0)
    load(tiles_of(0))
    ready(tiles_of(0))
    project(unit1, tiles_of(0), qkv1)
    complete(1)
    load(tiles_of(1))
    saves[2].start()
    attention(qkv1, None, mixed1)
    saves[3].start()
    ready(tiles_of(1))

    def put_after1(cols, y):
        y = y + base1[:, cols].astype(F32) + added[:, cols]
        y_ref[:, cols] = y

    matmul(mixed1, tile(tiles_of(1)[0]), 512, put_after1)

    def split(i):
        rows = at(i, ROWS)
        out1[pl.ds(4 * i, 4)] = y_ref[rows, :].reshape(4, 8, TILE).astype(BF16)

    each(y_ref.shape[0] // ROWS, split)

    slot = 4 * f + t
    others = [(a, b) for a in range(8) for b in range(4) if a or b]

    def turn_copy(i, d, dst_slot):
        return remote(out1.at[8 * d[1] + d[0]], in2.at[dst_slot], turn_s.at[i], turn_r.at[i], d)

    own_turn = pltpu.make_async_copy(out1.at[8 * t + f], in2.at[slot], turn_l)
    own_turn.start()
    for i, (a, b) in enumerate(others):
        turn_copy(i, (xor_any(f, a), xor_any(t, b)), slot).start()
    complete(2)
    load(tiles_of(2))
    complete(3)
    load(tiles_of(3))
    own_turn.wait()
    for i, (a, b) in enumerate(others):
        d = (xor_any(f, a), xor_any(t, b))
        turn_copy(i, d, 4 * d[0] + d[1]).wait()

    def join(i):
        base2[at(i, ROWS), :] = in2[pl.ds(4 * i, 4)].astype(F32).reshape(ROWS, TILE).astype(BF16)

    each(base2.shape[0] // ROWS, join)
    norm_rows(lambda rows: base2[rows, :].astype(F32), g2, s2, unit2)
    ready(tiles_of(2))
    project(unit2, tiles_of(2), qkv2)
    advance(12)
    attention(qkv2, bias, mixed2)
    for i in (4, 5, 6, 7):
        saves[i].start()
    advance(14)
    ready(tiles_of(3))

    def put_after2(cols, y):
        after2[:, cols] = y + base2[:, cols].astype(F32)

    matmul(mixed2, tile(tiles_of(3)[0]), 512, put_after2)
    norm_rows(lambda rows: after2[rows, :], g3, s3, unit3)
    complete(4)
    load(tiles_of(4))
    saves[8].start()
    saves[9].start()

    own_grad.wait()
    for i in range(1, 8):
        grad_copy(i, xor_any(f, i)).wait()

    def join_grad(i):
        g2d[at(i, ROWS), :] = g_in[pl.ds(4 * i, 4)].astype(F32).reshape(ROWS, TILE).astype(BF16)

    each(g2d.shape[0] // ROWS, join_grad)

    for j, i in enumerate(tiles_of(4)):
        tile_load(i).wait()

        def put_pre(cols, y, j=j):
            cols = pl.ds(pl.multiple_of(cols.start + j * TILE, 256), 256)
            v = y + b_in[:, cols]
            th = jnp.tanh(GELU_A * (v + GELU_B * v * v * v))
            act[:, cols] = (0.5 * v * (1.0 + th)).astype(BF16)
            rise = 0.5 * (1.0 + th) + 0.5 * v * (1.0 - th * th) * GELU_A * (1.0 + 3.0 * GELU_B * v * v)
            slope[:, cols] = rise.astype(BF16)

        matmul(unit3, tile(i), 256, put_pre)

    saves[10].start()
    saves[11].start()

    shard = shards[5].shape[0]
    swaps = [
        remote(act.at[:, pl.ds(pl.multiple_of((2 * q + 1 - core) * shard, shard), shard)],
               act_x.at[:, pl.ds(q * shard, shard)], x_s.at[q], x_r.at[q], to_sib)
        for q in range(4)
    ]
    swaps.append(remote(g2d, g_x, x_s.at[4], x_r.at[4], to_sib))
    for c in swaps:
        c.start()
    advance(16)
    for c in swaps:
        c.wait()
    wgrad(core, shard, act, act_x, g2d, g_x, gout, lt)
    saves[12].start()
    complete(5)
    ids = tiles_of(5)
    load(ids)
    for j, i in enumerate(ids):
        tile_load(i).wait()

        def part(h, i=i, j=j):
            cols = at(h, 512)
            y = dot(act[:, j * TILE : (j + 1) * TILE], wt[i % SLOTS, :, cols])
            y_ref[:, cols] = y + (after2[:, cols] + b_out[:, cols] if j == 0 else y_ref[:, cols])

        each(2, part)

    def split_res(i):
        res_out[pl.ds(4 * i, 4)] = y_ref[at(i, ROWS), :].reshape(4, 8, TILE).astype(BF16)

    each(y_ref.shape[0] // ROWS, split_res)

    saves[13].start()
    for k in range(n):
        for kind in range(7):
            copy(k, kind).wait_send()
    for c in saves:
        c.wait()


def forward(mats, tokens, grad4, added, vecs, bias):
    width = tokens.shape[2]
    rows = tokens.shape[0] * tokens.shape[1]
    ff = mats[4].shape[1]
    fulls = [(8 * m.shape[0], m.shape[1]) for m in mats]
    chunks = gather_chunks([m.shape for m in mats])
    tiles = weight_tiles(fulls)
    n = len(chunks)
    dma = pltpu.SemaphoreType.DMA
    units = mats[5].shape[0] // 128
    blocks = (32, 8, width)
    held = [
        ((rows, w), d)
        for w, d in (
            (width, BF16), (width, BF16), (3 * width, BF16), (width, BF16),
            (width, BF16), (width, BF16), (3 * width, BF16), (width, BF16),
            (width, F32), (width, BF16), (ff, BF16), (width, BF16),
        )
    ]
    held += [((units, 4, 128, TILE), BF16), (blocks, BF16)]
    outs = [jax.ShapeDtypeStruct(s, BF16) for s in fulls]
    outs += [jax.ShapeDtypeStruct(s, d) for s, d in held]
    return pl.pallas_call(
        functools.partial(forward_kernel, chunks, tiles),
        out_shape=outs,
        in_specs=[HBM_SPEC] * 8 + [VMEM_SPEC] * 10,
        out_specs=[HBM_SPEC] * len(outs),
        scratch_shapes=[pltpu.VMEM(s, d) for s, d in held] + [
            pltpu.VMEM((rows, ff), BF16),
            pltpu.VMEM((SLOTS, TILE, TILE), BF16),
            pltpu.VMEM((rows, width), BF16),
            pltpu.VMEM(blocks, BF16), pltpu.VMEM(blocks, BF16), pltpu.VMEM(blocks, BF16),
            pltpu.VMEM((rows, width), F32),
            pltpu.VMEM((rows, ff // 2), BF16), pltpu.VMEM((rows, width), BF16),
            pltpu.VMEM((512, 2 * rows), BF16),
            dma((n, 7)), dma((n, 7)), dma((16,)), dma((len(tiles),)),
            dma((3,)), dma((3,)), dma, dma((7,)), dma((7,)), dma,
            dma((31,)), dma((31,)), dma, dma((5,)), dma((5,)), dma((14,)),
        ],
        compiler_params=params(collective_id=0, has_side_effects=True),
        name="forward",
    )(*mats, tokens, grad4, added, *vecs, bias)


DEEP = 3
RING = 8
SLOTS_B = 4


def add_into(dst, a, b):
    def step(i):
        r = at(i, 16)
        dst[r, :] = (a[r, :].astype(F32) + b[r, :].astype(F32)).astype(dst.dtype)

    each(dst.shape[0] // 16, step)


def backward_kernel(tiles, units, *refs):
    full = refs[:6]
    (gout_h, res_h, base1_h, unit1_h, qkv1_h, mixed1_h, base2_h, unit2_h, qkv2_h, mixed2_h,
     after2_h, unit3_h, slope_h, g_h) = refs[6:20]
    added, gain1, gain2, gain3, bias, hot = refs[20:26]
    outs = refs[26:32]
    small_out, tokens_grad, result = refs[32:35]
    (base1, unit1, qkv1, mixed1, base2, unit2, qkv2, mixed2, after2, unit3, slope, g2d,
     wt, gbuf, r1, r2, zin, zpeer, dpre_x, unit3_x, mix2_x, low2_x, unit2_x, dqkv2_x,
     mix1_x, low1_x, unit1_x, dqkv1_x, du, dafter, low2, low1, dmix, dqkv, turn_out, turn_in, tg,
     sm, smr, lt, acc, emb,
     lsem, tsem, s1s, s1r, s2s, s2r, zs, zr, zps, zpr, osem, sms, smrs, xs, xr,
     turn_s, turn_r, turn_l, o7s, o7r, o7l, z3s, z3r, z3l) = refs[35:]
    f = lax.axis_index("frame")
    t = lax.axis_index("tile")
    core = lax.rem(f, 2)
    chip = f // 2
    leaf = (t == 0) | (t == 3)
    inner = jnp.logical_not(leaf)
    sib = xor(f, 1)
    cx, cy, cd = xor(chip, 1), xor(chip, 2), xor_any(chip, 3)
    to_sib, to_x, to_y = (sib, t), (xor(f, 2), t), (xor(f, 4), t)
    to_z, to_peer = (f, xor(t, 1)), (f, 3 - t)

    kept = [(g_h, g2d), (slope_h, slope), (gout_h, gbuf.at[0]), (after2_h, after2), (unit3_h, unit3),
            (mixed2_h, mixed2), (qkv2_h, qkv2), (base2_h, base2), (unit2_h, unit2),
            (mixed1_h, mixed1), (qkv1_h, qkv1), (base1_h, base1), (unit1_h, unit1)]
    loads = [pltpu.make_async_copy(h, v, lsem.at[i]) for i, (h, v) in enumerate(kept)]

    def tile_load(i):
        a, r, c = tiles[i]
        src = full[a].at[pl.ds(r, TILE), pl.ds(c, TILE)]
        return pltpu.make_async_copy(src, wt.at[i % SLOTS_B], tsem.at[i])

    for c in loads[:3]:
        c.start()
    for i in range(SLOTS_B):
        tile_load(i).start()
    for c in loads[3:]:
        c.start()
    greet([(xor_any(f, a), xor_any(t, b)) for a in range(8) for b in range(4) if a or b])

    n = len(units)

    def hop(u):
        return (to_x, cx, to_y, cy) if u % 2 == 0 else (to_y, cy, to_x, cx)

    def part(u, p):
        return gbuf.at[u // 4 % 3, u % 4, p]

    def step1(u):
        dev1, p1, dev2, p2 = hop(u)
        k = u % RING
        return (
            remote(part(u, cd), r1.at[k, 1], s1s.at[u, 1], s1r.at[u, 1], dev1),
            remote(part(u, p1), r1.at[k, 0], s1s.at[u, 0], s1r.at[u, 0], dev1),
        )

    def step2(u):
        _, _, dev2, p2 = hop(u)
        return remote(part(u, p2), r2.at[u % RING], s2s.at[u], s2r.at[u], dev2)

    def to_inner(u):
        return remote(part(u, chip), zin.at[u % RING], zs.at[u], zr.at[u], to_z)

    def across(u):
        return remote(part(u, chip), zpeer.at[u % RING], zps.at[u], zpr.at[u], to_peer)

    def emit(u, src):
        a, r, c = units[u]
        return pltpu.make_async_copy(src, outs[a].at[pl.ds(r, 128), pl.ds(c, TILE)], osem.at[u])

    state = {"ready": 0, "issued": 0, "done": 0, "step": 0}

    def issue():
        while state["issued"] < min(state["ready"], state["done"] + DEEP):
            for c in step1(state["issued"]):
                c.start()
            state["issued"] += 1

    def offer(count):
        state["ready"] += count
        issue()

    def reduce_step():
        s = state["step"]
        state["step"] += 1
        u = s
        if u < n:
            assert u < state["issued"]
            p2 = hop(u)[3]
            far, near = step1(u)
            far.wait_recv()
            add_into(part(u, p2), part(u, p2), r1.at[u % RING, 1])
            step2(u).start()
            near.wait_recv()
            add_into(part(u, chip), part(u, chip), r1.at[u % RING, 0])
            state["done"] += 1
            issue()
        u = s - 1
        if 0 <= u < n:
            step2(u).wait_recv()
            add_into(part(u, chip), part(u, chip), r2.at[u % RING])

            @pl.when(leaf)
            def _(u=u):
                to_inner(u).start()

        u = s - 2
        if 0 <= u < n:
            @pl.when(inner)
            def _(u=u):
                to_inner(u).wait_recv()
                add_into(part(u, chip), part(u, chip), zin.at[u % RING])
                across(u).start()

        u = s - 3
        if 0 <= u < n:
            @pl.when(inner)
            def _(u=u):
                across(u).wait()
                add_into(part(u, chip), part(u, chip), zpeer.at[u % RING])
                to_inner(u).start()
                emit(u, part(u, chip)).start()

        u = s - 4
        if 0 <= u < n:
            @pl.when(leaf)
            def _(u=u):
                to_inner(u).wait()
                emit(u, zin.at[u % RING]).start()

        u = s - 5
        if 0 <= u < n:
            for c in step1(u):
                c.wait_send()
            step2(u).wait_send()

            @pl.when(inner)
            def _(u=u):
                to_inner(u).wait_send()

            emit(u, part(u, chip)).wait()

    def reduce_to(s):
        while state["step"] < s:
            reduce_step()

    def share(i, left, left_x, right, right_x):
        shard = left.shape[1] // 8
        copies = [
            remote(left.at[:, pl.ds(pl.multiple_of((2 * p + 1 - core) * shard, shard), shard)],
                   left_x.at[:, pl.ds(p * shard, shard)], xs.at[i, p], xr.at[i, p], to_sib)
            for p in range(4)
        ]
        copies.append(remote(right, right_x, xs.at[i, 4], xr.at[i, 4], to_sib))
        for c in copies:
            c.start()
        return copies

    def shared(copies):
        for c in copies:
            c.wait()

    def res_copy(i, dst):
        d = xor_any(f, i)
        return remote(res_h.at[pl.ds(4 * d, 4)], result.at[:, dst], o7s.at[i - 1], o7r.at[i - 1], (d, t))

    own_res = pltpu.make_async_copy(res_h.at[pl.ds(4 * f, 4)], result.at[:, f], o7l)

    loads[2].wait()
    offer(4)
    loads[0].wait()
    loads[1].wait()

    sm[0] = jnp.zeros_like(sm[0])
    for j in range(4):
        tile_load(j).wait()

        def put_dpre(rows, y, j=j):
            cols = pl.ds(pl.multiple_of(rows.start + j * TILE, 256), 256)
            d = (y * slope[:, cols].astype(F32)).astype(BF16)
            slope[:, cols] = d
            sm[0, 15 + j : 16 + j, rows] = jnp.sum(d.astype(F32), 0, keepdims=True)

        matmul_nt(g2d, wt.at[j], 256, put_dpre)
        tile_load(j + 4).start()
    dpre = slope
    loads[4].wait()
    swap3 = share(0, unit3, unit3_x, dpre, dpre_x)
    reduce_to(1)

    def back_through(first, count, x_ref, after):
        for j in range(count):
            i = first + j
            tile_load(i).wait()

            def put(rows, y, j=j):
                du[:, rows] = y if j == 0 else du[:, rows] + y

            def run(h, i=i, j=j, put=put):
                rows = at(h, 256)
                put(rows, dot_nt(x_ref[:, j * TILE : (j + 1) * TILE], wt[i % SLOTS_B, rows, :]))

            each(TILE // 256, run)
            if i + SLOTS_B < len(tiles):
                tile_load(i + SLOTS_B).start()

    back_through(4, 4, dpre, None)
    loads[3].wait()
    sm[0, 14:15, :] = jnp.zeros((1, TILE), F32)

    def store3(rows, dh):
        g = g2d[rows, :].astype(F32)
        d = g + dh
        dafter[rows, :] = d
        low2[rows, :] = d.astype(BF16)
        sm[0, 14:15, :] += jnp.sum(g, 0, keepdims=True)

    norm_back(lambda rows: after2[rows, :], du, gain3, sm.at[0, pl.ds(12, 1)], sm.at[0, pl.ds(13, 1)], acc, store3)
    loads[5].wait()
    swap2o = share(1, mixed2, mix2_x, low2, low2_x)
    reduce_to(2)
    shared(swap3)
    wgrad(core, unit3.shape[1] // 8, unit3, unit3_x, dpre, dpre_x, gbuf.at[1], lt)
    offer(4)

    def put_mix(rows, y):
        dmix[:, rows] = y.astype(BF16)

    tile_load(8).wait()
    matmul_nt(low2, wt.at[8 % SLOTS_B], 512, put_mix)
    tile_load(12).start()
    loads[6].wait()
    reduce_to(3)
    attention_back(qkv2, bias, dmix, dqkv)
    loads[8].wait()
    swap2 = share(2, unit2, unit2_x, dqkv, dqkv2_x)
    reduce_to(4)
    back_through(9, 3, dqkv, None)
    loads[7].wait()

    def store2(rows, dh):
        d = dafter[rows, :] + dh
        dafter[rows, :] = d

    norm_back(lambda rows: base2[rows, :].astype(F32), du, gain2, sm.at[0, pl.ds(10, 1)], sm.at[0, pl.ds(11, 1)], acc, store2)

    def split(i):
        turn_out[pl.ds(4 * i, 4)] = dafter[at(i, ROWS), :].reshape(4, 8, TILE).astype(BF16)

    each(dafter.shape[0] // ROWS, split)

    slot = 8 * t + f
    others = [(a, b) for a in range(8) for b in range(4) if a or b]

    def turn_copy(i, d, dst_slot):
        return remote(turn_out.at[4 * d[0] + d[1]], turn_in.at[dst_slot], turn_s.at[i], turn_r.at[i], d)

    own_turn = pltpu.make_async_copy(turn_out.at[4 * f + t], turn_in.at[slot], turn_l)
    own_turn.start()
    for i, (a, b) in enumerate(others):
        turn_copy(i, (xor_any(f, a), xor_any(t, b)), slot).start()
    shared(swap2o)
    wgrad(core, TILE // 8, mixed2, mix2_x, low2, low2_x, gbuf.at[2, pl.ds(0, 1)], lt)
    shared(swap2)
    wgrad(core, TILE // 8, unit2, unit2_x, dqkv, dqkv2_x, gbuf.at[2, pl.ds(1, 3)], lt)
    offer(4)
    reduce_to(5)
    own_turn.wait()
    for i, (a, b) in enumerate(others):
        d = (xor_any(f, a), xor_any(t, b))
        turn_copy(i, d, 8 * d[1] + d[0]).wait()

    def join(i):
        low1[at(i, ROWS), :] = turn_in[pl.ds(4 * i, 4)].astype(F32).reshape(ROWS, TILE).astype(BF16)

    each(low1.shape[0] // ROWS, join)
    for c in loads[9:]:
        c.wait()
    swap1o = share(3, mixed1, mix1_x, low1, low1_x)
    tile_load(12).wait()
    matmul_nt(low1, wt.at[12 % SLOTS_B], 512, put_mix)
    reduce_to(6)
    attention_back(qkv1, None, dmix, dqkv)
    swap1 = share(4, unit1, unit1_x, dqkv, dqkv1_x)
    shared(swap1o)
    wgrad(core, TILE // 8, mixed1, mix1_x, low1, low1_x, gbuf.at[0, pl.ds(0, 1)], lt)
    offer(1)
    reduce_to(7)
    back_through(13, 3, dqkv, None)
    reduce_to(9)
    shared(swap1)
    wgrad(core, TILE // 8, unit1, unit1_x, dqkv, dqkv1_x, gbuf.at[0, pl.ds(1, 3)], lt)
    offer(3)
    emb[...] = jnp.zeros_like(emb)

    def store1(rows, dh):
        d = low1[rows, :].astype(F32) + dh
        tg[rows, :] = d.astype(BF16)
        emb[...] += fold(d)

    norm_back(lambda rows: base1[rows, :].astype(F32) + added[...], du, gain1, sm.at[0, pl.ds(8, 1)], sm.at[0, pl.ds(9, 1)], acc, store1)
    sm[0, 0:8, :] = hot[...] * jnp.sum(emb[...], 0, keepdims=True)

    def token_copy(i, d, dst):
        return remote(tg.at[pl.ds(pl.multiple_of(d * 64, 64), 64)], tokens_grad.at[dst], z3s.at[i - 1], z3r.at[i - 1], (f, d))

    own_tokens = pltpu.make_async_copy(tg.at[pl.ds(pl.multiple_of(t * 64, 64), 64)], tokens_grad.at[t], z3l)
    own_tokens.start()
    for i in (1, 2, 3):
        token_copy(i, xor_any(t, i), t).start()

    def small_copy(i, dev):
        return remote(sm.at[i], smr.at[i], sms.at[i], smrs.at[i], dev)

    def small_down():
        return remote(sm.at[5], smr.at[3], sms.at[5], smrs.at[3], to_z)

    hops = (to_sib, to_x, to_y)
    small_copy(0, to_sib).start()
    for i in range(3):
        reduce_to(state["step"] + 1)
        small_copy(i, hops[i]).wait()
        sm[i + 1] = sm[i] + smr[i]
        if i < 2:
            small_copy(i + 1, hops[i + 1]).start()

    @pl.when(leaf)
    def _():
        small_copy(3, to_z).start()

    reduce_to(state["step"] + 1)

    @pl.when(inner)
    def _():
        small_copy(3, to_z).wait_recv()
        sm[4] = sm[3] + smr[3]
        small_copy(4, to_peer).start()

    reduce_to(state["step"] + 1)

    @pl.when(inner)
    def _():
        small_copy(4, to_peer).wait()
        sm[5] = sm[4] + smr[4]
        small_down().start()
        small_out[...] = sm[5]

    own_res.start()
    for i in range(1, 8):
        res_copy(i, f).start()
    reduce_to(n + 5)

    @pl.when(leaf)
    def _():
        small_copy(3, to_z).wait()
        small_out[...] = smr[3]

    @pl.when(inner)
    def _():
        small_down().wait_send()

    own_tokens.wait()
    for i in (1, 2, 3):
        d = xor_any(t, i)
        token_copy(i, d, d).wait()
    own_res.wait()
    for i in range(1, 8):
        res_copy(i, xor_any(f, i)).wait()


def backward(fulls, kept, added, gains, bias, hot, tokens_shape, result_shape):
    width = tokens_shape[2]
    rows = tokens_shape[0] * tokens_shape[1]
    order = (5, 4, 3, 2, 1, 0)
    shapes = [w.shape for w in fulls]
    all_tiles = weight_tiles(shapes)
    tiles = [x for a in order for x in all_tiles if x[0] == a]
    shards = [(s[0] // 8, s[1]) for s in shapes]
    units = [
        (a, r, c) for a in order for r in range(0, shards[a][0], 128) for c in range(0, shards[a][1], TILE)
    ]
    n = len(units)
    ff = shapes[4][1]
    dma = pltpu.SemaphoreType.DMA
    blocks = (32, 8, width)
    unit = (128, TILE)
    bf = lambda *s: pltpu.VMEM(s, BF16)
    fl = lambda *s: pltpu.VMEM(s, F32)
    half, quarter = width // 2, width // 4
    return pl.pallas_call(
        functools.partial(backward_kernel, tiles, units),
        out_shape=[jax.ShapeDtypeStruct(s, BF16) for s in shards] + [
            jax.ShapeDtypeStruct((24, width), F32),
            jax.ShapeDtypeStruct(tokens_shape, BF16),
            jax.ShapeDtypeStruct(result_shape, BF16),
        ],
        in_specs=[HBM_SPEC] * (6 + len(kept)) + [VMEM_SPEC] * 6,
        out_specs=[HBM_SPEC] * 6 + [VMEM_SPEC] + [HBM_SPEC] * 2,
        scratch_shapes=[
            bf(rows, width), bf(rows, width), bf(rows, 3 * width), bf(rows, width),
            bf(rows, width), bf(rows, width), bf(rows, 3 * width), bf(rows, width),
            fl(rows, width), bf(rows, width), bf(rows, ff), bf(rows, width),
            bf(SLOTS_B, TILE, TILE), bf(3, 4, 4, *unit), bf(RING, 2, *unit), bf(RING, *unit),
            bf(RING, *unit), bf(RING, *unit),
            bf(rows, ff), bf(rows, half),
            bf(rows, half), bf(rows, width), bf(rows, half), bf(rows, 3 * width),
            bf(rows, half), bf(rows, width), bf(rows, half), bf(rows, 3 * width),
            fl(rows, width), fl(rows, width), bf(rows, width), bf(rows, width), bf(rows, width),
            bf(rows, 3 * width), bf(*blocks), bf(*blocks), bf(rows, width),
            fl(6, 24, width), fl(5, 24, width), bf(512, 2 * rows), fl(2, 8, width), fl(8, width),
            dma((13,)), dma((len(tiles),)), dma((n, 2)), dma((n, 2)), dma((n,)), dma((n,)),
            dma((n,)), dma((n,)), dma((n,)), dma((n,)), dma((n,)), dma((6,)), dma((6,)), dma((5, 5)), dma((5, 5)),
            dma((31,)), dma((31,)), dma, dma((7,)), dma((7,)), dma, dma((3,)), dma((3,)), dma,
        ],
        compiler_params=params(collective_id=1, has_side_effects=True),
        name="backward",
    )(*fulls, *kept, added, *gains, bias, hot)


def plain_norm(h, gain, shift):
    cen = h - jnp.mean(h, -1, keepdims=True)
    inv = lax.rsqrt(jnp.mean(cen * cen, -1, keepdims=True) + EPS)
    return cen * inv * gain + shift


def attn_fwd_kernel(masked, base_ref, added_ref, gain_ref, shift_ref, wqkv_ref, wo_ref, *rest):
    if masked:
        bias_ref, unit_ref, qkv_ref, mixed_ref, after_ref = rest
    else:
        bias_ref = None
        unit_ref, qkv_ref, mixed_ref, after_ref = rest

    def load(rows):
        return base_ref[rows, :].astype(F32) + added_ref[...]

    norm_rows(load, gain_ref, shift_ref, unit_ref)

    def put_qkv(cols, y):
        qkv_ref[:, cols] = y.astype(BF16)

    matmul(unit_ref, wqkv_ref, 512, put_qkv)
    attention(qkv_ref, bias_ref, mixed_ref)

    def put_after(cols, y):
        y = y + base_ref[:, cols].astype(F32) + added_ref[:, cols]
        after_ref[:, cols] = y.astype(after_ref.dtype)

    matmul(mixed_ref, wo_ref, 512, put_after)


def attn_fwd(base, added, gain, shift, wqkv, wo, bias, out_type, name):
    rows, width = base.shape
    ins = [base, added, gain, shift, wqkv, wo] + ([bias] if bias is not None else [])
    shapes = [(width, BF16), (3 * width, BF16), (width, BF16), (width, out_type)]
    return pl.pallas_call(
        functools.partial(attn_fwd_kernel, bias is not None),
        out_shape=[jax.ShapeDtypeStruct((rows, w), d) for w, d in shapes],
        in_specs=[VMEM_SPEC] * len(ins),
        out_specs=[VMEM_SPEC] * 4,
        compiler_params=params(),
        name=name,
    )(*ins)


def attn_bwd_kernel(masked, base_ref, added_ref, gain_ref, wqkv_ref, wo_ref, dout_ref, qkv_ref, *rest):
    if masked:
        bias_ref, *rest = rest
    else:
        bias_ref = None
    dlow_ref, dqkv_ref, dbase_ref, dgain_ref, dshift_ref, dmix_ref, du_ref, acc_ref = rest

    def cast(i):
        rows = at(i, ROWS)
        dlow_ref[rows, :] = dout_ref[rows, :].astype(BF16)

    each(dlow_ref.shape[0] // ROWS, cast)

    def put_mix(rows, y):
        dmix_ref[:, rows] = y.astype(BF16)

    matmul_nt(dlow_ref, wo_ref, 512, put_mix)
    attention_back(qkv_ref, bias_ref, dmix_ref, dqkv_ref)

    def put_du(rows, y):
        du_ref[:, rows] = y

    matmul_nt(dqkv_ref, wqkv_ref, 256, put_du)

    def load(rows):
        return base_ref[rows, :].astype(F32) + added_ref[...]

    def store(rows, dh):
        dbase_ref[rows, :] = (dout_ref[rows, :].astype(F32) + dh).astype(dbase_ref.dtype)

    norm_back(load, du_ref, gain_ref, dgain_ref, dshift_ref, acc_ref, store)


def attn_bwd(base, added, gain, wqkv, wo, dout, qkv, bias, out_type, name):
    rows, width = base.shape
    ins = [base, added, gain, wqkv, wo, dout, qkv] + ([bias] if bias is not None else [])
    outs = [
        jax.ShapeDtypeStruct((rows, width), BF16),
        jax.ShapeDtypeStruct((rows, 3 * width), BF16),
        jax.ShapeDtypeStruct((rows, width), out_type),
        jax.ShapeDtypeStruct((1, width), F32),
        jax.ShapeDtypeStruct((1, width), F32),
    ]
    return pl.pallas_call(
        functools.partial(attn_bwd_kernel, bias is not None),
        out_shape=outs,
        in_specs=[VMEM_SPEC] * len(ins),
        out_specs=[VMEM_SPEC] * len(outs),
        scratch_shapes=[
            pltpu.VMEM((rows, width), BF16),
            pltpu.VMEM((rows, width), F32),
            pltpu.VMEM((2, 8, width), F32),
        ],
        compiler_params=params(),
        name=name,
    )(*ins)


def ffn_bwd_kernel(g_ref, slope_ref, after_ref, gain_ref, win_ref, wout_ref,
                   dslope_ref, dafter_ref, dgain_ref, dshift_ref, dbin_ref, dbout_ref, du_ref, acc_ref):
    def put_dpre(rows, y):
        d = (y * slope_ref[:, rows].astype(F32)).astype(BF16)
        dslope_ref[:, rows] = d
        dbin_ref[:, rows] = jnp.sum(d.astype(F32), 0, keepdims=True)

    matmul_nt(g_ref, wout_ref, 512, put_dpre)

    def put_du(rows, y):
        du_ref[:, rows] = y

    matmul_nt(dslope_ref, win_ref, 256, put_du)
    dbout_ref[...] = jnp.zeros_like(dbout_ref)

    def store(rows, dh):
        g = g_ref[rows, :].astype(F32)
        dafter_ref[rows, :] = g + dh
        dbout_ref[...] += jnp.sum(g, 0, keepdims=True)

    norm_back(lambda rows: after_ref[rows, :], du_ref, gain_ref, dgain_ref, dshift_ref, acc_ref, store)


def ffn_bwd(g, slope, after, gain, win, wout):
    rows, width = after.shape
    ff = win.shape[1]
    row = lambda n: jax.ShapeDtypeStruct((1, n), F32)
    return pl.pallas_call(
        ffn_bwd_kernel,
        out_shape=[
            jax.ShapeDtypeStruct((rows, ff), BF16),
            jax.ShapeDtypeStruct((rows, width), F32),
            row(width), row(width), row(ff), row(width),
        ],
        in_specs=[VMEM_SPEC] * 6,
        out_specs=[VMEM_SPEC] * 6,
        scratch_shapes=[pltpu.VMEM((rows, width), F32), pltpu.VMEM((2, 8, width), F32)],
        compiler_params=params(),
        name="ffn_backward",
    )(g, slope, after, gain, win, wout)


def per_device(on_boxes, tokens, out_grad, actions, segments, frame_mask, embed,
               ln1_gain, ln1_shift, spatial_qkv, spatial_out,
               ln2_gain, ln2_shift, temporal_qkv, temporal_out,
               ln3_gain, ln3_shift, ffn_in, ffn_in_bias, ffn_out, ffn_out_bias):
    frames_dev, tile_tokens, width = tokens.shape
    n_frame = lax.axis_size("frame")
    n_tile = lax.axis_size("tile")
    f = lax.axis_index("frame")
    t = lax.axis_index("tile")
    frames = frames_dev * n_frame
    place = tile_tokens // n_frame
    rows = frames_dev * tile_tokens
    row = lambda v: v[None, :]

    mats = (spatial_qkv, spatial_out, temporal_qkv, temporal_out, ffn_in, ffn_out)

    grad4 = out_grad.reshape(frames_dev, n_frame, place, width)
    action = lax.dynamic_index_in_dim(actions, t, keepdims=False)
    added = lax.dynamic_slice_in_dim(embed, action, 1, 0)

    blocks = n_frame * n_tile

    def turn(x, forward):
        x = x.reshape(blocks, rows // blocks, width)
        if forward:
            y = x.reshape(n_tile, n_frame, -1, width).transpose(1, 0, 2, 3)
            y = lax.all_to_all(y.reshape(x.shape), ("frame", "tile"), 0, 0, tiled=True)
        else:
            y = lax.all_to_all(x, ("frame", "tile"), 0, 0, tiled=True)
            y = y.reshape(n_frame, n_tile, -1, width).transpose(1, 0, 2, 3)
        return y.reshape(rows, width)

    number = jnp.arange(rows, dtype=jnp.int32)
    of_frame, of_place = number // place, number % place
    seg_row = jnp.repeat(segments, place)
    open_row = jnp.repeat(frame_mask, place)
    allowed = (
        (seg_row[:, None] == seg_row[None, :])
        & (of_place[:, None] == of_place[None, :])
        & (of_frame[None, :] <= of_frame[:, None])
        & ((open_row[None, :] == 1) | (of_frame[None, :] == of_frame[:, None]))
    )
    bias = jnp.where(allowed, 0.0, -1e30).astype(F32)
    nothing = jnp.zeros((1, width), F32)
    vecs = [row(v) for v in (ln1_gain, ln1_shift, ln2_gain, ln2_shift, ln3_gain, ln3_shift, ffn_in_bias, ffn_out_bias)]
    one_hot = (action == jnp.arange(embed.shape[0], dtype=jnp.int32)).astype(F32)[:, None]
    if on_boxes:
        fwd = forward(mats, tokens, grad4, added, vecs, bias)
        fulls, kept = fwd[:6], fwd[6:]
        kept = (kept[12], kept[13], *kept[:12])
        hot = jnp.broadcast_to(one_hot, embed.shape)
        *summed, small, tokens_grad, result = backward(
            fulls, kept, added, (vecs[0], vecs[2], vecs[4]), bias, hot, tokens.shape, grad4.shape)
        summed = [x.astype(F32) for x in summed]
        n_act = embed.shape[0]
        d_embed, lines = small[:n_act], small[n_act:]
        dg1, ds1, dg2, ds2, dg3, ds3, d_bout = (lines[i] for i in range(7))
        d_bin = lines[7 : 7 + ffn_in_bias.shape[0] // width].reshape(-1)
    else:
        w_qs, w_os, w_qt, w_ot, w_in, w_out = (lax.all_gather(m, "frame", axis=0, tiled=True) for m in mats)
        base1 = lax.all_to_all(tokens, "tile", 0, 0, tiled=True).reshape(rows, width)
        g = lax.all_to_all(grad4.transpose(1, 0, 2, 3), "frame", 0, 0, tiled=True).reshape(rows, width)
        unit1, qkv1, mixed1, after1 = attn_fwd(
            base1, added, vecs[0], vecs[1], w_qs, w_os, None, BF16, "spatial_forward")
        base2 = turn(after1, True)
        unit2, qkv2, mixed2, after2 = attn_fwd(
            base2, nothing, vecs[2], vecs[3], w_qt, w_ot, bias, F32, "temporal_forward")
        unit3 = plain_norm(after2, ln3_gain, ln3_shift).astype(BF16)
        pre = jnp.dot(unit3, w_in, preferred_element_type=F32) + ffn_in_bias
        th = jnp.tanh(GELU_A * (pre + GELU_B * pre * pre * pre))
        act = (0.5 * pre * (1.0 + th)).astype(BF16)
        slope = 0.5 * (1.0 + th) + 0.5 * pre * (1.0 - th * th) * GELU_A * (1.0 + 3.0 * GELU_B * pre * pre)
        slope = slope.astype(BF16)
        result = after2 + jnp.dot(act, w_out, preferred_element_type=F32) + ffn_out_bias
        result = result.astype(BF16).reshape(n_frame, frames_dev, place, width)
        result = lax.all_to_all(result, "frame", 0, 0, tiled=True).transpose(1, 0, 2, 3)
        d_pre, d_after2, dg3, ds3, d_bin, d_bout = ffn_bwd(g, slope, after2, vecs[4], w_in, w_out)
        low2, d_qkv2, d_after1, dg2, ds2 = attn_bwd(
            base2, nothing, vecs[2], w_qt, w_ot, d_after2, qkv2, bias, BF16, "temporal_backward")
        d_out1 = turn(d_after1, False)
        low1, d_qkv1, d_start, dg1, ds1 = attn_bwd(
            base1, added, vecs[0], w_qs, w_os, d_out1, qkv1, None, F32, "spatial_backward")
        tokens_grad = d_start.astype(BF16).reshape(n_tile, tile_tokens, width)
        tokens_grad = lax.all_to_all(tokens_grad, "tile", 0, 0, tiled=True)
        d_embed = one_hot * jnp.sum(d_start, 0, keepdims=True)
        pairs = ((unit1, d_qkv1), (mixed1, low1), (unit2, d_qkv2), (mixed2, low2), (unit3, d_pre), (act, g))
        summed = []
        for a, b in pairs:
            part = lax.dot_general(a, b, (((0,), (0,)), ((), ())), preferred_element_type=F32)
            part = lax.psum_scatter(part, "frame", scatter_dimension=0, tiled=True)
            summed.append(lax.psum(part.astype(BF16), "tile").astype(F32))
        d_embed, dg1, ds1, dg2, ds2, dg3, ds3, d_bin, d_bout = lax.psum(
            (d_embed, dg1[0], ds1[0], dg2[0], ds2[0], dg3[0], ds3[0], d_bin[0], d_bout[0]), ("frame", "tile"))

    result = result.reshape(tokens.shape)
    return (result, tokens_grad, d_embed, dg1, ds1, summed[0], summed[1], dg2, ds2, summed[2], summed[3],
            dg3, ds3, summed[4], d_bin, summed[5], d_bout)


def solution(mesh):
    shard = P("frame", "tile", None)
    mat = P("frame", None)
    rep = P()
    in_specs = (shard, shard, P("frame"), rep, rep, rep, rep, rep, mat, mat, rep, rep, mat, mat,
                rep, rep, mat, rep, mat, rep)
    out_specs = (shard, shard, rep, rep, rep, mat, mat, rep, rep, mat, mat, rep, rep, mat, rep, mat, rep)
    on_boxes = mesh.shape["frame"] == 8 and mesh.shape["tile"] == 4
    return jax.shard_map(
        functools.partial(per_device, on_boxes),
        mesh=mesh, in_specs=in_specs, out_specs=out_specs, check_vma=False)
```

time: 543 us -> 374 us (0.69); the launches traced: 534 us -> 374 us
  Pallas kernels: 463 us -> 350 us
  local copies, waits for them, and re-layouts: 59.9 us -> 9.72 us
  other arithmetic: 3.8 us -> 11.5 us
    pallas_call x11 -> x1, Pallas kernels: 293 us -> 193 us  [backward(): pl.pallas_call(functools.partial(backward_kernel, tiles, units), out_shap...]
    dynamic_slice x5 -> x0, local copies, waits for them, and re-layouts: 17.9 us -> none  [wgrad_units(): lax.dynamic_index_in_dim(parts, 1 - core, 2, False).reshape(tok, 4 * shard)]
    unnamed x45 -> x20, local copies, waits for them, and re-layouts: 16.9 us -> 3.2 us
    pallas_call x1, Pallas kernels: 170 us -> 157 us  [forward(): pl.pallas_call(functools.partial(forward_kernel, chunks, tiles), out_shap...]
    convert_element_type x1 -> x7, other arithmetic: 0.62 us -> 9.92 us  [the longest x6 9.27 us: per_device(): summed = [x.astype(F32) for x in summed]]
    transpose x4 -> x0, local copies, waits for them, and re-layouts: 6.11 us -> none  [per_device(): summed[i] = part.transpose(0, 2, 1, 3).reshape(n_row * 128, n_col * 1024)]
    reshape x6 -> x0, local copies, waits for them, and re-layouts: 5.99 us -> none  [the longest x5 5.98 us: wgrad_units(): parts = left.reshape(tok, 4, 2, shard)]
  transfers between devices with their start and end apart: 10 -> 0, of which waited for: 1 -> 0; matrix products, arithmetic and copies ran while one was open for 7% -> 0% of each run, Pallas kernels for 16% -> 0%
where the time goes in v3:
time: 374 us
  Pallas kernels  350 us (94%)
  other arithmetic  11.5 us (3%)
  local copies, waits for them, and re-layouts  9.72 us (3%)
    pallas_call x1, Pallas kernels, backward(): pl.pallas_call(functools.partial(backward_kernel, tiles, units), out_shap...  193 us
    pallas_call x1, Pallas kernels, forward(): pl.pallas_call(functools.partial(forward_kernel, chunks, tiles), out_shap...  157 us
    convert_element_type x6, other arithmetic, per_device(): summed = [x.astype(F32) for x in summed]  9.27 us

profile of v3, /device:TPU:0, one launch (start us, length us, event | category | flops | bytes accessed | tf_op | source)
XLA Modules:
  0.0 374.0 jit_solution(10989445617545388800)
XLA Ops:
  0.7 0.0 copy-start
  0.7 1.2 dynamic_slice.7
  3.9 0.6 compare_convert_fusion
  4.5 0.7 broadcast_compare_fusion
  5.2 0.0 copy-done
  5.2 0.6 constant_dynamic-slice_fusion.refs_8_.refs_20_
  5.8 0.1 broadcast_in_dim.59
  5.9 0.1 eq.70
  6.0 0.7 broadcast_in_dim.58
  6.7 0.1 eq.62
  6.8 0.7 broadcast_in_dim.62.refs_25_
  7.5 0.9 and_select_fusion.refs_17_.refs_24_
  8.3 157.0 %forward.1 = (bf16[1024,3072]{1,0:T(8,128)(2,1)}, bf16[1024,1024]{1,0:T(8,128)(2,1)}, bf16[1024,3072]{1,0:T(8,128)(2,1)}, bf16[1024,1024]{1,0:T(8,128)(2,1)}, bf...) custom-call(bf16[128,3072]{1,0:T(8,128)(2,1)} %refs_0_.1, ...), custom_call_target="tpu_custom_call" | custom-call | tf_op jit(solution)/shard_map/forward/pallas_call | solution.py:556
  165.3 193.1 %backward.1 = (bf16[128,3072]{1,0:T(8,128)(2,1)}, bf16[128,1024]{1,0:T(8,128)(2,1)}, bf16[128,3072]{1,0:T(8,128)(2,1)}, bf16[128,1024]{1,0:T(8,128)(2,1)}, bf16[...) custom-call(bf16[1024,3072]{1,0:T(8,128)(2,1)} %get-tuple-element.46, ...), custom_call_target="tpu_custom_call" | custom-call | tf_op jit(solution)/shard_map/backward/pallas_call | solution.py:982
  358.5 0.0 copy-start.5
  358.5 0.0 copy-start.4
  358.5 1.0 slice_bitcast_fusion
  359.5 0.6 copy.39
  360.1 1.6 fusion.1
  361.7 1.4 slice.36
  363.1 1.8 convert_element_type.27
  364.9 1.8 convert_element_type.29
  366.7 0.0 copy-done.5
  366.7 0.0 copy-start.3
  366.7 1.3 convert_element_type.26
  368.0 0.0 copy-done.4
  368.0 1.3 convert_element_type.28
  369.3 0.0 copy-done.3
  369.3 0.0 copy-start.2
  369.3 0.0 copy-start.1
  369.3 1.5 convert_element_type.30
  370.8 0.0 copy-done.2
  370.8 0.0 copy-start.7
  370.8 0.0 copy-start.6
  370.8 1.6 convert_element_type.31
  372.4 0.0 copy-done.7
  372.4 0.8 copy.42
  373.2 0.0 copy-done.6
  373.2 0.8 copy.43
  374.0 0.0 copy-done.1
  (1 shorter events, 0.0 us)
Async XLA Ops:
  0.7 4.5 %copy-start = (f32[8,1024]{1,0:T(8,128)S(1)}, f32[8,1024]{1,0:T(8,128)}, u32[]{:S(2)}) copy-start(f32[8,1024]{1,0:T(8,128)} %param.25) | copy-start | bytes 98308
  358.5 8.2 %copy-start.5 = (bf16[128,3072]{1,0:T(8,128)(2,1)S(1)}, bf16[128,3072]{1,0:T(8,128)(2,1)}, u32[]{:S(2)}) copy-start(bf16[128,3072]{1,0:T(8,128)(2,1)} %get-tuple-element.69) | copy-start | bytes 2359300
  358.5 9.5 %copy-start.4 = (bf16[128,3072]{1,0:T(8,128)(2,1)S(1)}, bf16[128,3072]{1,0:T(8,128)(2,1)}, u32[]{:S(2)}) copy-start(bf16[128,3072]{1,0:T(8,128)(2,1)} %get-tuple-element.71) | copy-start | bytes 2359300
  366.7 2.6 copy-start.3
  369.3 1.5 copy-start.2
  369.3 4.7 %copy-start.1 = (f32[8,1024]{1,0:T(8,128)S(1)}, f32[8,1024]{1,0:T(8,128)}, u32[]{:S(2)}) copy-start(f32[8,1024]{1,0:T(8,128)} %param.25) | copy-start | bytes 98308
  370.8 1.6 copy-start.7
  370.8 2.4 copy-start.6

commit v4 on v3

v4 whole, which is shorter than its diff:
```python
import functools

import jax
import jax.numpy as jnp
from jax import lax
from jax.experimental import pallas as pl
from jax.experimental.pallas import tpu as pltpu
from jax.sharding import PartitionSpec as P

HD = 64
LANES = 128
EPS = 1e-5
MESH = pl.DeviceIdType.MESH
F32 = jnp.float32
BF16 = jnp.bfloat16
VMEM_SPEC = pl.BlockSpec(memory_space=pltpu.VMEM)
HBM_SPEC = pl.BlockSpec(memory_space=pltpu.HBM)


def params(**kw):
    return pltpu.CompilerParams(vmem_limit_bytes=60 * 1024 * 1024, **kw)


def at(j, size):
    return pl.ds(pl.multiple_of(j * size, size), size)


def each(n, fn):
    def step(i, carry):
        fn(i)
        return carry

    lax.fori_loop(0, n, step, 0)


def dot(a, b):
    return jnp.dot(a, b, preferred_element_type=F32)


def dot_nt(a, b):
    return lax.dot_general(a, b, (((1,), (1,)), ((), ())), preferred_element_type=F32)


def dot_tn(a, b):
    return lax.dot_general(a, b, (((0,), (0,)), ((), ())), preferred_element_type=F32)


def normed(h):
    cen = h - jnp.mean(h, -1, keepdims=True)
    inv = lax.rsqrt(jnp.mean(cen * cen, -1, keepdims=True) + EPS)
    return cen * inv, inv


ROWS = 32


def norm_rows(load, gain_ref, shift_ref, unit_ref):
    def step(i):
        rows = at(i, ROWS)
        xhat, _ = normed(load(rows))
        unit_ref[rows, :] = (xhat * gain_ref[...] + shift_ref[...]).astype(BF16)

    each(unit_ref.shape[0] // ROWS, step)


def fold(x):
    return jnp.sum(x.reshape(x.shape[0] // 8, 8, x.shape[1]), 0)


def norm_back(load, du_ref, gain_ref, dgain_ref, dshift_ref, acc_ref, store):
    acc_ref[...] = jnp.zeros_like(acc_ref)

    def step(i):
        rows = at(i, ROWS)
        xhat, inv = normed(load(rows))
        du = du_ref[rows, :]
        acc_ref[0] += fold(du * xhat)
        acc_ref[1] += fold(du)
        dx = du * gain_ref[...]
        dh = inv * (
            dx - jnp.mean(dx, -1, keepdims=True) - xhat * jnp.mean(dx * xhat, -1, keepdims=True)
        )
        store(rows, dh)

    each(du_ref.shape[0] // ROWS, step)
    dgain_ref[...] = jnp.sum(acc_ref[0], 0, keepdims=True)
    dshift_ref[...] = jnp.sum(acc_ref[1], 0, keepdims=True)


def head_masks():
    lane = lax.broadcasted_iota(jnp.int32, (1, LANES), 1)
    low = jnp.where(lane < HD, 1.0, 0.0)
    return low.astype(BF16), (1.0 - low).astype(BF16)


def head_probs(qm, k, bias_ref):
    s = dot_nt(qm, k) * (HD**-0.5)
    if bias_ref is not None:
        s = s + bias_ref[...]
    e = jnp.exp(s - jnp.max(s, -1, keepdims=True))
    return e * (1.0 / jnp.sum(e, -1, keepdims=True))


def attention(qkv_ref, bias_ref, mixed_ref):
    width = mixed_ref.shape[1]
    per = width // LANES
    masks = head_masks()

    def pair(p):
        q, k, v = (qkv_ref[:, at(p + i * per, LANES)] for i in range(3))
        out = 0.0
        for m in masks:
            out = out + dot(head_probs(q * m, k, bias_ref).astype(BF16), v * m)
        mixed_ref[:, at(p, LANES)] = out.astype(BF16)

    each(per, pair)


def attention_back(qkv_ref, bias_ref, dmix_ref, dqkv_ref):
    width = dmix_ref.shape[1]
    per = width // LANES
    masks = head_masks()
    scale = HD**-0.5

    def pair(p):
        q, k, v = (qkv_ref[:, at(p + i * per, LANES)] for i in range(3))
        dm = dmix_ref[:, at(p, LANES)]
        dq = dk = dv = 0.0
        for m in masks:
            qm = q * m
            dmm = dm * m
            probs = head_probs(qm, k, bias_ref)
            dp = dot_nt(dmm, v)
            ds = probs * (dp - jnp.sum(probs * dp, -1, keepdims=True))
            ds = ds.astype(BF16)
            dq = dq + dot(ds, k * m)
            dk = dk + dot_tn(ds, qm)
            dv = dv + dot_tn(probs.astype(BF16), dmm)
        dqkv_ref[:, at(p, LANES)] = (dq * scale).astype(BF16)
        dqkv_ref[:, at(p + per, LANES)] = (dk * scale).astype(BF16)
        dqkv_ref[:, at(p + 2 * per, LANES)] = dv.astype(BF16)

    each(per, pair)


def matmul(x_ref, w_ref, block, store):
    def step(j):
        cols = at(j, block)
        store(cols, dot(x_ref[...], w_ref[:, cols]))

    each(w_ref.shape[1] // block, step)


def matmul_nt(x_ref, w_ref, block, store):
    def step(j):
        rows = at(j, block)
        store(rows, dot_nt(x_ref[...], w_ref[rows, :]))

    each(w_ref.shape[0] // block, step)


def wgrad(core, shard, left, left_x, right, right_x, out, lt):
    tok = left.shape[0]
    col_blocks = right.shape[1] // TILE
    for rb in range(shard // 128):
        for q in range(4):
            cols = pl.ds(pl.multiple_of((2 * q + core) * shard + rb * 128, 128), 128)
            lt[q * 128 : (q + 1) * 128, :tok] = left[:, cols].T
            cols = pl.ds(q * shard + rb * 128, 128)
            lt[q * 128 : (q + 1) * 128, tok:] = left_x[:, cols].T

        def step(j, rb=rb):
            cols = at(j, 512)
            y = dot(lt[:, :tok], right[:, cols]) + dot(lt[:, tok:], right_x[:, cols])
            y = y.astype(BF16)
            unit = rb * col_blocks + j // 2
            half = pl.ds(pl.multiple_of(lax.rem(j, 2) * 512, 512), 512)
            for q in range(4):
                out[unit, q, :, half] = y[q * 128 : (q + 1) * 128]

        each(2 * col_blocks, step)


GELU_A = 0.7978845608
GELU_B = 0.044715


def xor(a, b):
    bit = lax.rem(a // b, 2)
    return a + b - 2 * b * bit


def greet(partners):
    barrier = pltpu.get_barrier_semaphore()
    for p in partners:
        pl.semaphore_signal(barrier, inc=1, device_id=p, device_id_type=MESH)
    pl.semaphore_wait(barrier, len(partners))


def remote(src, dst, ssem, rsem, dev):
    return pltpu.make_async_remote_copy(
        src_ref=src, dst_ref=dst, send_sem=ssem, recv_sem=rsem, device_id=dev, device_id_type=MESH
    )


def xor_any(a, bits):
    for b in (1, 2, 4, 8, 16):
        if bits & b:
            a = xor(a, b)
    return a


TILE = 1024
SLOTS = 4
AHEAD = 3
DEEP = 3
RING = 6


def gather_chunks(shapes):
    out = []
    for i, (rows, cols) in enumerate(shapes):
        step = rows
        while step * cols > 128 * 1024 and step % 32 == 0:
            step //= 2
        out += [(i, r, step) for r in range(0, rows, step)]
    return out


def weight_tiles(shapes):
    return [
        (i, r, c)
        for i, (rows, cols) in enumerate(shapes)
        for r in range(0, rows, TILE)
        for c in range(0, cols, TILE)
    ]


def add_into(dst, a, b):
    def step(i):
        r = at(i, 16)
        dst[r, :] = (a[r, :].astype(F32) + b[r, :].astype(F32)).astype(dst.dtype)

    each(dst.shape[0] // 16, step)


def layer_kernel(chunks, tiles, units, *refs):
    shards = refs[:6]
    (tokens, grad4, actions, segments, frame_mask, embed,
     gain1, shift1, gain2, shift2, gain3, shift3, b_in, b_out) = refs[6:20]
    full = refs[20:26]
    outs = refs[26:32]
    small_out, tokens_grad, result = refs[32:35]
    (base1, unit1, qkv1, mixed1, base2, unit2, qkv2, mixed2, after2, unit3, slope, g2d, act,
     wt, gbuf, r1, r2, zin, zpeer, act_x, g_x, dpre_x, unit3_x, mix2_x, low2_x, unit2_x, dqkv2_x,
     mix1_x, low1_x, unit1_x, dqkv1_x, du, low2, low1, dmix, dqkv,
     out1, in2, g_in, res_out, turn_out, turn_in, bias, added, sm, smr, lt, acc, emb,
     ssem, rsem, bsem, tsem, z3s, z3r, z3l, f7s, f7r, f7l, turn_s, turn_r, turn_l, back_s, back_r, back_l,
     s1s, s1r, s2s, s2r, zs, zr, zps, zpr, osem, sms, smrs, xs, xr, o7s, o7r, o7l, t3s, t3r, t3l) = refs[35:]
    f = lax.axis_index("frame")
    t = lax.axis_index("tile")
    core = lax.rem(f, 2)
    chip = f // 2
    odd = lax.rem(t, 2)
    leaf = (t == 0) | (t == 3)
    inner = jnp.logical_not(leaf)
    fx, fy, sib = xor(f, 2), xor(f, 4), xor(f, 1)
    first = fx + (fy - fx) * odd
    second = fy + (fx - fy) * odd
    diag = xor_any(f, 6)
    cx, cy, cd = xor(chip, 1), xor(chip, 2), xor_any(chip, 3)
    to_sib, to_first, to_second = (sib, t), (first, t), (second, t)
    to_x, to_y, to_z, to_peer = (fx, t), (fy, t), (f, xor(t, 1)), (f, 3 - t)
    others = [(a, b) for a in range(8) for b in range(4) if a or b]
    greet([(xor_any(f, a), xor_any(t, b)) for a, b in others])

    def piece(k, owner):
        a, r, rows = chunks[k]
        return full[a].at[pl.ds(pl.multiple_of(owner * shards[a].shape[0] + r, 16), rows)]

    def own(k):
        a, r, rows = chunks[k]
        return shards[a].at[pl.ds(r, rows)]

    def copy(k, kind):
        dev = (to_first, to_second, to_z, to_sib, to_sib, to_sib, to_sib)[kind]
        owner = (f, first, first, f, first, diag, second)[kind]
        src = own(k) if kind in (0, 3) else piece(k, owner)
        return remote(src, piece(k, owner), ssem.at[k, kind], rsem.at[k, kind], dev)

    def arrived(k, kind):
        owner = (first, diag, second, sib, xor(first, 1), xor(diag, 1), xor(second, 1))[kind]
        dst = piece(k, owner)
        remote(dst, dst, ssem.at[k, kind], rsem.at[k, kind], to_sib).wait_recv()

    n_chunks = len(chunks)
    progress = [0, 0]

    def relay():
        k = progress[1]
        progress[1] += 1
        for kind in (1, 2):
            arrived(k, kind)
            copy(k, kind + 4).start()

    def advance(hops):
        while progress[0] < min(hops, n_chunks):
            k = progress[0]
            progress[0] += 1
            copy(k, 3).start()
            arrived(k, 0)
            if k + AHEAD < n_chunks:
                copy(k + AHEAD, 0).start()
            for kind in (1, 2, 4):
                copy(k, kind).start()
            if k >= 1:
                relay()
        if hops > n_chunks and progress[1] < n_chunks:
            relay()

    def complete(a):
        ks = [k for k in range(n_chunks) if chunks[k][0] == a]
        advance(ks[-1] + 2)
        for k in ks:
            for kind in (3, 4, 5, 6):
                arrived(k, kind)

    bounce = []
    for a, shard in enumerate(shards):
        for r in range(0, shard.shape[0], 128):
            for c in range(0, shard.shape[1], TILE):
                i = len(bounce)
                bounce.append((a, r, c, wt.at[2 + i // 8, pl.ds(i % 8 * 128, 128)]))

    def bounce_in(i):
        a, r, c, via = bounce[i]
        return pltpu.make_async_copy(shards[a].at[pl.ds(r, 128), pl.ds(c, TILE)], via, bsem.at[i])

    def bounce_out(i):
        a, r, c, via = bounce[i]
        row = pl.multiple_of(f * shards[a].shape[0] + r, 128)
        return pltpu.make_async_copy(via, full[a].at[pl.ds(row, 128), pl.ds(c, TILE)], bsem.at[i])

    def tile_load(i):
        a, r, c = tiles[i]
        src = full[a].at[pl.ds(r, TILE), pl.ds(c, TILE)]
        return pltpu.make_async_copy(src, wt.at[i % SLOTS], tsem.at[i])

    def load(ids):
        for i in ids:
            if i < len(tiles):
                tile_load(i).start()

    n = len(units)

    def hop(u):
        return (to_x, cx, to_y, cy) if u % 2 == 0 else (to_y, cy, to_x, cx)

    def part(u, p):
        return gbuf.at[u // 4 % 3, u % 4, p]

    def step1(u):
        dev1, p1, _, _ = hop(u)
        k = u % RING
        return (
            remote(part(u, cd), r1.at[k, 1], s1s.at[u, 1], s1r.at[u, 1], dev1),
            remote(part(u, p1), r1.at[k, 0], s1s.at[u, 0], s1r.at[u, 0], dev1),
        )

    def step2(u):
        _, _, dev2, p2 = hop(u)
        return remote(part(u, p2), r2.at[u % RING], s2s.at[u], s2r.at[u], dev2)

    def along(u):
        return remote(part(u, chip), zin.at[u % RING], zs.at[u], zr.at[u], to_z)

    def across(u):
        return remote(part(u, chip), zpeer.at[u % RING], zps.at[u], zpr.at[u], to_peer)

    def emit(u, src):
        a, r, c = units[u]
        return pltpu.make_async_copy(src, outs[a].at[pl.ds(r, 128), pl.ds(c, TILE)], osem.at[u])

    state = {"ready": 0, "issued": 0, "done": 0, "step": 0}

    def issue():
        while state["issued"] < min(state["ready"], state["done"] + DEEP):
            for c in step1(state["issued"]):
                c.start()
            state["issued"] += 1

    def offer(count):
        state["ready"] += count
        issue()

    def reduce_step():
        s = state["step"]
        state["step"] += 1
        u = s
        if u < n:
            assert u < state["issued"]
            p2 = hop(u)[3]
            far, near = step1(u)
            far.wait_recv()
            add_into(part(u, p2), part(u, p2), r1.at[u % RING, 1])
            step2(u).start()
            near.wait_recv()
            add_into(part(u, chip), part(u, chip), r1.at[u % RING, 0])
            state["done"] += 1
            issue()
        u = s - 1
        if 0 <= u < n:
            step2(u).wait_recv()
            add_into(part(u, chip), part(u, chip), r2.at[u % RING])

            @pl.when(leaf)
            def _(u=u):
                along(u).start()

        u = s - 2
        if 0 <= u < n:
            @pl.when(inner)
            def _(u=u):
                along(u).wait_recv()
                add_into(part(u, chip), part(u, chip), zin.at[u % RING])
                across(u).start()

        u = s - 3
        if 0 <= u < n:
            @pl.when(inner)
            def _(u=u):
                across(u).wait()
                add_into(part(u, chip), part(u, chip), zpeer.at[u % RING])
                along(u).start()
                emit(u, part(u, chip)).start()

        u = s - 4
        if 0 <= u < n:
            @pl.when(leaf)
            def _(u=u):
                along(u).wait()
                emit(u, zin.at[u % RING]).start()

        u = s - 5
        if 0 <= u < n:
            for c in step1(u):
                c.wait_send()
            step2(u).wait_send()

            @pl.when(inner)
            def _(u=u):
                along(u).wait_send()

            emit(u, part(u, chip)).wait()

    def reduce_to(s):
        while state["step"] < s:
            reduce_step()

    def share(i, left, left_x, right, right_x):
        shard = left.shape[1] // 8
        copies = [
            remote(left.at[:, pl.ds(pl.multiple_of((2 * p + 1 - core) * shard, shard), shard)],
                   left_x.at[:, pl.ds(p * shard, shard)], xs.at[i, p], xr.at[i, p], to_sib)
            for p in range(4)
        ]
        copies.append(remote(right, right_x, xs.at[i, 4], xr.at[i, 4], to_sib))
        for c in copies:
            c.start()
        return copies

    def wait_all(copies):
        for c in copies:
            c.wait()

    def rows_of(ref, i):
        return ref.at[pl.ds(pl.multiple_of(i * 64, 64), 64)]

    def over_tile(src, dst, ssems, rsems, lsem):
        ds = [xor_any(t, i) for i in (1, 2, 3)]
        own = pltpu.make_async_copy(src(t), dst(t), lsem)
        go = [remote(src(d), dst(t), ssems.at[i], rsems.at[i], (f, d)) for i, d in enumerate(ds)]
        end = [remote(src(d), dst(d), ssems.at[i], rsems.at[i], (f, d)) for i, d in enumerate(ds)]
        return [own] + go, [own] + end

    def over_frame(src, dst, ssems, rsems, lsem):
        ds = [xor_any(f, i) for i in range(1, 8)]
        own = pltpu.make_async_copy(src(f), dst(f), lsem)
        go = [remote(src(d), dst(f), ssems.at[i], rsems.at[i], (d, t)) for i, d in enumerate(ds)]
        end = [remote(src(d), dst(d), ssems.at[i], rsems.at[i], (d, t)) for i, d in enumerate(ds)]
        return [own] + go, [own] + end

    def over_both(src, dst, ssems, rsems, lsem):
        ds = [(xor_any(f, a), xor_any(t, b)) for a, b in others]
        own = pltpu.make_async_copy(src(f, t), dst(f, t), lsem)
        go = [remote(src(*d), dst(f, t), ssems.at[i], rsems.at[i], d) for i, d in enumerate(ds)]
        end = [remote(src(*d), dst(*d), ssems.at[i], rsems.at[i], d) for i, d in enumerate(ds)]
        return [own] + go, [own] + end

    def start_all(copies):
        for c in copies:
            c.start()

    def split(load_rows, dst):
        def step(i):
            dst[pl.ds(4 * i, 4)] = load_rows(at(i, ROWS)).reshape(4, 8, TILE).astype(BF16)

        each(dst.shape[0] // 4, step)

    def join(src, dst):
        def step(i):
            dst[at(i, ROWS), :] = src[pl.ds(4 * i, 4)].astype(F32).reshape(ROWS, TILE).astype(BF16)

        each(src.shape[0] // 4, step)

    tok_go, tok_end = over_tile(lambda d: tokens.at[d], lambda d: rows_of(base1, d), z3s, z3r, z3l)
    start_all(tok_go)
    for k in range(AHEAD):
        copy(k, 0).start()
    for i in range(len(bounce)):
        bounce_in(i).start()
    grad_go, grad_end = over_frame(
        lambda d: grad4.at[:, d], lambda d: g_in.at[pl.ds(4 * d, 4)], f7s, f7r, f7l)

    which = jnp.sum(jnp.where(lax.broadcasted_iota(jnp.int32, (1, 4), 1) == t, actions[...], 0), -1, keepdims=True)
    hot = jnp.where(lax.broadcasted_iota(jnp.int32, (8, 1), 0) == which, 1.0, 0.0)
    added[...] = jnp.sum(hot * embed[...], 0, keepdims=True)
    n_frames = segments.shape[1]
    n_rows = bias.shape[0]
    place = n_rows // n_frames

    def column(ref):
        a = lax.broadcasted_iota(jnp.int32, (n_frames, n_frames), 0)
        b = lax.broadcasted_iota(jnp.int32, (n_frames, n_frames), 1)
        return jnp.sum(jnp.where(a == b, ref[...].astype(F32), 0.0), 1, keepdims=True)

    by_row = lax.broadcasted_iota(jnp.int32, (n_rows, n_frames), 0) // place
    by_row = by_row == lax.broadcasted_iota(jnp.int32, (n_rows, n_frames), 1)
    by_col = lax.broadcasted_iota(jnp.int32, (n_frames, n_rows), 1) // place
    by_col = by_col == lax.broadcasted_iota(jnp.int32, (n_frames, n_rows), 0)
    seg_q = jnp.sum(jnp.where(by_row, segments[...].astype(F32), 0.0), 1, keepdims=True)
    seg_k = jnp.sum(jnp.where(by_col, column(segments), 0.0), 0, keepdims=True)
    open_k = jnp.sum(jnp.where(by_col, column(frame_mask), 0.0), 0, keepdims=True)
    row_q = lax.broadcasted_iota(jnp.int32, (n_rows, n_rows), 0)
    row_k = lax.broadcasted_iota(jnp.int32, (n_rows, n_rows), 1)
    allowed = (
        (seg_q == seg_k)
        & (lax.rem(row_q, place) == lax.rem(row_k, place))
        & (row_k // place <= row_q // place)
        & ((open_k == 1.0) | (row_k == row_q))
    )
    bias[...] = jnp.where(allowed, 0.0, -1e30)

    advance(1)
    for i in range(len(bounce)):
        bounce_in(i).wait()
        bounce_out(i).start()
    wait_all(tok_end)
    norm_rows(lambda rows: base1[rows, :].astype(F32) + added[...], gain1, shift1, unit1)
    start_all(grad_go)
    for i in range(len(bounce)):
        bounce_out(i).wait()

    def project(unit, ids, out_ref):
        for j, i in enumerate(ids):
            tile_load(i).wait()

            def put(cols, y, j=j):
                start = pl.multiple_of(cols.start + j * TILE, 512)
                out_ref[:, pl.ds(start, 512)] = y.astype(BF16)

            matmul(unit, wt.at[i % SLOTS], 512, put)

    complete(0)
    load((0, 1, 2))
    project(unit1, (0, 1, 2), qkv1)
    complete(1)
    load((3,))
    attention(qkv1, None, mixed1)
    tile_load(3).wait()

    def put_after1(cols, y):
        du[:, cols] = y + base1[:, cols].astype(F32) + added[:, cols]

    matmul(mixed1, wt.at[3], 512, put_after1)
    split(lambda rows: du[rows, :], out1)

    turn_go, turn_end = over_both(
        lambda a, b: out1.at[8 * b + a], lambda a, b: in2.at[4 * a + b], turn_s, turn_r, turn_l)
    start_all(turn_go)
    complete(2)
    load((4, 5, 6))
    complete(3)
    load((7,))
    wait_all(turn_end)
    join(in2, base2)
    norm_rows(lambda rows: base2[rows, :].astype(F32), gain2, shift2, unit2)
    project(unit2, (4, 5, 6), qkv2)
    advance(12)
    attention(qkv2, bias, mixed2)
    advance(14)
    tile_load(7).wait()

    def put_after2(cols, y):
        after2[:, cols] = y + base2[:, cols].astype(F32)

    matmul(mixed2, wt.at[3], 512, put_after2)
    norm_rows(lambda rows: after2[rows, :], gain3, shift3, unit3)
    complete(4)
    load((8, 9, 10, 11))
    wait_all(grad_end)
    join(g_in, g2d)

    for j in range(4):
        tile_load(8 + j).wait()

        def put_pre(cols, y, j=j):
            cols = pl.ds(pl.multiple_of(cols.start + j * TILE, 256), 256)
            v = y + b_in[:, cols]
            th = jnp.tanh(GELU_A * (v + GELU_B * v * v * v))
            act[:, cols] = (0.5 * v * (1.0 + th)).astype(BF16)
            rise = 0.5 * (1.0 + th) + 0.5 * v * (1.0 - th * th) * GELU_A * (1.0 + 3.0 * GELU_B * v * v)
            slope[:, cols] = rise.astype(BF16)

        matmul(unit3, wt.at[j], 256, put_pre)

    swap4 = share(0, act, act_x, g2d, g_x)
    advance(16)
    wait_all(swap4)
    wgrad(core, act.shape[1] // 8, act, act_x, g2d, g_x, gbuf.at[0], lt)
    complete(5)
    load((12, 13, 14, 15))
    offer(4)

    sm[0] = jnp.zeros_like(sm[0])
    for j in range(4):
        tile_load(12 + j).wait()

        def put_dpre(rows, y, j=j):
            cols = pl.ds(pl.multiple_of(rows.start + j * TILE, 256), 256)
            d = (y * slope[:, cols].astype(F32)).astype(BF16)
            slope[:, cols] = d
            sm[0, 15 + j : 16 + j, rows] = jnp.sum(d.astype(F32), 0, keepdims=True)

        matmul_nt(g2d, wt.at[j], 256, put_dpre)

        def add_up(h, j=j):
            cols = at(h, 512)
            y = dot(act[:, j * TILE : (j + 1) * TILE], wt[j, :, cols])
            du[:, cols] = y + (after2[:, cols] + b_out[:, cols] if j == 0 else du[:, cols])

        each(2, add_up)
        load((16 + j,))
    dpre = slope
    swap3 = share(1, unit3, unit3_x, dpre, dpre_x)
    split(lambda rows: du[rows, :], res_out)
    res_go, res_end = over_frame(
        lambda d: res_out.at[pl.ds(4 * d, 4)], lambda d: result.at[:, d], o7s, o7r, o7l)
    reduce_to(1)

    def back_through(first_tile, count, x_ref):
        for j in range(count):
            i = first_tile + j
            tile_load(i).wait()

            def run(h, i=i, j=j):
                rows = at(h, 256)
                y = dot_nt(x_ref[:, j * TILE : (j + 1) * TILE], wt[i % SLOTS, rows, :])
                du[:, rows] = y if j == 0 else du[:, rows] + y

            each(TILE // 256, run)
            load((i + SLOTS,))

    back_through(16, 4, dpre)

    def store3(rows, dh):
        g = g2d[rows, :].astype(F32)
        d = g + dh
        after2[rows, :] = d
        low2[rows, :] = d.astype(BF16)
        sm[0, 14:15, :] += jnp.sum(g, 0, keepdims=True)

    norm_back(lambda rows: after2[rows, :], du, gain3, sm.at[0, pl.ds(12, 1)], sm.at[0, pl.ds(13, 1)], acc, store3)
    dafter = after2
    swap2o = share(2, mixed2, mix2_x, low2, low2_x)
    reduce_to(2)
    wait_all(swap3)
    wgrad(core, TILE // 8, unit3, unit3_x, dpre, dpre_x, gbuf.at[1], lt)
    offer(4)

    def put_mix(rows, y):
        dmix[:, rows] = y.astype(BF16)

    tile_load(20).wait()
    matmul_nt(low2, wt.at[0], 512, put_mix)
    load((24,))
    reduce_to(3)
    attention_back(qkv2, bias, dmix, dqkv)
    swap2 = share(3, unit2, unit2_x, dqkv, dqkv2_x)
    reduce_to(4)
    back_through(21, 3, dqkv)

    def store2(rows, dh):
        dafter[rows, :] = dafter[rows, :] + dh

    norm_back(lambda rows: base2[rows, :].astype(F32), du, gain2, sm.at[0, pl.ds(10, 1)], sm.at[0, pl.ds(11, 1)], acc, store2)
    split(lambda rows: dafter[rows, :], turn_out)

    back_go, back_end = over_both(
        lambda a, b: turn_out.at[4 * a + b], lambda a, b: turn_in.at[8 * b + a], back_s, back_r, back_l)
    start_all(back_go)
    wait_all(swap2o)
    wgrad(core, TILE // 8, mixed2, mix2_x, low2, low2_x, gbuf.at[2, pl.ds(0, 1)], lt)
    wait_all(swap2)
    wgrad(core, TILE // 8, unit2, unit2_x, dqkv, dqkv2_x, gbuf.at[2, pl.ds(1, 3)], lt)
    offer(4)
    reduce_to(5)
    wait_all(back_end)
    join(turn_in, low1)
    swap1o = share(4, mixed1, mix1_x, low1, low1_x)
    tile_load(24).wait()
    matmul_nt(low1, wt.at[0], 512, put_mix)
    reduce_to(6)
    attention_back(qkv1, None, dmix, dqkv)
    swap1 = share(5, unit1, unit1_x, dqkv, dqkv1_x)
    wait_all(swap1o)
    wgrad(core, TILE // 8, mixed1, mix1_x, low1, low1_x, gbuf.at[0, pl.ds(0, 1)], lt)
    offer(1)
    reduce_to(7)
    back_through(25, 3, dqkv)
    reduce_to(9)
    wait_all(swap1)
    wgrad(core, TILE // 8, unit1, unit1_x, dqkv, dqkv1_x, gbuf.at[0, pl.ds(1, 3)], lt)
    offer(3)
    emb[...] = jnp.zeros_like(emb)

    def store1(rows, dh):
        d = low1[rows, :].astype(F32) + dh
        low2[rows, :] = d.astype(BF16)
        emb[...] += fold(d)

    norm_back(lambda rows: base1[rows, :].astype(F32) + added[...], du, gain1, sm.at[0, pl.ds(8, 1)], sm.at[0, pl.ds(9, 1)], acc, store1)
    sm[0, 0:8, :] = hot * jnp.sum(emb[...], 0, keepdims=True)

    last_go, last_end = over_tile(lambda d: rows_of(low2, d), lambda d: tokens_grad.at[d], t3s, t3r, t3l)
    start_all(last_go)

    def small_copy(i, dev):
        return remote(sm.at[i], smr.at[i], sms.at[i], smrs.at[i], dev)

    def small_down():
        return remote(sm.at[5], smr.at[3], sms.at[5], smrs.at[3], to_z)

    hops = (to_sib, to_x, to_y)
    small_copy(0, to_sib).start()
    for i in range(3):
        reduce_to(state["step"] + 1)
        small_copy(i, hops[i]).wait()
        sm[i + 1] = sm[i] + smr[i]
        if i < 2:
            small_copy(i + 1, hops[i + 1]).start()

    @pl.when(leaf)
    def _():
        small_copy(3, to_z).start()

    reduce_to(state["step"] + 1)

    @pl.when(inner)
    def _():
        small_copy(3, to_z).wait_recv()
        sm[4] = sm[3] + smr[3]
        small_copy(4, to_peer).start()

    start_all(res_go)
    reduce_to(state["step"] + 1)

    @pl.when(inner)
    def _():
        small_copy(4, to_peer).wait()
        sm[5] = sm[4] + smr[4]
        small_down().start()
        small_out[...] = sm[5]

    reduce_to(n + 5)

    @pl.when(leaf)
    def _():
        small_copy(3, to_z).wait()
        small_out[...] = smr[3]

    @pl.when(inner)
    def _():
        small_down().wait_send()

    wait_all(last_end)
    wait_all(res_end)
    for k in range(n_chunks):
        for kind in range(7):
            copy(k, kind).wait_send()


def layer(mats, tokens, grad4, actions, segments, frame_mask, embed, vecs):
    width = tokens.shape[2]
    rows = tokens.shape[0] * tokens.shape[1]
    ff = mats[4].shape[1]
    fulls = [(8 * m.shape[0], m.shape[1]) for m in mats]
    chunks = gather_chunks([m.shape for m in mats])
    by_mat = weight_tiles(fulls)
    order = (5, 4, 3, 2, 1, 0)
    tiles = by_mat + [x for a in order[1:] for x in by_mat if x[0] == a]
    units = [
        (a, r, c) for a in order
        for r in range(0, mats[a].shape[0], 128) for c in range(0, mats[a].shape[1], TILE)
    ]
    n = len(units)
    n_chunks = len(chunks)
    dma = pltpu.SemaphoreType.DMA
    blocks = (32, 8, width)
    unit = (128, TILE)
    bf = lambda *s: pltpu.VMEM(s, BF16)
    fl = lambda *s: pltpu.VMEM(s, F32)
    half = width // 2
    scratch = [
        bf(rows, width), bf(rows, width), bf(rows, 3 * width), bf(rows, width),
        bf(rows, width), bf(rows, width), bf(rows, 3 * width), bf(rows, width),
        fl(rows, width), bf(rows, width), bf(rows, ff), bf(rows, width), bf(rows, ff),
        bf(SLOTS, TILE, TILE), bf(3, 4, 4, *unit), bf(RING, 2, *unit), bf(RING, *unit),
        bf(RING, *unit), bf(RING, *unit),
        bf(rows, ff // 2), bf(rows, width), bf(rows, ff), bf(rows, half),
        bf(rows, half), bf(rows, width), bf(rows, half), bf(rows, 3 * width),
        bf(rows, half), bf(rows, width), bf(rows, half), bf(rows, 3 * width),
        fl(rows, width), bf(rows, width), bf(rows, width), bf(rows, width), bf(rows, 3 * width),
        bf(*blocks), bf(*blocks), bf(*blocks), bf(*blocks), bf(*blocks), bf(*blocks),
        fl(rows, rows), fl(1, width),
        fl(6, 24, width), fl(5, 24, width), bf(512, 2 * rows), fl(2, 8, width), fl(8, width),
    ]
    sems = [
        (n_chunks, 7), (n_chunks, 7), (16,), (len(tiles),), (3,), (3,), (), (7,), (7,), (),
        (31,), (31,), (), (31,), (31,), (),
        (n, 2), (n, 2), (n,), (n,), (n,), (n,), (n,), (n,), (n,), (6,), (6,), (6, 5), (6, 5),
        (7,), (7,), (), (3,), (3,), (),
    ]
    return pl.pallas_call(
        functools.partial(layer_kernel, chunks, tiles, units),
        out_shape=[jax.ShapeDtypeStruct(s, BF16) for s in fulls]
        + [jax.ShapeDtypeStruct(m.shape, BF16) for m in mats]
        + [
            jax.ShapeDtypeStruct((24, width), F32),
            jax.ShapeDtypeStruct(tokens.shape, BF16),
            jax.ShapeDtypeStruct(grad4.shape, BF16),
        ],
        in_specs=[HBM_SPEC] * 8 + [VMEM_SPEC] * (4 + len(vecs)),
        out_specs=[HBM_SPEC] * 12 + [VMEM_SPEC] + [HBM_SPEC] * 2,
        scratch_shapes=scratch + [dma(s) if s else dma for s in sems],
        compiler_params=params(collective_id=0, has_side_effects=True),
        name="layer",
    )(*mats, tokens, grad4, actions, segments, frame_mask, embed, *vecs)


def plain_norm(h, gain, shift):
    cen = h - jnp.mean(h, -1, keepdims=True)
    inv = lax.rsqrt(jnp.mean(cen * cen, -1, keepdims=True) + EPS)
    return cen * inv * gain + shift


def attn_fwd_kernel(masked, base_ref, added_ref, gain_ref, shift_ref, wqkv_ref, wo_ref, *rest):
    if masked:
        bias_ref, unit_ref, qkv_ref, mixed_ref, after_ref = rest
    else:
        bias_ref = None
        unit_ref, qkv_ref, mixed_ref, after_ref = rest

    def load(rows):
        return base_ref[rows, :].astype(F32) + added_ref[...]

    norm_rows(load, gain_ref, shift_ref, unit_ref)

    def put_qkv(cols, y):
        qkv_ref[:, cols] = y.astype(BF16)

    matmul(unit_ref, wqkv_ref, 512, put_qkv)
    attention(qkv_ref, bias_ref, mixed_ref)

    def put_after(cols, y):
        y = y + base_ref[:, cols].astype(F32) + added_ref[:, cols]
        after_ref[:, cols] = y.astype(after_ref.dtype)

    matmul(mixed_ref, wo_ref, 512, put_after)


def attn_fwd(base, added, gain, shift, wqkv, wo, bias, out_type, name):
    rows, width = base.shape
    ins = [base, added, gain, shift, wqkv, wo] + ([bias] if bias is not None else [])
    shapes = [(width, BF16), (3 * width, BF16), (width, BF16), (width, out_type)]
    return pl.pallas_call(
        functools.partial(attn_fwd_kernel, bias is not None),
        out_shape=[jax.ShapeDtypeStruct((rows, w), d) for w, d in shapes],
        in_specs=[VMEM_SPEC] * len(ins),
        out_specs=[VMEM_SPEC] * 4,
        compiler_params=params(),
        name=name,
    )(*ins)


def attn_bwd_kernel(masked, base_ref, added_ref, gain_ref, wqkv_ref, wo_ref, dout_ref, qkv_ref, *rest):
    if masked:
        bias_ref, *rest = rest
    else:
        bias_ref = None
    dlow_ref, dqkv_ref, dbase_ref, dgain_ref, dshift_ref, dmix_ref, du_ref, acc_ref = rest

    def cast(i):
        rows = at(i, ROWS)
        dlow_ref[rows, :] = dout_ref[rows, :].astype(BF16)

    each(dlow_ref.shape[0] // ROWS, cast)

    def put_mix(rows, y):
        dmix_ref[:, rows] = y.astype(BF16)

    matmul_nt(dlow_ref, wo_ref, 512, put_mix)
    attention_back(qkv_ref, bias_ref, dmix_ref, dqkv_ref)

    def put_du(rows, y):
        du_ref[:, rows] = y

    matmul_nt(dqkv_ref, wqkv_ref, 256, put_du)

    def load(rows):
        return base_ref[rows, :].astype(F32) + added_ref[...]

    def store(rows, dh):
        dbase_ref[rows, :] = (dout_ref[rows, :].astype(F32) + dh).astype(dbase_ref.dtype)

    norm_back(load, du_ref, gain_ref, dgain_ref, dshift_ref, acc_ref, store)


def attn_bwd(base, added, gain, wqkv, wo, dout, qkv, bias, out_type, name):
    rows, width = base.shape
    ins = [base, added, gain, wqkv, wo, dout, qkv] + ([bias] if bias is not None else [])
    outs = [
        jax.ShapeDtypeStruct((rows, width), BF16),
        jax.ShapeDtypeStruct((rows, 3 * width), BF16),
        jax.ShapeDtypeStruct((rows, width), out_type),
        jax.ShapeDtypeStruct((1, width), F32),
        jax.ShapeDtypeStruct((1, width), F32),
    ]
    return pl.pallas_call(
        functools.partial(attn_bwd_kernel, bias is not None),
        out_shape=outs,
        in_specs=[VMEM_SPEC] * len(ins),
        out_specs=[VMEM_SPEC] * len(outs),
        scratch_shapes=[
            pltpu.VMEM((rows, width), BF16),
            pltpu.VMEM((rows, width), F32),
            pltpu.VMEM((2, 8, width), F32),
        ],
        compiler_params=params(),
        name=name,
    )(*ins)


def ffn_bwd_kernel(g_ref, slope_ref, after_ref, gain_ref, win_ref, wout_ref,
                   dslope_ref, dafter_ref, dgain_ref, dshift_ref, dbin_ref, dbout_ref, du_ref, acc_ref):
    def put_dpre(rows, y):
        d = (y * slope_ref[:, rows].astype(F32)).astype(BF16)
        dslope_ref[:, rows] = d
        dbin_ref[:, rows] = jnp.sum(d.astype(F32), 0, keepdims=True)

    matmul_nt(g_ref, wout_ref, 512, put_dpre)

    def put_du(rows, y):
        du_ref[:, rows] = y

    matmul_nt(dslope_ref, win_ref, 256, put_du)
    dbout_ref[...] = jnp.zeros_like(dbout_ref)

    def store(rows, dh):
        g = g_ref[rows, :].astype(F32)
        dafter_ref[rows, :] = g + dh
        dbout_ref[...] += jnp.sum(g, 0, keepdims=True)

    norm_back(lambda rows: after_ref[rows, :], du_ref, gain_ref, dgain_ref, dshift_ref, acc_ref, store)


def ffn_bwd(g, slope, after, gain, win, wout):
    rows, width = after.shape
    ff = win.shape[1]
    row = lambda n: jax.ShapeDtypeStruct((1, n), F32)
    return pl.pallas_call(
        ffn_bwd_kernel,
        out_shape=[
            jax.ShapeDtypeStruct((rows, ff), BF16),
            jax.ShapeDtypeStruct((rows, width), F32),
            row(width), row(width), row(ff), row(width),
        ],
        in_specs=[VMEM_SPEC] * 6,
        out_specs=[VMEM_SPEC] * 6,
        scratch_shapes=[pltpu.VMEM((rows, width), F32), pltpu.VMEM((2, 8, width), F32)],
        compiler_params=params(),
        name="ffn_backward",
    )(g, slope, after, gain, win, wout)


def per_device(on_boxes, tokens, out_grad, actions, segments, frame_mask, embed,
               ln1_gain, ln1_shift, spatial_qkv, spatial_out,
               ln2_gain, ln2_shift, temporal_qkv, temporal_out,
               ln3_gain, ln3_shift, ffn_in, ffn_in_bias, ffn_out, ffn_out_bias):
    frames_dev, tile_tokens, width = tokens.shape
    n_frame = lax.axis_size("frame")
    n_tile = lax.axis_size("tile")
    f = lax.axis_index("frame")
    t = lax.axis_index("tile")
    frames = frames_dev * n_frame
    place = tile_tokens // n_frame
    rows = frames_dev * tile_tokens
    row = lambda v: v[None, :]

    mats = (spatial_qkv, spatial_out, temporal_qkv, temporal_out, ffn_in, ffn_out)

    grad4 = out_grad.reshape(frames_dev, n_frame, place, width)
    blocks = n_frame * n_tile

    def turn(x, forward):
        x = x.reshape(blocks, rows // blocks, width)
        if forward:
            y = x.reshape(n_tile, n_frame, -1, width).transpose(1, 0, 2, 3)
            y = lax.all_to_all(y.reshape(x.shape), ("frame", "tile"), 0, 0, tiled=True)
        else:
            y = lax.all_to_all(x, ("frame", "tile"), 0, 0, tiled=True)
            y = y.reshape(n_frame, n_tile, -1, width).transpose(1, 0, 2, 3)
        return y.reshape(rows, width)

    vecs = [row(v) for v in (ln1_gain, ln1_shift, ln2_gain, ln2_shift, ln3_gain, ln3_shift, ffn_in_bias, ffn_out_bias)]
    if on_boxes:
        *rest, small, tokens_grad, result = layer(
            mats, tokens, grad4, row(actions), row(segments), row(frame_mask), embed, vecs)
        summed = rest[6:]
        summed = [x.astype(F32) for x in summed]
        n_act = embed.shape[0]
        d_embed, lines = small[:n_act], small[n_act:]
        dg1, ds1, dg2, ds2, dg3, ds3, d_bout = (lines[i] for i in range(7))
        d_bin = lines[7 : 7 + ffn_in_bias.shape[0] // width].reshape(-1)
    else:
        action = lax.dynamic_index_in_dim(actions, t, keepdims=False)
        added = lax.dynamic_slice_in_dim(embed, action, 1, 0)
        one_hot = (action == jnp.arange(embed.shape[0], dtype=jnp.int32)).astype(F32)[:, None]
        number = jnp.arange(rows, dtype=jnp.int32)
        of_frame, of_place = number // place, number % place
        seg_row = jnp.repeat(segments, place)
        open_row = jnp.repeat(frame_mask, place)
        allowed = (
            (seg_row[:, None] == seg_row[None, :])
            & (of_place[:, None] == of_place[None, :])
            & (of_frame[None, :] <= of_frame[:, None])
            & ((open_row[None, :] == 1) | (of_frame[None, :] == of_frame[:, None]))
        )
        bias = jnp.where(allowed, 0.0, -1e30).astype(F32)
        nothing = jnp.zeros((1, width), F32)
        w_qs, w_os, w_qt, w_ot, w_in, w_out = (lax.all_gather(m, "frame", axis=0, tiled=True) for m in mats)
        base1 = lax.all_to_all(tokens, "tile", 0, 0, tiled=True).reshape(rows, width)
        g = lax.all_to_all(grad4.transpose(1, 0, 2, 3), "frame", 0, 0, tiled=True).reshape(rows, width)
        unit1, qkv1, mixed1, after1 = attn_fwd(
            base1, added, vecs[0], vecs[1], w_qs, w_os, None, BF16, "spatial_forward")
        base2 = turn(after1, True)
        unit2, qkv2, mixed2, after2 = attn_fwd(
            base2, nothing, vecs[2], vecs[3], w_qt, w_ot, bias, F32, "temporal_forward")
        unit3 = plain_norm(after2, ln3_gain, ln3_shift).astype(BF16)
        pre = jnp.dot(unit3, w_in, preferred_element_type=F32) + ffn_in_bias
        th = jnp.tanh(GELU_A * (pre + GELU_B * pre * pre * pre))
        act = (0.5 * pre * (1.0 + th)).astype(BF16)
        slope = 0.5 * (1.0 + th) + 0.5 * pre * (1.0 - th * th) * GELU_A * (1.0 + 3.0 * GELU_B * pre * pre)
        slope = slope.astype(BF16)
        result = after2 + jnp.dot(act, w_out, preferred_element_type=F32) + ffn_out_bias
        result = result.astype(BF16).reshape(n_frame, frames_dev, place, width)
        result = lax.all_to_all(result, "frame", 0, 0, tiled=True).transpose(1, 0, 2, 3)
        d_pre, d_after2, dg3, ds3, d_bin, d_bout = ffn_bwd(g, slope, after2, vecs[4], w_in, w_out)
        low2, d_qkv2, d_after1, dg2, ds2 = attn_bwd(
            base2, nothing, vecs[2], w_qt, w_ot, d_after2, qkv2, bias, BF16, "temporal_backward")
        d_out1 = turn(d_after1, False)
        low1, d_qkv1, d_start, dg1, ds1 = attn_bwd(
            base1, added, vecs[0], w_qs, w_os, d_out1, qkv1, None, F32, "spatial_backward")
        tokens_grad = d_start.astype(BF16).reshape(n_tile, tile_tokens, width)
        tokens_grad = lax.all_to_all(tokens_grad, "tile", 0, 0, tiled=True)
        d_embed = one_hot * jnp.sum(d_start, 0, keepdims=True)
        pairs = ((unit1, d_qkv1), (mixed1, low1), (unit2, d_qkv2), (mixed2, low2), (unit3, d_pre), (act, g))
        summed = []
        for a, b in pairs:
            part = lax.dot_general(a, b, (((0,), (0,)), ((), ())), preferred_element_type=F32)
            part = lax.psum_scatter(part, "frame", scatter_dimension=0, tiled=True)
            summed.append(lax.psum(part.astype(BF16), "tile").astype(F32))
        d_embed, dg1, ds1, dg2, ds2, dg3, ds3, d_bin, d_bout = lax.psum(
            (d_embed, dg1[0], ds1[0], dg2[0], ds2[0], dg3[0], ds3[0], d_bin[0], d_bout[0]), ("frame", "tile"))

    result = result.reshape(tokens.shape)
    return (result, tokens_grad, d_embed, dg1, ds1, summed[0], summed[1], dg2, ds2, summed[2], summed[3],
            dg3, ds3, summed[4], d_bin, summed[5], d_bout)


def solution(mesh):
    shard = P("frame", "tile", None)
    mat = P("frame", None)
    rep = P()
    in_specs = (shard, shard, P("frame"), rep, rep, rep, rep, rep, mat, mat, rep, rep, mat, mat,
                rep, rep, mat, rep, mat, rep)
    out_specs = (shard, shard, rep, rep, rep, mat, mat, rep, rep, mat, mat, rep, rep, mat, rep, mat, rep)
    on_boxes = mesh.shape["frame"] == 8 and mesh.shape["tile"] == 4
    return jax.shard_map(
        functools.partial(per_device, on_boxes),
        mesh=mesh, in_specs=in_specs, out_specs=out_specs, check_vma=False)
```

time: 374 us -> 354 us (0.947)
  Pallas kernels: 350 us -> 337 us
    pallas_call x2 -> x1, Pallas kernels: 350 us -> 337 us  [layer(): pl.pallas_call(functools.partial(layer_kernel, chunks, tiles, units), out...]
where the time goes in v4:
time: 354 us; the launch traced here: 353 us
  Pallas kernels  337 us (95%)
  other arithmetic  9.27 us (3%)
  local copies, waits for them, and re-layouts  6.23 us (2%)
    pallas_call x1, Pallas kernels, layer(): pl.pallas_call(functools.partial(layer_kernel, chunks, tiles, units), out...  337 us
    convert_element_type x6, other arithmetic, per_device(): summed = [x.astype(F32) for x in summed]  9.27 us

profile of v4, /device:TPU:0, one launch (start us, length us, event | category | flops | bytes accessed | tf_op | source)
XLA Modules:
  0.0 353.2 jit_solution(6883469748448698109)
XLA Ops:
  0.7 337.0 %layer.1 = (bf16[1024,3072]{1,0:T(8,128)(2,1)}, bf16[1024,1024]{1,0:T(8,128)(2,1)}, bf16[1024,3072]{1,0:T(8,128)(2,1)}, bf16[1024,1024]{1,0:T(8,128)(2,1)}, bf16...) custom-call(bf16[128,3072]{1,0:T(8,128)(2,1)} %refs_0_.1, ...), custom_call_target="tpu_custom_call" | custom-call | tf_op jit(solution)/shard_map/layer/pallas_call | solution.py:844
  337.7 0.0 copy-start.3
  337.7 0.0 copy-start.2
  337.7 1.0 slice_bitcast_fusion
  338.6 0.6 copy.39
  339.3 1.7 fusion
  340.9 1.4 slice.36
  342.3 1.8 convert_element_type.19
  344.1 1.8 convert_element_type.21
  345.9 0.0 copy-done.3
  345.9 0.0 copy-start.1
  345.9 1.3 convert_element_type.18
  347.2 0.0 copy-done.2
  347.2 1.3 convert_element_type.20
  348.5 0.0 copy-done.1
  348.5 0.0 copy-start
  348.5 1.5 convert_element_type.22
  350.0 0.0 copy-done
  350.0 0.0 copy-start.5
  350.0 0.0 copy-start.4
  350.0 1.6 convert_element_type.23
  351.6 0.0 copy-done.5
  351.6 0.8 copy.42
  352.4 0.0 copy-done.4
  352.4 0.8 copy.43
Async XLA Ops:
  337.7 8.2 %copy-start.3 = (bf16[128,3072]{1,0:T(8,128)(2,1)S(1)}, bf16[128,3072]{1,0:T(8,128)(2,1)}, u32[]{:S(2)}) copy-start(bf16[128,3072]{1,0:T(8,128)(2,1)} %get-tuple-element.29) | copy-start | bytes 2359300
  337.7 9.5 %copy-start.2 = (bf16[128,3072]{1,0:T(8,128)(2,1)S(1)}, bf16[128,3072]{1,0:T(8,128)(2,1)}, u32[]{:S(2)}) copy-start(bf16[128,3072]{1,0:T(8,128)(2,1)} %get-tuple-element.31) | copy-start | bytes 2359300
  345.9 2.6 copy-start.1
  348.5 1.5 copy-start
  350.0 1.6 copy-start.5
  350.0 2.4 copy-start.4

commit v5 on v4

--- a/solution.py
+++ b/solution.py
@@ -101,19 +101,21 @@
     return e * (1.0 / jnp.sum(e, -1, keepdims=True))
 
 
-def attention(qkv_ref, bias_ref, mixed_ref):
+def attention(qkv_ref, bias_ref, mixed_ref, part=0, parts=1):
     width = mixed_ref.shape[1]
     per = width // LANES
+    count = per // parts
     masks = head_masks()
 
     def pair(p):
+        p = p + part * count
         q, k, v = (qkv_ref[:, at(p + i * per, LANES)] for i in range(3))
         out = 0.0
         for m in masks:
             out = out + dot(head_probs(q * m, k, bias_ref).astype(BF16), v * m)
         mixed_ref[:, at(p, LANES)] = out.astype(BF16)
 
-    each(per, pair)
+    each(count, pair)
 
 
 def attention_back(qkv_ref, bias_ref, dmix_ref, dqkv_ref):
@@ -213,6 +215,8 @@
 TILE = 1024
 SLOTS = 4
 AHEAD = 3
+LAG = 2
+PACE = (6, 7, 8, 10, 12, 13, 14, 15, 16, 17, 18)
 DEEP = 3
 RING = 6
 
@@ -294,33 +298,33 @@
         remote(dst, dst, ssem.at[k, kind], rsem.at[k, kind], to_sib).wait_recv()
 
     n_chunks = len(chunks)
-    progress = [0, 0]
-
-    def relay():
-        k = progress[1]
-        progress[1] += 1
-        for kind in (1, 2):
-            arrived(k, kind)
-            copy(k, kind + 4).start()
-
-    def advance(hops):
+    progress = [0, 0, AHEAD]
+
+    def relay_to(k):
+        while progress[1] < min(k, progress[0]):
+            k1 = progress[1]
+            progress[1] += 1
+            for kind in (1, 2):
+                arrived(k1, kind)
+                copy(k1, kind + 4).start()
+
+    def advance(hops, ahead=AHEAD, lag=LAG):
         while progress[0] < min(hops, n_chunks):
             k = progress[0]
             progress[0] += 1
             copy(k, 3).start()
             arrived(k, 0)
-            if k + AHEAD < n_chunks:
-                copy(k + AHEAD, 0).start()
+            while progress[2] < min(k + 1 + ahead, n_chunks):
+                copy(progress[2], 0).start()
+                progress[2] += 1
             for kind in (1, 2, 4):
                 copy(k, kind).start()
-            if k >= 1:
-                relay()
-        if hops > n_chunks and progress[1] < n_chunks:
-            relay()
+            relay_to(k + 1 - lag)
 
     def complete(a):
         ks = [k for k in range(n_chunks) if chunks[k][0] == a]
         advance(ks[-1] + 2)
+        relay_to(ks[-1] + 1)
         for k in ks:
             for kind in (3, 4, 5, 6):
                 arrived(k, kind)
@@ -357,29 +361,32 @@
         return (to_x, cx, to_y, cy) if u % 2 == 0 else (to_y, cy, to_x, cx)
 
     def part(u, p):
-        return gbuf.at[u // 4 % 3, u % 4, p]
+        _, _, _, rows, unit, top = units[u]
+        return gbuf.at[unit // 4 % 3, unit % 4, p, pl.ds(top, rows)]
+
+    def slot(ref, u, *more):
+        return ref.at[(u % RING, *more, pl.ds(0, units[u][3]))]
 
     def step1(u):
         dev1, p1, _, _ = hop(u)
-        k = u % RING
         return (
-            remote(part(u, cd), r1.at[k, 1], s1s.at[u, 1], s1r.at[u, 1], dev1),
-            remote(part(u, p1), r1.at[k, 0], s1s.at[u, 0], s1r.at[u, 0], dev1),
+            remote(part(u, cd), slot(r1, u, 1), s1s.at[u, 1], s1r.at[u, 1], dev1),
+            remote(part(u, p1), slot(r1, u, 0), s1s.at[u, 0], s1r.at[u, 0], dev1),
         )
 
     def step2(u):
         _, _, dev2, p2 = hop(u)
-        return remote(part(u, p2), r2.at[u % RING], s2s.at[u], s2r.at[u], dev2)
+        return remote(part(u, p2), slot(r2, u), s2s.at[u], s2r.at[u], dev2)
 
     def along(u):
-        return remote(part(u, chip), zin.at[u % RING], zs.at[u], zr.at[u], to_z)
+        return remote(part(u, chip), slot(zin, u), zs.at[u], zr.at[u], to_z)
 
     def across(u):
-        return remote(part(u, chip), zpeer.at[u % RING], zps.at[u], zpr.at[u], to_peer)
+        return remote(part(u, chip), slot(zpeer, u), zps.at[u], zpr.at[u], to_peer)
 
     def emit(u, src):
-        a, r, c = units[u]
-        return pltpu.make_async_copy(src, outs[a].at[pl.ds(r, 128), pl.ds(c, TILE)], osem.at[u])
+        a, r, c, rows, _, _ = units[u]
+        return pltpu.make_async_copy(src, outs[a].at[pl.ds(r, rows), pl.ds(c, TILE)], osem.at[u])
 
     state = {"ready": 0, "issued": 0, "done": 0, "step": 0}
 
@@ -402,16 +409,16 @@
             p2 = hop(u)[3]
             far, near = step1(u)
             far.wait_recv()
-            add_into(part(u, p2), part(u, p2), r1.at[u % RING, 1])
+            add_into(part(u, p2), part(u, p2), slot(r1, u, 1))
             step2(u).start()
             near.wait_recv()
-            add_into(part(u, chip), part(u, chip), r1.at[u % RING, 0])
+            add_into(part(u, chip), part(u, chip), slot(r1, u, 0))
             state["done"] += 1
             issue()
         u = s - 1
         if 0 <= u < n:
             step2(u).wait_recv()
-            add_into(part(u, chip), part(u, chip), r2.at[u % RING])
+            add_into(part(u, chip), part(u, chip), slot(r2, u))
 
             @pl.when(leaf)
             def _(u=u):
@@ -422,7 +429,7 @@
             @pl.when(inner)
             def _(u=u):
                 along(u).wait_recv()
-                add_into(part(u, chip), part(u, chip), zin.at[u % RING])
+                add_into(part(u, chip), part(u, chip), slot(zin, u))
                 across(u).start()
 
         u = s - 3
@@ -430,7 +437,7 @@
             @pl.when(inner)
             def _(u=u):
                 across(u).wait()
-                add_into(part(u, chip), part(u, chip), zpeer.at[u % RING])
+                add_into(part(u, chip), part(u, chip), slot(zpeer, u))
                 along(u).start()
                 emit(u, part(u, chip)).start()
 
@@ -439,7 +446,7 @@
             @pl.when(leaf)
             def _(u=u):
                 along(u).wait()
-                emit(u, zin.at[u % RING]).start()
+                emit(u, slot(zin, u)).start()
 
         u = s - 5
         if 0 <= u < n:
@@ -574,9 +581,13 @@
     complete(0)
     load((0, 1, 2))
     project(unit1, (0, 1, 2), qkv1)
+    advance(PACE[0])
     complete(1)
     load((3,))
-    attention(qkv1, None, mixed1)
+    attention(qkv1, None, mixed1, 0, 2)
+    advance(PACE[1])
+    attention(qkv1, None, mixed1, 1, 2)
+    advance(PACE[2])
     tile_load(3).wait()
 
     def put_after1(cols, y):
@@ -588,17 +599,22 @@
     turn_go, turn_end = over_both(
         lambda a, b: out1.at[8 * b + a], lambda a, b: in2.at[4 * a + b], turn_s, turn_r, turn_l)
     start_all(turn_go)
+    advance(PACE[3])
     complete(2)
     load((4, 5, 6))
     complete(3)
     load((7,))
+    advance(PACE[4])
     wait_all(turn_end)
     join(in2, base2)
     norm_rows(lambda rows: base2[rows, :].astype(F32), gain2, shift2, unit2)
+    advance(PACE[5])
     project(unit2, (4, 5, 6), qkv2)
-    advance(12)
-    attention(qkv2, bias, mixed2)
-    advance(14)
+    advance(PACE[6])
+    attention(qkv2, bias, mixed2, 0, 2)
+    advance(PACE[7])
+    attention(qkv2, bias, mixed2, 1, 2)
+    advance(PACE[8])
     tile_load(7).wait()
 
     def put_after2(cols, y):
@@ -623,9 +639,11 @@
             slope[:, cols] = rise.astype(BF16)
 
         matmul(unit3, wt.at[j], 256, put_pre)
+        if j == 1:
+            advance(PACE[9])
 
     swap4 = share(0, act, act_x, g2d, g_x)
-    advance(16)
+    advance(PACE[10])
     wait_all(swap4)
     wgrad(core, act.shape[1] // 8, act, act_x, g2d, g_x, gbuf.at[0], lt)
     complete(5)
@@ -731,7 +749,7 @@
     reduce_to(9)
     wait_all(swap1)
     wgrad(core, TILE // 8, unit1, unit1_x, dqkv, dqkv1_x, gbuf.at[0, pl.ds(1, 3)], lt)
-    offer(3)
+    offer(6)
     emb[...] = jnp.zeros_like(emb)
 
     def store1(rows, dh):
@@ -772,7 +790,6 @@
         sm[4] = sm[3] + smr[3]
         small_copy(4, to_peer).start()
 
-    start_all(res_go)
     reduce_to(state["step"] + 1)
 
     @pl.when(inner)
@@ -782,6 +799,8 @@
         small_down().start()
         small_out[...] = sm[5]
 
+    reduce_to(n + 1)
+    start_all(res_go)
     reduce_to(n + 5)
 
     @pl.when(leaf)
@@ -809,10 +828,14 @@
     by_mat = weight_tiles(fulls)
     order = (5, 4, 3, 2, 1, 0)
     tiles = by_mat + [x for a in order[1:] for x in by_mat if x[0] == a]
-    units = [
+    whole = [
         (a, r, c) for a in order
         for r in range(0, mats[a].shape[0], 128) for c in range(0, mats[a].shape[1], TILE)
     ]
+    units = []
+    for i, (a, r, c) in enumerate(whole):
+        step = 64 if i >= len(whole) - 3 else 128
+        units += [(a, r + top, c, step, i, top) for top in range(0, 128, step)]
     n = len(units)
     n_chunks = len(chunks)
     dma = pltpu.SemaphoreType.DMA
@@ -858,6 +881,64 @@
     )(*mats, tokens, grad4, actions, segments, frame_mask, embed, *vecs)
 
 
+def widen_kernel(n_mats, *refs):
+    mats, (small, grad, res) = refs[:n_mats], refs[n_mats : n_mats + 3]
+    wide = refs[n_mats + 3 : 2 * n_mats + 3]
+    embed_g, g1, s1, g2, s2, g3, s3, b_out, b_in, grad_out, res_out = refs[2 * n_mats + 3 : 2 * n_mats + 14]
+    low = refs[2 * n_mats + 14 : 3 * n_mats + 14]
+    high = refs[3 * n_mats + 14 : 4 * n_mats + 14]
+    passing, isem, osem = refs[4 * n_mats + 14 :]
+    ins = [pltpu.make_async_copy(m, v, isem.at[i]) for i, (m, v) in enumerate(zip(mats, low))]
+    outs = [pltpu.make_async_copy(v, w, osem.at[i]) for i, (v, w) in enumerate(zip(high, wide))]
+    for i, (a, b) in enumerate(((grad, grad_out), (res, res_out))):
+        ins.append(pltpu.make_async_copy(a, passing.at[i], isem.at[n_mats + i]))
+        outs.append(pltpu.make_async_copy(passing.at[i], b, osem.at[n_mats + i]))
+    for c in ins:
+        c.start()
+    n_act = embed_g.shape[0]
+    embed_g[...] = small[0:n_act, :]
+    for i, ref in enumerate((g1, s1, g2, s2, g3, s3, b_out)):
+        ref[...] = small[n_act + i : n_act + i + 1, :]
+    width = small.shape[1]
+    for i in range(b_in.shape[1] // width):
+        b_in[:, i * width : (i + 1) * width] = small[n_act + 7 + i : n_act + 8 + i, :]
+    for i in range(n_mats):
+        ins[i].wait()
+
+        def step(j, i=i):
+            rows = at(j, 16)
+            high[i][rows, :] = low[i][rows, :].astype(F32)
+
+        each(low[i].shape[0] // 16, step)
+        outs[i].start()
+    for i in (n_mats, n_mats + 1):
+        ins[i].wait()
+        outs[i].start()
+    for c in outs:
+        c.wait()
+
+
+def widen(mats, small, grad, res, n_act, ff):
+    n = len(mats)
+    width = small.shape[1]
+    lines = [(n_act, width)] + [(1, width)] * 7 + [(1, ff)]
+    res = res.reshape(grad.shape)
+    return pl.pallas_call(
+        functools.partial(widen_kernel, n),
+        out_shape=[jax.ShapeDtypeStruct(m.shape, F32) for m in mats]
+        + [jax.ShapeDtypeStruct(s, F32) for s in lines]
+        + [jax.ShapeDtypeStruct(grad.shape, grad.dtype)] * 2,
+        in_specs=[HBM_SPEC] * n + [VMEM_SPEC] + [HBM_SPEC] * 2,
+        out_specs=[HBM_SPEC] * n + [VMEM_SPEC] * 9 + [HBM_SPEC] * 2,
+        scratch_shapes=[pltpu.VMEM(m.shape, BF16) for m in mats]
+        + [pltpu.VMEM(m.shape, F32) for m in mats]
+        + [pltpu.VMEM((2,) + grad.shape, grad.dtype)]
+        + [pltpu.SemaphoreType.DMA((n + 2,))] * 2,
+        compiler_params=params(),
+        name="widen",
+    )(*mats, small, grad, res)
+
+
 def plain_norm(h, gain, shift):
     cen = h - jnp.mean(h, -1, keepdims=True)
     inv = lax.rsqrt(jnp.mean(cen * cen, -1, keepdims=True) + EPS)
@@ -1037,11 +1118,10 @@
         *rest, small, tokens_grad, result = layer(
             mats, tokens, grad4, row(actions), row(segments), row(frame_mask), embed, vecs)
         summed = rest[6:]
-        summed = [x.astype(F32) for x in summed]
-        n_act = embed.shape[0]
-        d_embed, lines = small[:n_act], small[n_act:]
-        dg1, ds1, dg2, ds2, dg3, ds3, d_bout = (lines[i] for i in range(7))
-        d_bin = lines[7 : 7 + ffn_in_bias.shape[0] // width].reshape(-1)
+        *outs, tokens_grad, result = widen(
+            summed, small, tokens_grad, result, embed.shape[0], ffn_in_bias.shape[0])
+        summed, d_embed = outs[:6], outs[6]
+        dg1, ds1, dg2, ds2, dg3, ds3, d_bout, d_bin = (x[0] for x in outs[7:])
     else:
         action = lax.dynamic_index_in_dim(actions, t, keepdims=False)
         added = lax.dynamic_slice_in_dim(embed, action, 1, 0)

time: 354 us -> 323 us (0.912)
  Pallas kernels: 337 us -> 322 us
  other arithmetic: 9.27 us -> 0 us
  local copies, waits for them, and re-layouts: 6.23 us -> 0 us
    pallas_call x1, Pallas kernels: 337 us -> 315 us  [layer(): pl.pallas_call(functools.partial(layer_kernel, chunks, tiles, units), out...]
    convert_element_type x6 -> x0, other arithmetic: 9.27 us -> none  [per_device(): summed = [x.astype(F32) for x in summed]]
    pallas_call x0 -> x1, Pallas kernels: none -> 6.55 us  [widen(): pl.pallas_call(functools.partial(widen_kernel, n), out_shape=[jax.ShapeDt...]
where the time goes in v5:
time: 323 us
  Pallas kernels  322 us (100%)
    pallas_call x1, Pallas kernels, layer(): pl.pallas_call(functools.partial(layer_kernel, chunks, tiles, units), out...  315 us
    pallas_call x1, Pallas kernels, widen(): pl.pallas_call(functools.partial(widen_kernel, n), out_shape=[jax.ShapeDt...  6.55 us

profile of v5, /device:TPU:0, one launch (start us, length us, event | category | flops | bytes accessed | tf_op | source)
XLA Modules:
  0.0 322.6 jit_solution(13286293059740288710)
XLA Ops:
  0.7 315.2 %layer.1 = (bf16[1024,3072]{1,0:T(8,128)(2,1)}, bf16[1024,1024]{1,0:T(8,128)(2,1)}, bf16[1024,3072]{1,0:T(8,128)(2,1)}, bf16[1024,1024]{1,0:T(8,128)(2,1)}, bf16...) custom-call(bf16[128,3072]{1,0:T(8,128)(2,1)} %refs_0_.1, ...), custom_call_target="tpu_custom_call" | custom-call | tf_op jit(solution)/shard_map/layer/pallas_call | solution.py:867
  315.9 6.6 %widen.1 = (f32[128,3072]{1,0:T(8,128)}, f32[128,1024]{1,0:T(8,128)}, f32[128,3072]{1,0:T(8,128)}, f32[128,1024]{1,0:T(8,128)}, f32[128,4096]{1,0:T(8,128)}, /*i...) custom-call(bf16[128,3072]{1,0:T(8,128)(2,1)} %get-tuple-element.43., ...), custom_call_target="tpu_custom_call" | custom-call | tf_op jit(solution)/shard_map/widen/pallas_call | solution.py:926

commit v6 on v5

--- a/solution.py
+++ b/solution.py
@@ -164,6 +164,7 @@
 def wgrad(core, shard, left, left_x, right, right_x, out, lt):
     tok = left.shape[0]
     col_blocks = right.shape[1] // TILE
+    lt = lt.at[:, pl.ds(0, 2 * tok)]
     for rb in range(shard // 128):
         for q in range(4):
             cols = pl.ds(pl.multiple_of((2 * q + core) * shard + rb * 128, 128), 128)
@@ -172,15 +173,13 @@
             lt[q * 128 : (q + 1) * 128, tok:] = left_x[:, cols].T
 
         def step(j, rb=rb):
-            cols = at(j, 512)
+            cols = at(j, TILE)
             y = dot(lt[:, :tok], right[:, cols]) + dot(lt[:, tok:], right_x[:, cols])
             y = y.astype(BF16)
-            unit = rb * col_blocks + j // 2
-            half = pl.ds(pl.multiple_of(lax.rem(j, 2) * 512, 512), 512)
             for q in range(4):
-                out[unit, q, :, half] = y[q * 128 : (q + 1) * 128]
-
-        each(2 * col_blocks, step)
+                out[rb * col_blocks + j, q] = y[q * 128 : (q + 1) * 128]
+
+        each(col_blocks, step)
 
 
 GELU_A = 0.7978845608
@@ -215,8 +214,10 @@
 TILE = 1024
 SLOTS = 4
 AHEAD = 3
+AHEAD2 = 3
+PRE = 512
 LAG = 2
-PACE = (6, 7, 8, 10, 12, 13, 14, 15, 16, 17, 18)
+PACE = (6, 7, 8, 10, 12, 13, 13, 14, 14, 16, 18)
 DEEP = 3
 RING = 6
 
@@ -225,7 +226,7 @@
     out = []
     for i, (rows, cols) in enumerate(shapes):
         step = rows
-        while step * cols > 128 * 1024 and step % 32 == 0:
+        while step * cols > (128 if i < 4 else 64) * 1024 and step % 32 == 0:
             step //= 2
         out += [(i, r, step) for r in range(0, rows, step)]
     return out
@@ -256,11 +257,13 @@
     outs = refs[26:32]
     small_out, tokens_grad, result = refs[32:35]
     (base1, unit1, qkv1, mixed1, base2, unit2, qkv2, mixed2, after2, unit3, slope, g2d, act,
-     wt, gbuf, r1, r2, zin, zpeer, act_x, g_x, dpre_x, unit3_x, mix2_x, low2_x, unit2_x, dqkv2_x,
-     mix1_x, low1_x, unit1_x, dqkv1_x, du, low2, low1, dmix, dqkv,
-     out1, in2, g_in, res_out, turn_out, turn_in, bias, added, sm, smr, lt, acc, emb,
+     wt, gbuf, r1, r2, zin, zpeer, zin2, zpeer2, act_x, g_x, dpre_x, unit3_x, mix2_x, low2_x, unit2_x, dqkv2_x,
+     mix1_x, low1_x, unit1_x, du, y_own, y_in, du_in, low2, low1, dmix, dqkv,
+     out1, in2, g_in, res_out, turn_in, bias, added, b_half, db_half, sm, smr, lt, acc, emb,
      ssem, rsem, bsem, tsem, z3s, z3r, z3l, f7s, f7r, f7l, turn_s, turn_r, turn_l, back_s, back_r, back_l,
-     s1s, s1r, s2s, s2r, zs, zr, zps, zpr, osem, sms, smrs, xs, xr, o7s, o7r, o7l, t3s, t3r, t3l) = refs[35:]
+     s1s, s1r, s2s, s2r, zs, zr, zps, zpr, zs2, zr2, zps2, zpr2, osem, sms, smrs, xs, xr, pairs, pairr,
+     o7s, o7r, o7l, t3s, t3r, t3l) = refs[35:]
+    turn_out, dqkv1_x = out1, qkv2
     f = lax.axis_index("frame")
     t = lax.axis_index("tile")
     core = lax.rem(f, 2)
@@ -278,22 +281,36 @@
     others = [(a, b) for a in range(8) for b in range(4) if a or b]
     greet([(xor_any(f, a), xor_any(t, b)) for a, b in others])
 
+    def split_ffn(a):
+        return a >= 4
+
+    def shard_rows(a):
+        return full[a].shape[0] // 8
+
     def piece(k, owner):
         a, r, rows = chunks[k]
-        return full[a].at[pl.ds(pl.multiple_of(owner * shards[a].shape[0] + r, 16), rows)]
+        return full[a].at[pl.ds(pl.multiple_of(owner * shard_rows(a) + r, 16), rows)]
 
     def own(k):
         a, r, rows = chunks[k]
-        return shards[a].at[pl.ds(r, rows)]
+        return piece(k, f) if split_ffn(a) else shards[a].at[pl.ds(r, rows)]
+
+    def ways(k):
+        if split_ffn(chunks[k][0]) and k % 2:
+            return second, to_second, first, to_first
+        return first, to_first, second, to_second
 
     def copy(k, kind):
-        dev = (to_first, to_second, to_z, to_sib, to_sib, to_sib, to_sib)[kind]
-        owner = (f, first, first, f, first, diag, second)[kind]
-        src = own(k) if kind in (0, 3) else piece(k, owner)
+        one, to_one, other, to_other = ways(k)
+        direct = split_ffn(chunks[k][0])
+        dev = (to_one, to_other, to_other if direct else to_z, to_sib, to_sib, to_sib, to_sib)[kind]
+        owner = (f, one, f if direct else one, f, one, diag, other)[kind]
+        src = own(k) if kind in (0, 3) or (kind == 2 and direct) else piece(k, owner)
         return remote(src, piece(k, owner), ssem.at[k, kind], rsem.at[k, kind], dev)
 
     def arrived(k, kind):
-        owner = (first, diag, second, sib, xor(first, 1), xor(diag, 1), xor(second, 1))[kind]
+        one, _, other, _ = ways(k)
+        owner = (one, diag, other, sib, xor(one, 1), xor(diag, 1), xor(other, 1))[kind]
         dst = piece(k, owner)
         remote(dst, dst, ssem.at[k, kind], rsem.at[k, kind], to_sib).wait_recv()
 
@@ -308,17 +325,21 @@
                 arrived(k1, kind)
                 copy(k1, kind + 4).start()
 
-    def advance(hops, ahead=AHEAD, lag=LAG):
+    def advance(hops, lag=LAG):
         while progress[0] < min(hops, n_chunks):
             k = progress[0]
             progress[0] += 1
-            copy(k, 3).start()
+            early = (3, 2) if split_ffn(chunks[k][0]) else (3,)
+            for kind in early:
+                copy(k, kind).start()
             arrived(k, 0)
+            ahead = AHEAD if k < 9 else AHEAD2
             while progress[2] < min(k + 1 + ahead, n_chunks):
                 copy(progress[2], 0).start()
                 progress[2] += 1
             for kind in (1, 2, 4):
-                copy(k, kind).start()
+                if kind not in early:
+                    copy(k, kind).start()
             relay_to(k + 1 - lag)
 
     def complete(a):
@@ -331,24 +352,38 @@
 
     bounce = []
     for a, shard in enumerate(shards):
-        for r in range(0, shard.shape[0], 128):
-            for c in range(0, shard.shape[1], TILE):
+        for r in range(0, shard_rows(a), 128):
+            for c in range(0, full[a].shape[1], TILE):
                 i = len(bounce)
-                bounce.append((a, r, c, wt.at[2 + i // 8, pl.ds(i % 8 * 128, 128)]))
+                via = wt.at[2 + i // 8, pl.ds(i % 8 * 128, 128)]
+                if a == 4:
+                    cuts = [(r, (c // 256 + b) * 512 + 256 * odd, 256, b * 256) for b in range(4)]
+                else:
+                    cuts = [(r + 256 * odd if a == 5 else r, c, TILE, 0)]
+                bounce.append((a, r, c, via, cuts))
 
     def bounce_in(i):
-        a, r, c, via = bounce[i]
-        return pltpu.make_async_copy(shards[a].at[pl.ds(r, 128), pl.ds(c, TILE)], via, bsem.at[i])
+        a, _, _, via, cuts = bounce[i]
+        return [
+            pltpu.make_async_copy(
+                shards[a].at[pl.ds(row if isinstance(row, int) else pl.multiple_of(row, 128), 128),
+                             pl.ds(col if isinstance(col, int) else pl.multiple_of(col, 256), wide)],
+                via.at[:, pl.ds(place, wide)], bsem.at[i, b])
+            for b, (row, col, wide, place) in enumerate(cuts)
+        ]
 
     def bounce_out(i):
-        a, r, c, via = bounce[i]
-        row = pl.multiple_of(f * shards[a].shape[0] + r, 128)
-        return pltpu.make_async_copy(via, full[a].at[pl.ds(row, 128), pl.ds(c, TILE)], bsem.at[i])
+        a, r, c, via, _ = bounce[i]
+        row = pl.multiple_of(f * shard_rows(a) + r, 128)
+        return pltpu.make_async_copy(via, full[a].at[pl.ds(row, 128), pl.ds(c, TILE)], bsem.at[i, 0])
 
     def tile_load(i):
         a, r, c = tiles[i]
         src = full[a].at[pl.ds(r, TILE), pl.ds(c, TILE)]
-        return pltpu.make_async_copy(src, wt.at[i % SLOTS], tsem.at[i])
+        return pltpu.make_async_copy(src, wt.at[slot_of(i)], tsem.at[i])
+
+    def slot_of(i):
+        return i % SLOTS if i < 12 else (i + 2) % SLOTS
 
     def load(ids):
         for i in ids:
@@ -362,7 +397,7 @@
 
     def part(u, p):
         _, _, _, rows, unit, top = units[u]
-        return gbuf.at[unit // 4 % 3, unit % 4, p, pl.ds(top, rows)]
+        return gbuf.at[unit // 4 % 2, unit % 4, p, pl.ds(top, rows)]
 
     def slot(ref, u, *more):
         return ref.at[(u % RING, *more, pl.ds(0, units[u][3]))]
@@ -384,9 +419,29 @@
     def across(u):
         return remote(part(u, chip), slot(zpeer, u), zps.at[u], zpr.at[u], to_peer)
 
-    def emit(u, src):
+    def halves(u):
+        return split_ffn(units[u][0])
+
+    def across2(u):
+        return remote(slot(zin, u), zpeer2.at[u], zps2.at[u], zpr2.at[u], to_peer)
+
+    def along2(u):
+        return remote(slot(zin, u), zin2.at[u], zs2.at[u], zr2.at[u], to_z)
+
+    def emit(u, src, half=None, k=0):
         a, r, c, rows, _, _ = units[u]
-        return pltpu.make_async_copy(src, outs[a].at[pl.ds(r, rows), pl.ds(c, TILE)], osem.at[u])
+        if a == 5:
+            row = pl.multiple_of(r + 256 * half, 128)
+            return [pltpu.make_async_copy(src, outs[a].at[pl.ds(row, rows), pl.ds(c, TILE)], osem.at[u, k])]
+        if a == 4:
+            return [
+                pltpu.make_async_copy(
+                    src.at[:, pl.ds(b * 256, 256)],
+                    outs[a].at[pl.ds(r, rows), pl.ds(pl.multiple_of((c // 256 + b) * 512 + 256 * half, 256), 256)],
+                    osem.at[u, k + b])
+                for b in range(4)
+            ]
+        return [pltpu.make_async_copy(src, outs[a].at[pl.ds(r, rows), pl.ds(c, TILE)], osem.at[u, k])]
 
     state = {"ready": 0, "issued": 0, "done": 0, "step": 0}
 
@@ -429,36 +484,58 @@
             @pl.when(inner)
             def _(u=u):
                 along(u).wait_recv()
-                add_into(part(u, chip), part(u, chip), slot(zin, u))
+                if halves(u):
+                    across2(u).start()
+                else:
+                    add_into(part(u, chip), part(u, chip), slot(zin, u))
                 across(u).start()
+
+        u = s - 5
+        if 0 <= u < n:
+            for c in step1(u):
+                c.wait_send()
+            step2(u).wait_send()
+
+            @pl.when(inner)
+            def _(u=u):
+                along(u).wait_send()
+                if halves(u):
+                    along2(u).wait_send()
+
+            if halves(u):
+                wait_all(emit(u, part(u, chip), odd, 0))
+                wait_all(emit(u, slot(zin, u), odd, 4))
+            else:
+                wait_all(emit(u, part(u, chip)))
 
         u = s - 3
         if 0 <= u < n:
             @pl.when(inner)
             def _(u=u):
                 across(u).wait()
-                add_into(part(u, chip), part(u, chip), slot(zpeer, u))
+                if halves(u):
+                    across2(u).wait()
+                    add_into(part(u, chip), part(u, chip), zpeer2.at[u])
+                    add_into(slot(zin, u), slot(zin, u), slot(zpeer, u))
+                    along2(u).start()
+                    start_all(emit(u, part(u, chip), odd, 0))
+                    start_all(emit(u, slot(zin, u), 1 - odd, 4))
+                else:
+                    add_into(part(u, chip), part(u, chip), slot(zpeer, u))
+                    start_all(emit(u, part(u, chip)))
                 along(u).start()
-                emit(u, part(u, chip)).start()
 
         u = s - 4
         if 0 <= u < n:
             @pl.when(leaf)
             def _(u=u):
                 along(u).wait()
-                emit(u, slot(zin, u)).start()
-
-        u = s - 5
-        if 0 <= u < n:
-            for c in step1(u):
-                c.wait_send()
-            step2(u).wait_send()
-
-            @pl.when(inner)
-            def _(u=u):
-                along(u).wait_send()
-
-            emit(u, part(u, chip)).wait()
+                if halves(u):
+                    along2(u).wait_recv()
+                    start_all(emit(u, slot(zin, u), 1 - odd, 0))
+                    start_all(emit(u, zin2.at[u], odd, 4))
+                else:
+                    start_all(emit(u, slot(zin, u)))
 
     def reduce_to(s):
         while state["step"] < s:
@@ -520,12 +597,15 @@
 
         each(src.shape[0] // 4, step)
 
+    def to_pair(i, src, dst):
+        return remote(src, dst, pairs.at[i], pairr.at[i], to_z)
+
     tok_go, tok_end = over_tile(lambda d: tokens.at[d], lambda d: rows_of(base1, d), z3s, z3r, z3l)
     start_all(tok_go)
     for k in range(AHEAD):
         copy(k, 0).start()
     for i in range(len(bounce)):
-        bounce_in(i).start()
+        start_all(bounce_in(i))
     grad_go, grad_end = over_frame(
         lambda d: grad4.at[:, d], lambda d: g_in.at[pl.ds(4 * d, 4)], f7s, f7r, f7l)
 
@@ -558,9 +638,11 @@
     )
     bias[...] = jnp.where(allowed, 0.0, -1e30)
 
+    for b in range(8):
+        b_half[:, b * 256 : (b + 1) * 256] = b_in[:, pl.ds(pl.multiple_of(b * 512 + 256 * odd, 256), 256)]
     advance(1)
     for i in range(len(bounce)):
-        bounce_in(i).wait()
+        wait_all(bounce_in(i))
         bounce_out(i).start()
     wait_all(tok_end)
     norm_rows(lambda rows: base1[rows, :].astype(F32) + added[...], gain1, shift1, unit1)
@@ -573,10 +655,9 @@
             tile_load(i).wait()
 
             def put(cols, y, j=j):
-                start = pl.multiple_of(cols.start + j * TILE, 512)
-                out_ref[:, pl.ds(start, 512)] = y.astype(BF16)
-
-            matmul(unit, wt.at[i % SLOTS], 512, put)
+                out_ref[:, j * TILE : (j + 1) * TILE] = y.astype(BF16)
+
+            matmul(unit, wt.at[i % SLOTS], TILE, put)
 
     complete(0)
     load((0, 1, 2))
@@ -593,7 +674,7 @@
     def put_after1(cols, y):
         du[:, cols] = y + base1[:, cols].astype(F32) + added[:, cols]
 
-    matmul(mixed1, wt.at[3], 512, put_after1)
+    matmul(mixed1, wt.at[3], TILE, put_after1)
     split(lambda rows: du[rows, :], out1)
 
     turn_go, turn_end = over_both(
@@ -607,6 +688,10 @@
     advance(PACE[4])
     wait_all(turn_end)
     join(in2, base2)
+    wait_all(grad_end)
+    join(g_in, g2d.at[pl.ds(0, n_rows)])
+    g_pair = to_pair(0, g2d.at[pl.ds(0, n_rows)], g2d.at[pl.ds(n_rows, n_rows)])
+    g_pair.start()
     norm_rows(lambda rows: base2[rows, :].astype(F32), gain2, shift2, unit2)
     advance(PACE[5])
     project(unit2, (4, 5, 6), qkv2)
@@ -620,76 +705,109 @@
     def put_after2(cols, y):
         after2[:, cols] = y + base2[:, cols].astype(F32)
 
-    matmul(mixed2, wt.at[3], 512, put_after2)
-    norm_rows(lambda rows: after2[rows, :], gain3, shift3, unit3)
+    matmul(mixed2, wt.at[3], TILE, put_after2)
+    mine, theirs = pl.ds(0, n_rows), pl.ds(n_rows, n_rows)
+    norm_rows(lambda rows: after2[rows, :], gain3, shift3, unit3.at[mine])
+    unit_pair = to_pair(1, unit3.at[mine], unit3.at[theirs])
+    unit_pair.start()
     complete(4)
-    load((8, 9, 10, 11))
-    wait_all(grad_end)
-    join(g_in, g2d)
-
-    for j in range(4):
-        tile_load(8 + j).wait()
-
-        def put_pre(cols, y, j=j):
-            cols = pl.ds(pl.multiple_of(cols.start + j * TILE, 256), 256)
-            v = y + b_in[:, cols]
-            th = jnp.tanh(GELU_A * (v + GELU_B * v * v * v))
-            act[:, cols] = (0.5 * v * (1.0 + th)).astype(BF16)
-            rise = 0.5 * (1.0 + th) + 0.5 * v * (1.0 - th * th) * GELU_A * (1.0 + 3.0 * GELU_B * v * v)
-            slope[:, cols] = rise.astype(BF16)
-
-        matmul(unit3, wt.at[j], 256, put_pre)
-        if j == 1:
+    load((8, 9))
+
+    for side in (0, 1):
+        if side:
+            unit_pair.wait()
             advance(PACE[9])
-
+        for j in range(2):
+            if side == 0:
+                tile_load(8 + j).wait()
+
+            def put_pre(cols, y, j=j, side=side):
+                cols = pl.ds(pl.multiple_of(cols.start + j * TILE, PRE), PRE)
+                rows = theirs if side else mine
+                v = y + b_half[:, cols]
+                th = jnp.tanh(GELU_A * (v + GELU_B * v * v * v))
+                act[rows, cols] = (0.5 * v * (1.0 + th)).astype(BF16)
+                rise = 0.5 * (1.0 + th) + 0.5 * v * (1.0 - th * th) * GELU_A * (1.0 + 3.0 * GELU_B * v * v)
+                slope[rows, cols] = rise.astype(BF16)
+
+            matmul(unit3.at[theirs if side else mine], wt.at[j], PRE, put_pre)
+
+    g_pair.wait()
     swap4 = share(0, act, act_x, g2d, g_x)
     advance(PACE[10])
     wait_all(swap4)
-    wgrad(core, act.shape[1] // 8, act, act_x, g2d, g_x, gbuf.at[0], lt)
+    wgrad(core, act.shape[1] // 8, act, act_x, g2d, g_x, gbuf.at[0, pl.ds(0, 2)], lt)
     complete(5)
-    load((12, 13, 14, 15))
-    offer(4)
+    load((10, 11))
+    offer(2)
 
     sm[0] = jnp.zeros_like(sm[0])
-    for j in range(4):
-        tile_load(12 + j).wait()
+    for j in range(2):
+        tile_load(10 + j).wait()
 
         def put_dpre(rows, y, j=j):
-            cols = pl.ds(pl.multiple_of(rows.start + j * TILE, 256), 256)
+            cols = pl.ds(pl.multiple_of(rows.start + j * TILE, 512), 512)
             d = (y * slope[:, cols].astype(F32)).astype(BF16)
             slope[:, cols] = d
-            sm[0, 15 + j : 16 + j, rows] = jnp.sum(d.astype(F32), 0, keepdims=True)
-
-        matmul_nt(g2d, wt.at[j], 256, put_dpre)
-
-        def add_up(h, j=j):
-            cols = at(h, 512)
-            y = dot(act[:, j * TILE : (j + 1) * TILE], wt[j, :, cols])
-            du[:, cols] = y + (after2[:, cols] + b_out[:, cols] if j == 0 else du[:, cols])
-
-        each(2, add_up)
-        load((16 + j,))
+            db_half[:, cols] = jnp.sum(d.astype(F32), 0, keepdims=True)
+
+        matmul_nt(g2d, wt.at[2 + j], 512, put_dpre)
     dpre = slope
     swap3 = share(1, unit3, unit3_x, dpre, dpre_x)
-    split(lambda rows: du[rows, :], res_out)
+    for b in range(8):
+        place_b = pl.ds(pl.multiple_of(b % 2 * 512 + 256 * odd, 256), 256)
+        sm[0, 15 + b // 2 : 16 + b // 2, place_b] = db_half[:, b * 256 : (b + 1) * 256]
+
+    def back_in(side, store):
+        def run(h):
+            rows = at(h, 512)
+            who = theirs if side else mine
+            y = dot_nt(dpre[who, :TILE], wt[0, rows, :]) + dot_nt(dpre[who, TILE:], wt[1, rows, :])
+            store(rows, y)
+
+        each(TILE // 512, run)
+
+    def put_theirs(rows, y):
+        dmix[:, rows] = y.astype(BF16)
+
+    def put_mine(rows, y):
+        du[:, rows] = y
+
+    back_in(1, put_theirs)
+    du_pair = to_pair(2, dmix, du_in)
+    du_pair.start()
+    back_in(0, put_mine)
+    load((14, 15))
+
+    def forward_out(side, store):
+        def run(h):
+            cols = at(h, 512)
+            who = theirs if side else mine
+            store(cols, dot(act[who, :TILE], wt[2, :, cols]) + dot(act[who, TILE:], wt[3, :, cols]))
+
+        each(TILE // 512, run)
+
+    def put_y_theirs(cols, y):
+        low1[:, cols] = y.astype(BF16)
+
+    def put_y_mine(cols, y):
+        y_own[:, cols] = y + after2[:, cols] + b_out[:, cols]
+
+    forward_out(1, put_y_theirs)
+    y_pair = to_pair(3, low1, y_in)
+    y_pair.start()
+    forward_out(0, put_y_mine)
+    load((12, 13))
     res_go, res_end = over_frame(
         lambda d: res_out.at[pl.ds(4 * d, 4)], lambda d: result.at[:, d], o7s, o7r, o7l)
     reduce_to(1)
-
-    def back_through(first_tile, count, x_ref):
-        for j in range(count):
-            i = first_tile + j
-            tile_load(i).wait()
-
-            def run(h, i=i, j=j):
-                rows = at(h, 256)
-                y = dot_nt(x_ref[:, j * TILE : (j + 1) * TILE], wt[i % SLOTS, rows, :])
-                du[:, rows] = y if j == 0 else du[:, rows] + y
-
-            each(TILE // 256, run)
-            load((i + SLOTS,))
-
-    back_through(16, 4, dpre)
+    du_pair.wait()
+
+    def add_du(i):
+        rows = at(i, ROWS)
+        du[rows, :] = du[rows, :] + du_in[rows, :].astype(F32)
+
+    each(n_rows // ROWS, add_du)
 
     def store3(rows, dh):
         g = g2d[rows, :].astype(F32)
@@ -701,22 +819,39 @@
     norm_back(lambda rows: after2[rows, :], du, gain3, sm.at[0, pl.ds(12, 1)], sm.at[0, pl.ds(13, 1)], acc, store3)
     dafter = after2
     swap2o = share(2, mixed2, mix2_x, low2, low2_x)
+    wait_all(swap3)
+    wgrad(core, TILE // 8, unit3, unit3_x, dpre, dpre_x, gbuf.at[0, pl.ds(2, 2)], lt)
+    offer(2)
     reduce_to(2)
-    wait_all(swap3)
-    wgrad(core, TILE // 8, unit3, unit3_x, dpre, dpre_x, gbuf.at[1], lt)
-    offer(4)
+    y_pair.wait()
+    split(lambda rows: y_own[rows, :] + y_in[rows, :].astype(F32), res_out)
+
+    def back_through(first_tile, count, x_ref):
+        ids = range(first_tile, first_tile + count)
+        for i in ids:
+            tile_load(i).wait()
+
+        def run(h):
+            rows = at(h, 512)
+            parts = [
+                dot_nt(x_ref[:, j * TILE : (j + 1) * TILE], wt[slot_of(i), rows, :]) for j, i in enumerate(ids)
+            ]
+            du[:, rows] = sum(parts[1:], parts[0])
+
+        each(TILE // 512, run)
+        load([i + SLOTS for i in ids])
 
     def put_mix(rows, y):
         dmix[:, rows] = y.astype(BF16)
 
-    tile_load(20).wait()
-    matmul_nt(low2, wt.at[0], 512, put_mix)
-    load((24,))
+    tile_load(12).wait()
+    matmul_nt(low2, wt.at[slot_of(12)], TILE, put_mix)
+    load((16,))
     reduce_to(3)
     attention_back(qkv2, bias, dmix, dqkv)
     swap2 = share(3, unit2, unit2_x, dqkv, dqkv2_x)
     reduce_to(4)
-    back_through(21, 3, dqkv)
+    back_through(13, 3, dqkv)
 
     def store2(rows, dh):
         dafter[rows, :] = dafter[rows, :] + dh
@@ -728,16 +863,16 @@
         lambda a, b: turn_out.at[4 * a + b], lambda a, b: turn_in.at[8 * b + a], back_s, back_r, back_l)
     start_all(back_go)
     wait_all(swap2o)
-    wgrad(core, TILE // 8, mixed2, mix2_x, low2, low2_x, gbuf.at[2, pl.ds(0, 1)], lt)
+    wgrad(core, TILE // 8, mixed2, mix2_x, low2, low2_x, gbuf.at[1, pl.ds(0, 1)], lt)
     wait_all(swap2)
-    wgrad(core, TILE // 8, unit2, unit2_x, dqkv, dqkv2_x, gbuf.at[2, pl.ds(1, 3)], lt)
+    wgrad(core, TILE // 8, unit2, unit2_x, dqkv, dqkv2_x, gbuf.at[1, pl.ds(1, 3)], lt)
     offer(4)
     reduce_to(5)
     wait_all(back_end)
     join(turn_in, low1)
     swap1o = share(4, mixed1, mix1_x, low1, low1_x)
-    tile_load(24).wait()
-    matmul_nt(low1, wt.at[0], 512, put_mix)
+    tile_load(16).wait()
+    matmul_nt(low1, wt.at[slot_of(16)], TILE, put_mix)
     reduce_to(6)
     attention_back(qkv1, None, dmix, dqkv)
     swap1 = share(5, unit1, unit1_x, dqkv, dqkv1_x)
@@ -745,7 +880,7 @@
     wgrad(core, TILE // 8, mixed1, mix1_x, low1, low1_x, gbuf.at[0, pl.ds(0, 1)], lt)
     offer(1)
     reduce_to(7)
-    back_through(25, 3, dqkv)
+    back_through(17, 3, dqkv)
     reduce_to(9)
     wait_all(swap1)
     wgrad(core, TILE // 8, unit1, unit1_x, dqkv, dqkv1_x, gbuf.at[0, pl.ds(1, 3)], lt)
@@ -823,14 +958,15 @@
     width = tokens.shape[2]
     rows = tokens.shape[0] * tokens.shape[1]
     ff = mats[4].shape[1]
-    fulls = [(8 * m.shape[0], m.shape[1]) for m in mats]
-    chunks = gather_chunks([m.shape for m in mats])
+    kept = [m.shape for m in mats[:4]] + [(mats[4].shape[0], ff // 2), (mats[5].shape[0] // 2, width)]
+    fulls = [(8 * r, c) for r, c in kept]
+    chunks = gather_chunks(kept)
     by_mat = weight_tiles(fulls)
     order = (5, 4, 3, 2, 1, 0)
-    tiles = by_mat + [x for a in order[1:] for x in by_mat if x[0] == a]
+    tiles = by_mat + [x for a in order[2:] for x in by_mat if x[0] == a]
     whole = [
         (a, r, c) for a in order
-        for r in range(0, mats[a].shape[0], 128) for c in range(0, mats[a].shape[1], TILE)
+        for r in range(0, kept[a][0], 128) for c in range(0, kept[a][1], TILE)
     ]
     units = []
     for i, (a, r, c) in enumerate(whole):
@@ -847,21 +983,23 @@
     scratch = [
         bf(rows, width), bf(rows, width), bf(rows, 3 * width), bf(rows, width),
         bf(rows, width), bf(rows, width), bf(rows, 3 * width), bf(rows, width),
-        fl(rows, width), bf(rows, width), bf(rows, ff), bf(rows, width), bf(rows, ff),
-        bf(SLOTS, TILE, TILE), bf(3, 4, 4, *unit), bf(RING, 2, *unit), bf(RING, *unit),
-        bf(RING, *unit), bf(RING, *unit),
-        bf(rows, ff // 2), bf(rows, width), bf(rows, ff), bf(rows, half),
+        fl(rows, width), bf(2 * rows, width), bf(2 * rows, ff // 2), bf(2 * rows, width), bf(2 * rows, ff // 2),
+        bf(SLOTS, TILE, TILE), bf(2, 4, 4, *unit), bf(RING, 2, *unit), bf(RING, *unit),
+        bf(RING, *unit), bf(RING, *unit), bf(4, *unit), bf(4, *unit),
+        bf(2 * rows, ff // 4), bf(2 * rows, width), bf(2 * rows, ff // 2), bf(2 * rows, half),
         bf(rows, half), bf(rows, width), bf(rows, half), bf(rows, 3 * width),
-        bf(rows, half), bf(rows, width), bf(rows, half), bf(rows, 3 * width),
-        fl(rows, width), bf(rows, width), bf(rows, width), bf(rows, width), bf(rows, 3 * width),
-        bf(*blocks), bf(*blocks), bf(*blocks), bf(*blocks), bf(*blocks), bf(*blocks),
-        fl(rows, rows), fl(1, width),
-        fl(6, 24, width), fl(5, 24, width), bf(512, 2 * rows), fl(2, 8, width), fl(8, width),
+        bf(rows, half), bf(rows, width), bf(rows, half),
+        fl(rows, width), fl(rows, width), bf(rows, width), bf(rows, width),
+        bf(rows, width), bf(rows, width), bf(rows, width), bf(rows, 3 * width),
+        bf(*blocks), bf(*blocks), bf(*blocks), bf(*blocks), bf(*blocks),
+        fl(rows, rows), fl(1, width), fl(1, ff // 2), fl(1, ff // 2),
+        fl(6, 24, width), fl(5, 24, width), bf(512, 4 * rows), fl(2, 8, width), fl(8, width),
     ]
     sems = [
-        (n_chunks, 7), (n_chunks, 7), (16,), (len(tiles),), (3,), (3,), (), (7,), (7,), (),
+        (n_chunks, 7), (n_chunks, 7), (12, 4), (len(tiles),), (3,), (3,), (), (7,), (7,), (),
         (31,), (31,), (), (31,), (31,), (),
-        (n, 2), (n, 2), (n,), (n,), (n,), (n,), (n,), (n,), (n,), (6,), (6,), (6, 5), (6, 5),
+        (n, 2), (n, 2), (n,), (n,), (n,), (n,), (n,), (n,), (4,), (4,), (4,), (4,), (n, 8), (6,), (6,), (6, 5), (6, 5),
+        (4,), (4,),
         (7,), (7,), (), (3,), (3,), (),
     ]
     return pl.pallas_call(

time: 323 us -> 320 us (level)
  Pallas kernels: 322 us -> 318 us
    pallas_call x1, Pallas kernels: 315 us -> 312 us  [layer(): pl.pallas_call(functools.partial(layer_kernel, chunks, tiles, units), out...]
where the time goes in v6:
time: 320 us; the launch traced here: 319 us
  Pallas kernels  318 us (99%)
    pallas_call x1, Pallas kernels, layer(): pl.pallas_call(functools.partial(layer_kernel, chunks, tiles, units), out...  312 us
    pallas_call x1, Pallas kernels, widen(): pl.pallas_call(functools.partial(widen_kernel, n), out_shape=[jax.ShapeDt...  6.55 us

profile of v6, /device:TPU:0, one launch (start us, length us, event | category | flops | bytes accessed | tf_op | source)
XLA Modules:
  0.0 319.0 jit_solution(12770547925929262926)
XLA Ops:
  0.7 311.6 %layer.1 = (bf16[1024,3072]{1,0:T(8,128)(2,1)}, bf16[1024,1024]{1,0:T(8,128)(2,1)}, bf16[1024,3072]{1,0:T(8,128)(2,1)}, bf16[1024,1024]{1,0:T(8,128)(2,1)}, bf16...) custom-call(bf16[128,3072]{1,0:T(8,128)(2,1)} %refs_0_.1, ...), custom_call_target="tpu_custom_call" | custom-call | tf_op jit(solution)/shard_map/layer/pallas_call | solution.py:1005
  312.3 6.6 %widen.1 = (f32[128,3072]{1,0:T(8,128)}, f32[128,1024]{1,0:T(8,128)}, f32[128,3072]{1,0:T(8,128)}, f32[128,1024]{1,0:T(8,128)}, f32[128,4096]{1,0:T(8,128)}, /*i...) custom-call(bf16[128,3072]{1,0:T(8,128)(2,1)} %get-tuple-element.43., ...), custom_call_target="tpu_custom_call" | custom-call | tf_op jit(solution)/shard_map/widen/pallas_call | solution.py:1064
